TPU v7x, 32 devices: a whole 2x2x4 slice. The times are simulated.
32 devices in a mesh: parts: 2 (over x), types: 8 (over z, y), tm: 2 (over core).
Axes of the slice: x: 2, y: 2, z: 4, core: 2. Of those that a mesh axis runs over, the one named last changes fastest.
Arguments:
- counts: int32 [1024, 8192], P(('parts', 'tm'), 'types'), parts along dimension 0, may hold values from 0 to 3
- mark_value: bfloat16 [1024, 8192], P(('parts', 'tm'), 'types'), parts along dimension 0, may hold values from 0.25 to 4
- base_rate: float32 [8192], P('types'), may hold values from 0.2 to 2
- excite: bfloat16 [4, 64, 6, 128, 128], P(None, 'types'), may hold values from -0.109375 to 0.109375
- block_col: int32 [64, 6], replicated, may hold values from 0 to 63, as said below
- row_fill: int32 [64], replicated, may hold values from 2 to 6, as said below
Outputs:
- grad_excite: bfloat16 [8, 64, 6, 128, 128], P('parts', 'types', None, 'tm'), parts along dimension 0
- grad_rate: float32 [16384], P(('parts', 'types', 'tm')), parts along dimension 0
There are 2 independent parts, one for each index of `parts`. A program takes and returns all parts, laid end to end along the dimension named above; an argument that names none is the same for every part. Nothing has to cross between parts.
Inputs may be any that keep to these rules, and one draw needn't show every extreme that they name: `block_col`: among the live blocks of the 8 block rows of one device, at most 6 name column blocks held by any one device (column block c is held by device c // 8); every device has exactly 6 such blocks from some device in every draw. `row_fill`: the first of each device's 8 block rows has all 6 blocks live.
All inputs are finite; a program needn't handle non-finite values.
Results may differ from a plain program's by a relative error of at most 0.012.
Values may be sent and summed in bfloat16 or wider, within the bound.
No kernel may reach another device: no remote copies, remote signals or barrier semaphores. Data moves between devices by JAX's collectives and lax.ppermute only.
A program may use at most 128 MiB of HBM per device.

v0:
```python
import jax
import jax.numpy as jnp
from jax import lax
from jax.sharding import PartitionSpec as P


def entering(part, axis, combine, identity):
    place = lax.axis_index(axis)
    gathered = jax.tree.map(lambda a: lax.all_gather(a, axis), part)
    state = jax.tree.map(lambda a, e: jnp.zeros_like(a) + jnp.asarray(e, a.dtype), part, identity)

    def one(lap, state):
        return combine(
            state, jax.tree.map(lambda a: lax.dynamic_index_in_dim(a, lap, 0, False), gathered)
        )

    return lax.fori_loop(0, place, one, state)


def running(earlier, later):
    return (earlier[0] * later[1] + later[0], earlier[1] * later[1])


def shards(counts, mark_value, base_rate, excite, block_col, row_fill):
    basis_count = excite.shape[0]
    row_blocks = excite.shape[1]
    slot_count = excite.shape[2]
    tile_size = excite.shape[4]
    bins = counts.shape[0]
    types_local = counts.shape[1]
    type_devices = lax.axis_size("types")
    overall_bin_count = bins * lax.axis_size("tm")
    own_index = lax.axis_index("types")
    entries = row_blocks * slot_count
    capacity = max(2, entries // type_devices)
    tau_scale = 2.0 * overall_bin_count / 8.0 ** jnp.arange(basis_count, dtype=jnp.float32)
    log_decay = -1.0 / tau_scale
    row_time = jnp.arange(bins + 1, dtype=jnp.float32)[:, None]
    col_time = jnp.arange(bins, dtype=jnp.float32)[None, :]
    lag_steps = row_time - 1.0 - col_time
    kernel = jnp.where(
        lag_steps[None] >= 0.0,
        (1.0 - jnp.exp(log_decay))[:, None, None]
        * jnp.exp(jnp.maximum(lag_steps, 0.0)[None] * log_decay[:, None, None]),
        jnp.float32(0.0),
    )
    decay_power = jnp.exp(jnp.arange(bins, dtype=jnp.float32)[None, :] * log_decay[:, None])
    group_decay = jnp.exp(bins * log_decay)[:, None]
    impact_bf = (counts.astype(jnp.float32) * mark_value.astype(jnp.float32)).astype(jnp.bfloat16)
    impact = lax.optimization_barrier(impact_bf).astype(jnp.float32)
    columns = block_col.reshape(type_devices, entries)
    fill = row_fill.reshape(type_devices, row_blocks)
    live_mask = (jnp.arange(slot_count)[None, None, :] < fill[:, :, None]).reshape(
        type_devices, entries
    )
    source = columns // row_blocks
    earlier_entry = jnp.arange(entries)[:, None] > jnp.arange(entries)[None, :]
    same_source = (
        (source[:, :, None] == source[:, None, :]) & live_mask[:, None, :] & earlier_entry[None]
    )
    position = jnp.sum(same_source.astype(jnp.int32), axis=2)
    matches = (
        live_mask[:, None, :]
        & (source[:, None, :] == own_index)
        & (position[:, None, :] == jnp.arange(capacity)[None, :, None])
    )
    local_block = jnp.sum(jnp.where(matches, columns[:, None, :] % row_blocks, 0), axis=2).reshape(
        -1
    )
    slot_all = jnp.clip(source * capacity + position, 0, type_devices * capacity - 1)
    own_slots = lax.dynamic_index_in_dim(slot_all, own_index, 0, keepdims=False)
    own_live = lax.dynamic_index_in_dim(live_mask, own_index, 0, keepdims=False)
    local_state = jnp.einsum("btu,uk->btk", kernel, impact, precision=lax.Precision.HIGHEST)
    group_end = local_state[:, bins]
    identity = (
        jnp.zeros((basis_count, types_local), jnp.float32),
        jnp.ones((basis_count, 1), jnp.float32),
    )
    incoming = entering((group_end, group_decay), "tm", running, identity)[0]
    full_state = local_state[:, :bins] + decay_power[:, :, None] * incoming[:, None, :]
    state_bf = full_state.astype(jnp.bfloat16).reshape(basis_count, bins, row_blocks, tile_size)
    outgoing = jnp.take(state_bf, local_block, axis=2).reshape(
        basis_count, bins, type_devices, capacity * tile_size
    )
    received = lax.all_to_all(outgoing, "types", split_axis=2, concat_axis=2, tiled=True)
    received = received.reshape(basis_count, bins, type_devices * capacity, tile_size)
    gathered = jnp.take(received, own_slots, axis=2)
    gathered = jnp.where(own_live[None, None, :, None], gathered, jnp.zeros((), jnp.bfloat16))
    stacked = gathered.reshape(basis_count, bins, row_blocks, slot_count, tile_size)
    excited = jnp.einsum("bispq,btisq->tip", excite, stacked, preferred_element_type=jnp.float32)
    intensity = excited.reshape(bins, types_local) + base_rate[None, :]
    weighted = 2.0 / overall_bin_count * (intensity - counts.astype(jnp.float32))
    rate_grad = jnp.sum(weighted, axis=0)
    weighted_bf = weighted.astype(jnp.bfloat16).reshape(bins, row_blocks, tile_size)
    excite_grad = jnp.einsum(
        "tip,btisq->bispq", weighted_bf, stacked, preferred_element_type=jnp.float32
    )
    grad_part, rate_portion = (
        lax.psum_scatter(
            excite_grad.astype(jnp.bfloat16), "tm", scatter_dimension=3, tiled=True
        ).astype(jnp.float32),
        lax.psum_scatter(
            rate_grad.astype(jnp.bfloat16), "tm", scatter_dimension=0, tiled=True
        ).astype(jnp.float32),
    )
    return (grad_part.astype(jnp.bfloat16), rate_portion)


def solution(mesh):
    return jax.shard_map(
        shards,
        mesh=mesh,
        in_specs=(
            P(("parts", "tm"), "types"),
            P(("parts", "tm"), "types"),
            P("types"),
            P(None, "types", None, None, None),
            P(),
            P(),
        ),
        out_specs=(P("parts", "types", None, "tm", None), P(("parts", "types", "tm"))),
        check_vma=False,
    )
```

profile of v0, /device:TPU:0, one launch (start us, length us, event | category | flops | bytes accessed | tf_op | source)
XLA Modules:
  0.0 442.5 jit_solution(10473754793142476016)
XLA Ops:
  7.3 0.7 lt.96
  8.2 0.8 copy.46
  9.9 1.9 all_gather.6
  12.1 1.5 multiply_convert_fusion
  13.7 2.1 fusion.6
  15.8 2.0 copy-done
  17.8 1.8 all-gather
  19.8 2.9 copy_bitcast_fusion
  22.7 6.3 %gather_fusion = bf16[48,4,256,128]{3,2,1,0:T(8,128)(2,1)} fusion(bf16[4,256,8,128]{3,1,2,0:T(8,128)(2,1)S(1)} %copy_bitcast_fusion, s32[1024]{0:T(1024)S(1)} %pad_clamp_fusion.1), kind=kCustom, calls=%fused_computation | custom fusion | bytes 25166016 | tf_op jit(solution)/shard_map/jit(_take)/gather | solution.py:82
  29.0 16.7 %copy.53 = bf16[4,256,48,128]{1,3,2,0:T(8,128)(2,1)} copy(bf16[4,256,48,128]{3,1,0,2:T(8,128)(2,1)} %bitcast.49) | data formatting | bytes 25165824 | tf_op jit(solution)/shard_map/jit(_take)/gather | solution.py:82
  45.7 6.5 %bitcast_select_fusion = bf16[4,256,8,768]{1,3,2,0:T(8,128)(2,1)S(1)} fusion(pred[8,768]{1,0:T(8,128)(4,1)S(1)} %broadcast_bitcast_fusion, bf16[4,256,8,768]{1,3,2,0:T(8,128)(2,1)} %bitcast.50), kind=kLoop, calls=%fused_computation.6 | loop fusion | flops 6291456 | bytes 25171968 | tf_op jit(solution)/shard_map/jit(_take)/select_n | solution.py:82
  52.2 5.2 %copy.54 = bf16[4,256,8,768]{1,3,0,2:T(8,128)(2,1)} copy(bf16[4,256,8,768]{1,3,2,0:T(8,128)(2,1)S(1)} %bitcast_select_fusion) | data formatting | bytes 25165824 | tf_op jit(solution)/shard_map/jit(_take)/select_n | solution.py:82
  57.4 7.1 %all-to-all-start = ((bf16[4,256,8,768]{1,3,0,2:T(8,128)(2,1)}), bf16[4,256,8,768]{1,3,0,2:T(8,128)(2,1)}, u32[]{:S(2)}, u32[]{:S(2)}) async-start(bf16[4,256,8,768]{1,3,0,2:T(8,128)(2,1)} %copy.54), calls=%async_computation | async-start | bytes 25165824 | tf_op jit(solution)/shard_map/all_to_all | solution.py:85
  65.2 272.8 %all-to-all-done = bf16[4,256,8,768]{1,3,0,2:T(8,128)(2,1)} async-done(((bf16[4,256,8,768]{1,3,0,2:T(8,128)(2,1)}), bf16[4,256,8,768]{1,3,0,2:T(8,128)(2,1)}, u32[]{:S(2)}, u32[]{:S(2)}) %all-to-all-start) | async-done | bytes 12582944 | tf_op jit(solution)/shard_map/all_to_all | solution.py:85
  338.1 10.6 %copy.55 = bf16[4,256,8,768]{1,3,2,0:T(8,128)(2,1)} copy(bf16[4,256,8,768]{1,3,0,2:T(8,128)(2,1)} %all-to-all-done) | data formatting | bytes 25165824 | tf_op jit(solution)/shard_map/all_to_all | solution.py:85
  348.6 16.6 %copy.56 = bf16[4,256,48,128]{3,1,2,0:T(8,128)(2,1)} copy(bf16[4,256,48,128]{1,3,2,0:T(8,128)(2,1)} %bitcast.48) | data formatting | bytes 25165824 | tf_op jit(solution)/shard_map/reshape | solution.py:86
  365.2 10.8 %gather_fusion.1 = bf16[48,4,256,128]{3,2,1,0:T(8,128)(2,1)} fusion(bf16[4,256,48,128]{3,1,2,0:T(8,128)(2,1)} %copy.56, s32[1024]{0:T(1024)S(1)} %pad_clamp_fusion), kind=kCustom, calls=%fused_computation.1 | custom fusion | bytes 25166016 | tf_op jit(solution)/shard_map/jit(_take)/gather | solution.py:87
  376.0 11.6 %copy.57 = bf16[4,256,48,128]{3,1,2,0:T(8,128)(2,1)} copy(bf16[4,256,48,128]{3,1,0,2:T(8,128)(2,1)} %bitcast.51) | data formatting | bytes 25165824 | tf_op jit(solution)/shard_map/jit(_take)/gather | solution.py:87
  387.6 8.5 %fusion.28 = f32[8,256,128,1,1]{1,2,4,0,3:T(8,128)S(1)} fusion(bf16[4,8,6,128,128]{4,3,2,1,0:T(8,128)(2,1)} %param.11, bf16[4,256,8,6,128]{4,1,3,2,0:T(8,128)(2,1)} %bitcast.52, pred[8,6]{1,0:T(8,128)(4,1)S(1)} %copy.50, pred[8,6]{1,0:T(8,128)(4,1)S(1)} %broadcast_in_dim.86), kind=kOutput, calls=%fused_computation.69 | convolution fusion | flops 1623195648 | bytes 19923040 | tf_op jit(solution)/shard_map/bispq,btisq->tip/dot_general | solution.py:90
  396.8 10.5 %convert_bitcast_fusion = bf16[4,8,6,128,128]{3,4,2,0,1:T(8,128)(2,1)} fusion(bf16[256,8,128,1,1]{2,1,0,4,3:T(8,128)(2,1)S(1)} %bitcast.55, bf16[4,256,8,6,128]{4,1,3,2,0:T(8,128)(2,1)} %bitcast.53, pred[8,6]{1,0:T(8,128)(4,1)S(1)} %copy.50, pred[8,6]{1,0:T(8,128)(4,1)S(1)} %broadcast_in_dim.86), kind=kOutput, calls=%fused_computation.8 | convolution fusion | flops 1626341376 | bytes 19398752 | tf_op jit(solution)/shard_map/tip,btisq->bispq/dot_general | solution.py:95
  407.3 9.0 %copy.61 = bf16[4,8,6,128,128]{4,1,2,0,3:T(8,128)(2,1)} copy(bf16[4,8,6,128,128]{3,4,2,0,1:T(8,128)(2,1)} %convert_bitcast_fusion) | data formatting | bytes 12582912 | tf_op jit(solution)/shard_map/convert_element_type | solution.py:100
  417.6 2.5 all-reduce
  420.7 9.4 %reduce-scatter.2.cloned.1.call-done = bf16[4,8,6,64,128]{4,1,2,0,3:T(8,128)(2,1)} async-done(((bf16[4,8,6,128,128]{4,1,2,0,3:T(8,128)(2,1)}), bf16[4,8,6,64,128]{4,1,2,0,3:T(8,128)(2,1)}) %reduce-scatter.2.cloned.1.call-update) | async-done | bytes 3145744 | tf_op jit(solution)/shard_map/reduce_scatter | solution.py:99
  430.1 5.6 %copy.62 = bf16[4,8,6,64,128]{4,3,2,1,0:T(8,128)(2,1)} copy(bf16[4,8,6,64,128]{4,1,2,0,3:T(8,128)(2,1)} %reduce-scatter.2.cloned.1.call-done) | data formatting | bytes 6291456
  (51 shorter events, 4.2 us)
Async XLA Ops:
  15.8 2.0 copy-start
  57.4 280.6 %all-to-all-start = ((bf16[4,256,8,768]{1,3,0,2:T(8,128)(2,1)}), bf16[4,256,8,768]{1,3,0,2:T(8,128)(2,1)}, u32[]{:S(2)}, u32[]{:S(2)}) async-start(bf16[4,256,8,768]{1,3,0,2:T(8,128)(2,1)} %copy.54), calls=%async_computation | async-start | bytes 25165824 | tf_op jit(solution)/shard_map/all_to_all | solution.py:85
  64.6 365.5 %reduce-scatter.2.cloned.1.call-start = ((), (), s32[]{:S(2)}) async-start(), calls=%async_computation.2 | async-start | bytes 9437184 | tf_op jit(solution)/shard_map/reduce_scatter | solution.py:99
  387.6 8.8 %copy-start.1 = (s32[256,1024]{1,0:T(8,128)S(1)}, s32[256,1024]{1,0:T(8,128)}, u32[]{:S(2)}) copy-start(s32[256,1024]{1,0:T(8,128)} %param.8) | copy-start | bytes 3145732
  387.6 8.8 %copy-start.2 = (f32[1024]{0:T(1024)S(1)}, f32[1024]{0:T(1024)}, u32[]{:S(2)}) copy-start(f32[1024]{0:T(1024)} %param.10) | copy-start | bytes 12292
  407.3 9.1 %copy-start.3 = (u32[32]{0:T(128)S(1)}, u32[32]{0:T(128)}, u32[]{:S(2)}) copy-start(u32[32]{0:T(128)} %constant.114) | copy-start | bytes 388
Sparse Core Ops, SparseCore 0:
  416.5 13.5 reduce-scatter.1
where the time goes:
time: 444 us; the launch traced here: 443 us
  waiting for transfers between devices  282 us (64%)
  local copies, waits for them, and re-layouts  97.9 us (22%)
  matrix products  21.1 us (5%)
  between operations  14.9 us (3%)
  other arithmetic  12.9 us (3%)
  starting transfers between devices  7.34 us (2%)
  blocking collectives  6.22 us (1%)
    all_to_all x1, waiting for transfers between devices, shards(): lax.all_to_all(outgoing, 'types', split_axis=2, concat_axis=2, tiled=True)  273 us
    gather x2, local copies, waits for them, and re-layouts, shards(): jnp.take(state_bf, local_block, axis=2)  23 us
    gather x2, local copies, waits for them, and re-layouts, shards(): gathered = jnp.take(received, own_slots, axis=2)  22.4 us
    reshape x1, local copies, waits for them, and re-layouts, shards(): received.reshape(basis_count, bins, type_devices * capacity, tile_size)  16.6 us
    all_to_all x1, local copies, waits for them, and re-layouts, shards(): lax.all_to_all(outgoing, 'types', split_axis=2, concat_axis=2, tiled=True)  10.6 us
    dot_general x1, matrix products, shards(): jnp.einsum('tip,btisq->bispq', weighted_bf, stacked, preferred_element_ty...  10.5 us
    reduce_scatter x1, waiting for transfers between devices, shards(): lax.psum_scatter(excite_grad.astype(jnp.bfloat16), 'tm', scatter_dimensio...  9.36 us
    convert_element_type x1, local copies, waits for them, and re-layouts, shards(): excite_grad.astype(jnp.bfloat16)  9.04 us
  transfers between devices with their start and end apart: 2, of which 2 were waited for; matrix products, arithmetic and copies ran while one was open for 0% of the time, Pallas kernels for 0%

commit v1 on v0

v1 whole, which is shorter than its diff:
```python
import functools
import jax
import jax.numpy as jnp
from jax import lax
from jax.experimental import pallas as pl
from jax.experimental.pallas import tpu as pltpu
from jax.sharding import PartitionSpec as P


def lag_tables(bins, basis_count, overall):
    log_decay = -(8.0 ** jnp.arange(basis_count, dtype=jnp.float32)) / (2.0 * overall)
    t = jnp.arange(bins, dtype=jnp.float32)
    lag = t[:, None] - 1.0 - t[None, :]
    weights = jnp.where(
        lag[None] >= 0.0,
        (1.0 - jnp.exp(log_decay))[:, None, None]
        * jnp.exp(jnp.maximum(lag, 0.0)[None] * log_decay[:, None, None]),
        jnp.float32(0.0),
    )
    power = jnp.exp(t[None, :, None] * log_decay[:, None, None])
    return weights.astype(jnp.bfloat16), jnp.broadcast_to(power, (basis_count, bins, 128))


def prepare_kernel(basis_count, overall, counts_ref, mark_ref, impact_ref, ends_ref):
    bins = counts_ref.shape[0]
    impact = (counts_ref[...].astype(jnp.float32) * mark_ref[...].astype(jnp.float32)).astype(
        jnp.bfloat16
    )
    impact_ref[...] = impact
    impact = impact.astype(jnp.float32)
    back = (bins - 1 - lax.broadcasted_iota(jnp.int32, (bins, 1), 0)).astype(jnp.float32)
    rows = []
    for b in range(basis_count):
        rate = (8.0**b) / (2.0 * overall)
        gain = (1.0 - jnp.exp(jnp.full((bins, 1), -rate, jnp.float32))) * jnp.exp(-rate * back)
        rows.append(jnp.sum(impact * gain, axis=0, keepdims=True))
    ends_ref[...] = jnp.concatenate(rows, axis=0)


def prepare(counts, mark, basis_count, overall):
    bins, types = counts.shape
    lanes = min(types, 256)
    return pl.pallas_call(
        functools.partial(prepare_kernel, basis_count, overall),
        grid=(types // lanes,),
        in_specs=[
            pl.BlockSpec((bins, lanes), lambda i: (0, i)),
            pl.BlockSpec((bins, lanes), lambda i: (0, i)),
        ],
        out_specs=[
            pl.BlockSpec((bins, lanes), lambda i: (0, i)),
            pl.BlockSpec((basis_count, lanes), lambda i: (0, i)),
        ],
        out_shape=[
            jax.ShapeDtypeStruct((bins, types), jnp.bfloat16),
            jax.ShapeDtypeStruct((basis_count, types), jnp.float32),
        ],
        compiler_params=pltpu.CompilerParams(vmem_limit_bytes=32 << 20),
        name="impact",
    )(counts, mark)


def rows_kernel(basis, slots, brows, overall, place_ref, col_ref, fill_ref, *refs):
    blocks = refs[:slots]
    carries = refs[slots : 2 * slots]
    (excite_ref, counts_ref, base_ref, lag_ref, power_ref, mine_ref, other_ref, rate_ref, states) = (
        refs[2 * slots :]
    )
    row = pl.program_id(0)
    own, half = place_ref[0], place_ref[1]
    bins = counts_ref.shape[0]
    tile = excite_ref.shape[-1]
    depth = basis * tile
    fill = fill_ref[own * brows + row]
    excited = jnp.zeros((bins, tile), jnp.float32)

    def build(pair):
        both = jnp.concatenate([blocks[2 * pair][0], blocks[2 * pair + 1][0]], axis=1)
        for b in range(basis):
            state = jnp.dot(lag_ref[b], both, preferred_element_type=jnp.float32)
            for k in range(2):
                s = 2 * pair + k
                carried = power_ref[b] * carries[s][0, b : b + 1, :]
                states[s, :, b * tile : (b + 1) * tile] = (
                    state[:, k * tile : (k + 1) * tile] + carried
                ).astype(jnp.bfloat16)

    total = jnp.zeros((bins, tile), jnp.float32)
    for pair in range(slots // 2):
        if pair == 0:
            build(0)
        else:
            pl.when(2 * pair < fill)(functools.partial(build, pair))
    for s in range(slots):
        weights = jnp.concatenate([excite_ref[b, 0, s] for b in range(basis)], axis=1)
        live = s < fill
        weights = jnp.where(live, weights, jnp.zeros_like(weights))
        state = jnp.where(live, states[s], jnp.zeros_like(states[s]))
        total = total + lax.dot_general(
            state, weights, (((1,), (1,)), ((), ())), preferred_element_type=jnp.float32
        )
    del excited
    intensity = total + base_ref[...]
    weighted = (2.0 / overall) * (intensity - counts_ref[...].astype(jnp.float32))
    rate_ref[0] = jnp.sum(weighted, axis=0, keepdims=True)
    turned = weighted.T.astype(jnp.bfloat16)
    part = tile // 2
    first, last = turned[:part], turned[part:]
    own_first = half == 0
    turned = jnp.concatenate(
        [jnp.where(own_first, first, last), jnp.where(own_first, last, first)], axis=0
    )
    for s in range(slots):
        live = s < fill

        @pl.when(live)
        def _(s=s):
            grad = jnp.dot(turned, states[s], preferred_element_type=jnp.float32).astype(
                jnp.bfloat16
            )
            for b in range(basis):
                piece = grad[:, b * tile : (b + 1) * tile]
                mine_ref[b, 0, s] = piece[:part]
                other_ref[b, 0, s] = piece[part:]

        @pl.when(jnp.logical_not(live))
        def _(s=s):
            for b in range(basis):
                mine_ref[b, 0, s] = jnp.zeros((part, tile), jnp.bfloat16)
                other_ref[b, 0, s] = jnp.zeros((part, tile), jnp.bfloat16)


def rows(place, cols, fill, gathered, entering, excite, counts, base_rate, lag, power, overall):
    basis, brows, slots, tile, _ = excite.shape
    bins = counts.shape[0]
    width = gathered.shape[2] // tile

    def block_at(s):
        def index(i, place, cols, fill):
            c = cols[(place[0] * brows + i) * slots + s]
            return lax.div(c, width), 0, lax.rem(c, width)

        return index

    whole3 = lambda i, *_: (0, 0, 0)
    part = tile // 2
    out_block = pl.BlockSpec((basis, 1, slots, part, tile), lambda i, *_: (0, i, 0, 0, 0))
    out_shape = jax.ShapeDtypeStruct((basis, brows, slots, part, tile), jnp.bfloat16)
    return pl.pallas_call(
        functools.partial(rows_kernel, basis, slots, brows, overall),
        grid_spec=pltpu.PrefetchScalarGridSpec(
            num_scalar_prefetch=3,
            grid=(brows,),
            in_specs=[pl.BlockSpec((1, bins, tile), block_at(s)) for s in range(slots)]
            + [pl.BlockSpec((1, basis, tile), block_at(s)) for s in range(slots)]
            + [
                pl.BlockSpec((basis, 1, slots, tile, tile), lambda i, *_: (0, i, 0, 0, 0)),
                pl.BlockSpec((bins, tile), lambda i, *_: (0, i)),
                pl.BlockSpec((1, tile), lambda i, *_: (0, i)),
                pl.BlockSpec((basis, bins, bins), whole3),
                pl.BlockSpec((basis, bins, tile), whole3),
            ],
            out_specs=[out_block, out_block, pl.BlockSpec((1, 1, tile), lambda i, *_: (i, 0, 0))],
            scratch_shapes=[pltpu.VMEM((slots, bins, basis * tile), jnp.bfloat16)],
        ),
        out_shape=[out_shape, out_shape, jax.ShapeDtypeStruct((brows, 1, tile), jnp.float32)],
        compiler_params=pltpu.CompilerParams(vmem_limit_bytes=40 << 20),
        name="rows",
    )(
        place,
        cols,
        fill,
        *([gathered] * slots),
        *([entering] * slots),
        excite,
        counts,
        base_rate.reshape(1, -1),
        lag,
        power,
    )


def shards(counts, mark_value, base_rate, excite, block_col, row_fill):
    basis, brows, slots, tile, _ = excite.shape
    bins = counts.shape[0]
    overall = bins * lax.axis_size("tm")
    half = lax.axis_index("tm")
    place = jnp.stack([lax.axis_index("types"), half]).astype(jnp.int32)
    impact, ends = prepare(counts, mark_value, basis, overall)
    gathered = lax.all_gather(impact, "types")
    entering = lax.all_gather(lax.ppermute(ends, "tm", [(0, 1)]), "types")
    lag, power = lag_tables(bins, basis, overall)
    mine, other, rate = rows(
        place,
        block_col.reshape(-1),
        row_fill,
        gathered,
        entering,
        excite,
        counts,
        base_rate,
        lag,
        power,
        overall,
    )
    swap = [(0, 1), (1, 0)]
    rate = rate.reshape(2, -1)
    got = lax.ppermute(other, "tm", swap)
    rate_got = lax.ppermute(lax.dynamic_index_in_dim(rate, 1 - half, 0, False), "tm", swap)
    grad = (mine.astype(jnp.float32) + got.astype(jnp.float32)).astype(jnp.bfloat16)
    return grad, lax.dynamic_index_in_dim(rate, half, 0, False) + rate_got


def solution(mesh):
    return jax.shard_map(
        shards,
        mesh=mesh,
        in_specs=(
            P(("parts", "tm"), "types"),
            P(("parts", "tm"), "types"),
            P("types"),
            P(None, "types", None, None, None),
            P(),
            P(),
        ),
        out_specs=(P("parts", "types", None, "tm", None), P(("parts", "types", "tm"))),
        check_vma=False,
    )
```

time: 444 us -> 136 us (0.31)
  waiting for transfers between devices: 282 us -> 45.4 us
  local copies, waits for them, and re-layouts: 97.9 us -> 7.08 us
  blocking collectives: 6.22 us -> 32.3 us
  Pallas kernels: 0 us -> 25.1 us
  matrix products: 21.1 us -> 0 us
  other arithmetic: 12.9 us -> 8.31 us
    all_to_all x1 -> x0, waiting for transfers between devices: 273 us -> none  [shards(): lax.all_to_all(outgoing, 'types', split_axis=2, concat_axis=2, tiled=True)]
    gather x4 -> x0, local copies, waits for them, and re-layouts: 45.4 us -> none  [the longest x2 23 us: shards(): jnp.take(state_bf, local_block, axis=2)]
    all_gather x0 -> x1, waiting for transfers between devices: none -> 41.5 us  [shards(): gathered = lax.all_gather(impact, 'types')]
    all_gather x2 -> x1, blocking collectives: 3.75 us -> 32.3 us  [shards(): entering = lax.all_gather(lax.ppermute(ends, 'tm', [(0, 1)]), 'types')]
    pallas_call x0 -> x2, Pallas kernels: none -> 25.1 us  [the longest x1 23.1 us: rows(): pl.pallas_call(functools.partial(rows_kernel, basis, slots, brows, overal...]
    dot_general x3 -> x0, matrix products: 21.1 us -> none  [the longest x1 10.5 us: shards(): jnp.einsum('tip,btisq->bispq', weighted_bf, stacked, preferred_element_ty...]
    reshape x4 -> x2, local copies, waits for them, and re-layouts: 17.1 us -> 0.15 us  [the longest x1 0.14 us: shards(): block_col.reshape(-1)]
    all_to_all x1 -> x0, local copies, waits for them, and re-layouts: 10.6 us -> none  [shards(): lax.all_to_all(outgoing, 'types', split_axis=2, concat_axis=2, tiled=True)]
  transfers between devices with their start and end apart: 2 -> 4, of which waited for: 2 -> 2; matrix products, arithmetic and copies ran while one was open for 0% -> 2% of each run, Pallas kernels for 0% -> 0%
where the time goes in v1:
time: 136 us; the launch traced here: 135 us
  waiting for transfers between devices  45.4 us (33%)
  blocking collectives  32.3 us (24%)
  Pallas kernels  25.1 us (18%)
  between operations  14.2 us (10%)
  other arithmetic  8.31 us (6%)
  local copies, waits for them, and re-layouts  7.08 us (5%)
  starting transfers between devices  2.97 us (2%)
    all_gather x1, waiting for transfers between devices, shards(): gathered = lax.all_gather(impact, 'types')  41.5 us
    all_gather x1, blocking collectives, shards(): entering = lax.all_gather(lax.ppermute(ends, 'tm', [(0, 1)]), 'types')  32.3 us
    pallas_call x1, Pallas kernels, rows(): pl.pallas_call(functools.partial(rows_kernel, basis, slots, brows, overal...  23.1 us
    convert_element_type x1, other arithmetic, shards(): (mine.astype(jnp.float32) + got.astype(jnp.float32)).astype(jnp.bfloat16)  6.39 us
    unnamed x17, local copies, waits for them, and re-layouts  6.22 us
    ppermute x1, waiting for transfers between devices, shards(): lax.ppermute(lax.dynamic_index_in_dim(rate, 1 - half, 0, False), 'tm', swap)  3.87 us
  transfers between devices with their start and end apart: 4, of which 2 were waited for; matrix products, arithmetic and copies ran while one was open for 2% of the time, Pallas kernels for 0%

profile of v1, /device:TPU:0, one launch (start us, length us, event | category | flops | bytes accessed | tf_op | source)
XLA Modules:
  0.0 135.3 jit_solution(17606684134022702867)
XLA Ops:
  7.2 0.0 all-gather.5.cloned.1.call-start
  7.2 1.2 copy-done.1
  8.4 1.0 copy-done.4
  9.5 2.0 %impact.1 = (bf16[256,1024]{1,0:T(8,128)(2,1)}, f32[4,1024]{1,0:T(4,128)S(1)}) custom-call(s32[256,1024]{1,0:T(8,128)S(1)} %copy-done.1, bf16[256,1024]{1,0:T(8,128)(2,1)S(1)} %copy-done.4), custom_call_target="tpu_custom_call" | custom-call | tf_op jit(solution)/shard_map/impact/pallas_call | solution.py:43
  11.5 2.4 %collective-permute-start = (f32[4,1024]{1,0:T(4,128)S(1)}, f32[4,1024]{1,0:T(4,128)S(1)}, u32[]{:S(2)}, u32[]{:S(2)}) collective-permute-start(f32[4,1024]{1,0:T(4,128)S(1)} %get-tuple-element.8), channel_id=1, source_target_pairs={{0,1},{2,3},{4,5},{6,7},{8,9},{10,11},{12,13},{14,15},{16,17},{18,... | collective-permute-start | bytes 49160 | tf_op jit(solution)/shard_map/ppermute | solution.py:191
  13.9 0.1 multiply_exponential_fusion
  14.0 0.1 fusion.1
  14.1 0.1 fusion
  14.2 0.3 select_convert_fusion.refs_15_
  14.5 0.1 pad_add_fusion.place_ref
  14.6 0.1 copy.9
  14.7 0.1 reshape.90.col_ref
  14.9 32.3 %all-gather.2.refs_6_.refs_7_.refs_8_.refs_9_.refs_10_.refs_11_ = f32[8,4,1024]{2,1,0:T(4,128)S(1)} all-gather(f32[1,4,1024]{2,1,0:T(4,128)S(1)} %bitcast.14), channel_id=3, replica_groups=mesh['parts'=2,'types'=8,'tm'=2] {'types'}, dimensions={0}, use_global_device_ids=true | all-gather | bytes 147456 | tf_op jit(solution)/shard_map/all_gather | solution.py:191
  47.1 41.5 %all-gather.5.cloned.1.call-done = bf16[2048,1024]{1,0:T(8,128)(2,1)} async-done(((bf16[256,1024]{1,0:T(8,128)(2,1)}), bf16[2048,1024]{1,0:T(8,128)(2,1)}) %all-gather.5.cloned.1.call-update) | async-done | bytes 4194320 | tf_op jit(solution)/shard_map/all_gather | solution.py:190
  88.7 0.2 broadcast_in_dim.16.refs_16_
  88.9 2.2 %copy-done = bf16[2048,1024]{1,0:T(8,128)(2,1)S(1)} copy-done((bf16[2048,1024]{1,0:T(8,128)(2,1)S(1)}, bf16[2048,1024]{1,0:T(8,128)(2,1)}, u32[]{:S(2)}) %copy-start) | copy-done | bytes 4194328
  91.1 23.1 %rows.1 = (bf16[4,8,6,64,128]{4,3,2,1,0:T(8,128)(2,1)S(1)}, bf16[4,8,6,64,128]{4,3,2,1,0:T(8,128)(2,1)}, f32[8,1,128]{2,1,0:T(1,128)S(1)}) custom-call(s32[2]{0:T(128)S(1)} %pad_add_fusion.place_ref, s32[384]{0:T(512)S(1)} %reshape.90.col_ref, s32[64]{0:T(128)S(1)} %copy-done.6, bf16[8,256,1024]{2,1,0:T(8,128)(2,1)S(1)} %bitcast.7, ...), custom_call_target="tpu_custom_call" | custom-call | tf_op jit(solution)/shard_map/rows/pallas_call | solution.py:149
  114.2 1.7 %copy-done.3 = bf16[4,8,6,64,128]{4,3,2,1,0:T(8,128)(2,1)} copy-done((bf16[4,8,6,64,128]{4,3,2,1,0:T(8,128)(2,1)}, bf16[4,8,6,64,128]{4,3,2,1,0:T(8,128)(2,1)S(1)}, u32[]{:S(2)}) %copy-start.3) | copy-done | bytes 3145752
  115.9 0.5 broadcast.95
  116.4 0.7 reduce.3
  117.1 0.6 collective-permute-start.2
  117.6 3.9 %collective-permute-done.2 = f32[512]{0:T(512)S(1)} collective-permute-done((f32[512]{0:T(512)S(1)}, f32[512]{0:T(512)S(1)}, u32[]{:S(2)}, u32[]{:S(2)}) %collective-permute-start.2) | collective-permute-done | bytes 2080 | tf_op jit(solution)/shard_map/ppermute | solution.py:209
  121.5 0.6 add.23
  122.1 6.4 %add_convert_fusion = bf16[4,8,6,64,128]{4,3,2,1,0:T(8,128)(2,1)} fusion(bf16[4,8,6,64,128]{4,3,2,1,0:T(8,128)(2,1)} %collective-permute-done.1, bf16[4,8,6,64,128]{4,3,2,1,0:T(8,128)(2,1)} %copy-done.3), kind=kLoop, calls=%fused_computation | loop fusion | flops 6291456 | bytes 9437184 | tf_op jit(solution)/shard_map/convert_element_type | solution.py:210
  (20 shorter events, 0.1 us)
Async XLA Ops:
  7.2 81.5 %all-gather.5.cloned.1.call-start = ((), (), s32[]{:S(2)}) async-start(), calls=%async_computation | async-start | bytes 4718592 | tf_op jit(solution)/shard_map/all_gather | solution.py:190
  7.2 1.2 copy-start.1
  8.4 1.0 copy-start.4
  9.5 5.1 %copy-start.7 = (s32[64,6]{0,1:T(8,128)S(1)}, s32[64,6]{0,1:T(8,128)}, u32[]{:S(2)}) copy-start(s32[64,6]{0,1:T(8,128)} %param.10) | copy-start | bytes 4612
  9.5 79.4 %copy-start.2 = (s32[256,1024]{1,0:T(8,128)S(1)}, s32[256,1024]{1,0:T(8,128)}, u32[]{:S(2)}) copy-start(s32[256,1024]{1,0:T(8,128)} %refs_13_.1) | copy-start | bytes 3145732
  9.5 79.4 %copy-start.5 = (f32[1024]{0:T(1024)S(1)}, f32[1024]{0:T(1024)}, u32[]{:S(2)}) copy-start(f32[1024]{0:T(1024)} %param.8) | copy-start | bytes 12292
  9.5 79.4 %copy-start.6 = (s32[64]{0:T(128)S(1)}, s32[64]{0:T(128)}, u32[]{:S(2)}) copy-start(s32[64]{0:T(128)} %fill_ref.1) | copy-start | bytes 772
  11.5 3.3 %collective-permute-start = (f32[4,1024]{1,0:T(4,128)S(1)}, f32[4,1024]{1,0:T(4,128)S(1)}, u32[]{:S(2)}, u32[]{:S(2)}) collective-permute-start(f32[4,1024]{1,0:T(4,128)S(1)} %get-tuple-element.8), channel_id=1, source_target_pairs={{0,1},{2,3},{4,5},{6,7},{8,9},{10,11},{12,13},{14,15},{16,17},{18,... | collective-permute-start | bytes 49160 | tf_op jit(solution)/shard_map/ppermute | solution.py:191
  88.9 2.2 %copy-start = (bf16[2048,1024]{1,0:T(8,128)(2,1)S(1)}, bf16[2048,1024]{1,0:T(8,128)(2,1)}, u32[]{:S(2)}) copy-start(bf16[2048,1024]{1,0:T(8,128)(2,1)} %all-gather.5.cloned.1.call-done) | copy-start | bytes 12582916
  114.2 1.7 %copy-start.3 = (bf16[4,8,6,64,128]{4,3,2,1,0:T(8,128)(2,1)}, bf16[4,8,6,64,128]{4,3,2,1,0:T(8,128)(2,1)S(1)}, u32[]{:S(2)}) copy-start(bf16[4,8,6,64,128]{4,3,2,1,0:T(8,128)(2,1)S(1)} %get-tuple-element.9) | copy-start | bytes 9437188
  115.9 6.2 %collective-permute-start.1 = (bf16[4,8,6,64,128]{4,3,2,1,0:T(8,128)(2,1)}, bf16[4,8,6,64,128]{4,3,2,1,0:T(8,128)(2,1)}, u32[]{:S(2)}, u32[]{:S(2)}) collective-permute-start(bf16[4,8,6,64,128]{4,3,2,1,0:T(8,128)(2,1)} %get-tuple-element.10), channel_id=1, source_target_pairs={{0,1},{1,0},{2,3},{3,2},{4,5},{5,4},{6,7},{7,6},{8,9},{9,8},{10,11... | collective-permute-start | bytes 9437192 | tf_op jit(solution)/shard_map/ppermute | solution.py:208
  117.1 4.4 %collective-permute-start.2 = (f32[512]{0:T(512)S(1)}, f32[512]{0:T(512)S(1)}, u32[]{:S(2)}, u32[]{:S(2)}) collective-permute-start(f32[512]{0:T(512)S(1)} %bitcast.16), channel_id=1, source_target_pairs={{0,1},{1,0},{2,3},{3,2},{4,5},{5,4},{6,7},{7,6},{8,9},{9,8},{10,11... | collective-permute-start | bytes 6152 | tf_op jit(solution)/shard_map/ppermute | solution.py:209
Sparse Core Ops, SparseCore 0:
  11.7 76.9 all-gather.4

commit v2 on v1

v2 whole, which is shorter than its diff:
```python
import functools
import jax
import jax.numpy as jnp
from jax import lax
from jax.experimental import pallas as pl
from jax.experimental.pallas import tpu as pltpu
from jax.sharding import PartitionSpec as P

STREAMS = 4
CARRY_ROWS = 16


def lag_tables(bins, basis_count, overall, lanes):
    log_decay = -(8.0 ** jnp.arange(basis_count, dtype=jnp.float32)) / (2.0 * overall)
    t = jnp.arange(bins, dtype=jnp.float32)
    lag = t[:, None] - 1.0 - t[None, :]
    weights = jnp.where(
        lag[None] >= 0.0,
        (1.0 - jnp.exp(log_decay))[:, None, None]
        * jnp.exp(jnp.maximum(lag, 0.0)[None] * log_decay[:, None, None]),
        jnp.float32(0.0),
    )
    power = jnp.exp(t[None, :, None] * log_decay[:, None, None])
    return weights.astype(jnp.bfloat16), jnp.broadcast_to(power, (basis_count, bins, lanes))


def impact_of(counts_ref, mark_ref, lanes):
    counts = counts_ref[:, lanes].astype(jnp.float32)
    return (counts * mark_ref[:, lanes].astype(jnp.float32)).astype(jnp.bfloat16)


def first_kernel(basis, overall, counts_ref, mark_ref, up_ref, down_ref, ends_ref):
    bins, types = counts_ref.shape
    lanes = types // STREAMS
    back = (bins - 1 - lax.broadcasted_iota(jnp.int32, (bins, 1), 0)).astype(jnp.float32)
    gains = []
    for b in range(basis):
        rate = (8.0**b) / (2.0 * overall)
        gains.append((1.0 - jnp.exp(jnp.full((bins, 1), -rate, jnp.float32))) * jnp.exp(-rate * back))
    for j in range(STREAMS):
        impact = impact_of(counts_ref, mark_ref, slice(j * lanes, (j + 1) * lanes))
        if j == 0:
            up_ref[...] = impact
        if j == 2:
            down_ref[...] = impact
        impact = impact.astype(jnp.float32)
        for b in range(basis):
            ends_ref[b : b + 1, j * lanes : (j + 1) * lanes] = jnp.sum(
                impact * gains[b], axis=0, keepdims=True
            )


def second_kernel(basis, counts_ref, mark_ref, enter_ref, up_ref, down_ref):
    bins, types = counts_ref.shape
    lanes = types // STREAMS
    for j, out_ref in ((1, up_ref), (3, down_ref)):
        out_ref[:bins] = impact_of(counts_ref, mark_ref, slice(j * lanes, (j + 1) * lanes))
        carry = jnp.concatenate(
            [enter_ref[:, (j - 1) * lanes : j * lanes], enter_ref[:, j * lanes : (j + 1) * lanes]],
            axis=0,
        )
        pad = jnp.zeros((CARRY_ROWS - 2 * basis, lanes), jnp.float32)
        out_ref[bins:] = jnp.concatenate([carry, pad], axis=0).astype(jnp.bfloat16)


def first(counts, mark, basis, overall):
    bins, types = counts.shape
    chunk = jax.ShapeDtypeStruct((bins, types // STREAMS), jnp.bfloat16)
    return pl.pallas_call(
        functools.partial(first_kernel, basis, overall),
        out_shape=[chunk, chunk, jax.ShapeDtypeStruct((basis, types), jnp.float32)],
        compiler_params=pltpu.CompilerParams(vmem_limit_bytes=32 << 20),
        name="first_chunks",
    )(counts, mark)


def second(counts, mark, enter, basis):
    bins, types = counts.shape
    chunk = jax.ShapeDtypeStruct((bins + CARRY_ROWS, types // STREAMS), jnp.bfloat16)
    return pl.pallas_call(
        functools.partial(second_kernel, basis),
        out_shape=[chunk, chunk],
        compiler_params=pltpu.CompilerParams(vmem_limit_bytes=32 << 20),
        name="second_chunks",
    )(counts, mark, enter)


def states_kernel(basis, step, tile, *refs):
    chunks = refs[:STREAMS]
    lag_ref, power_ref = refs[STREAMS : STREAMS + 2]
    out_ref, held, sems = refs[-3:]
    bins, lanes = chunks[0].shape
    per = lanes // tile
    copies = []
    for j in range(STREAMS):
        impact = chunks[j][:bins] if j % 2 else chunks[j][...]
        carry = chunks[j | 1][bins:].astype(jnp.float32)
        for b in range(basis):
            state = jnp.dot(lag_ref[b], impact, preferred_element_type=jnp.float32)
            row = (j % 2) * basis + b
            for q in range(per):
                at = slice(q * tile, (q + 1) * tile)
                held[j * per + q, :, b * tile : (b + 1) * tile] = (
                    state[:, at] + power_ref[b] * carry[row : row + 1, at]
                ).astype(jnp.bfloat16)
        copy = pltpu.make_async_copy(
            held.at[pl.ds(j * per, per)],
            out_ref.at[pl.ds((step * STREAMS + j) * per, per)],
            sems.at[j],
        )
        copy.start()
        copies.append(copy)
    for copy in copies:
        copy.wait()


def build_states(states, chunks, lag, power, step, steps, tile):
    basis, bins, _ = lag.shape
    lanes = chunks[0].shape[1]
    width = STREAMS * lanes // tile
    vmem = pl.BlockSpec(memory_space=pltpu.VMEM)
    given = [] if states is None else [states]
    return pl.pallas_call(
        functools.partial(states_kernel, basis, step, tile),
        in_specs=[vmem] * (STREAMS + 2) + [pl.BlockSpec(memory_space=pl.ANY)] * len(given),
        out_specs=pl.BlockSpec(memory_space=pl.ANY),
        out_shape=jax.ShapeDtypeStruct((steps * width, bins, basis * tile), jnp.bfloat16),
        scratch_shapes=[
            pltpu.VMEM((width, bins, basis * tile), jnp.bfloat16),
            pltpu.SemaphoreType.DMA((STREAMS,)),
        ],
        input_output_aliases={STREAMS + 2: 0} if given else {},
        compiler_params=pltpu.CompilerParams(vmem_limit_bytes=32 << 20),
        cost_estimate=pl.CostEstimate(
            flops=2 * basis * bins * bins * lanes * STREAMS,
            bytes_accessed=4 * 1024 * 1024,
            transcendentals=0,
        ),
        name="states",
    )(*chunks, lag, power, *given)


def rows_kernel(basis, slots, brows, overall, place_ref, col_ref, fill_ref, *refs):
    blocks = refs[:slots]
    excite_ref, counts_ref, base_ref, mine_ref, other_ref, rate_ref = refs[slots:]
    row = pl.program_id(0)
    own, half = place_ref[0], place_ref[1]
    tile = excite_ref.shape[-1]
    part = tile // 2
    fill = fill_ref[own * brows + row]
    weights = []
    for s in range(slots):
        weight = jnp.concatenate([excite_ref[b, 0, s] for b in range(basis)], axis=1)
        weights.append(jnp.where(s < fill, weight, jnp.zeros_like(weight)))
    state = jnp.concatenate([blocks[s][0] for s in range(slots)], axis=1)
    excited = lax.dot_general(
        state,
        jnp.concatenate(weights, axis=1),
        (((1,), (1,)), ((), ())),
        preferred_element_type=jnp.float32,
    )
    intensity = excited + base_ref[...]
    weighted = (2.0 / overall) * (intensity - counts_ref[...].astype(jnp.float32))
    rate_ref[0] = jnp.sum(weighted, axis=0, keepdims=True)
    turned = weighted.T.astype(jnp.bfloat16)
    upper, lower = turned[:part], turned[part:]
    turned = jnp.concatenate(
        [jnp.where(half == 0, upper, lower), jnp.where(half == 0, lower, upper)], axis=0
    )
    for s in range(slots):
        grad = jnp.dot(turned, blocks[s][0], preferred_element_type=jnp.float32)
        grad = jnp.where(s < fill, grad, jnp.zeros_like(grad)).astype(jnp.bfloat16)
        for b in range(basis):
            piece = grad[:, b * tile : (b + 1) * tile]
            mine_ref[b, 0, s] = piece[:part]
            other_ref[b, 0, s] = piece[part:]


def ring_place(index, n):
    return jnp.where(index % 2 == 0, index // 2, n - 1 - index // 2)


def rows(place, cols, fill, states, excite, counts, base_rate, overall, n):
    basis, brows, slots, tile, _ = excite.shape
    bins, types = counts.shape
    width = types // tile

    def block_at(s):
        def index(i, place, cols, fill):
            row = place[0] * brows + i
            c = cols[row * slots + s]
            block = lax.rem(c, width)
            ahead = ring_place(lax.div(c, width), n) - ring_place(place[0], n)
            ahead = jnp.where(block < width // 2, -ahead, ahead)
            ahead = jnp.where(ahead < 0, ahead + n, ahead)
            return jnp.where(s < fill[row], ahead * width + block, 0), 0, 0

        return index

    part = tile // 2
    out_block = pl.BlockSpec((basis, 1, slots, part, tile), lambda i, *_: (0, i, 0, 0, 0))
    out_shape = jax.ShapeDtypeStruct((basis, brows, slots, part, tile), jnp.bfloat16)
    return pl.pallas_call(
        functools.partial(rows_kernel, basis, slots, brows, overall),
        grid_spec=pltpu.PrefetchScalarGridSpec(
            num_scalar_prefetch=3,
            grid=(brows,),
            in_specs=[pl.BlockSpec((1, bins, basis * tile), block_at(s)) for s in range(slots)]
            + [
                pl.BlockSpec((basis, 1, slots, tile, tile), lambda i, *_: (0, i, 0, 0, 0)),
                pl.BlockSpec((bins, tile), lambda i, *_: (0, i)),
                pl.BlockSpec((1, tile), lambda i, *_: (0, i)),
            ],
            out_specs=[out_block, out_block, pl.BlockSpec((1, 1, tile), lambda i, *_: (i, 0, 0))],
        ),
        out_shape=[out_shape, out_shape, jax.ShapeDtypeStruct((brows, 1, tile), jnp.float32)],
        compiler_params=pltpu.CompilerParams(vmem_limit_bytes=40 << 20),
        name="rows",
    )(
        place,
        cols,
        fill,
        *([states] * slots),
        excite,
        counts,
        base_rate.reshape(1, -1),
    )


def shards(counts, mark_value, base_rate, excite, block_col, row_fill):
    basis, brows, slots, tile, _ = excite.shape
    bins = counts.shape[0]
    overall = bins * lax.axis_size("tm")
    n = lax.axis_size("types")
    half = lax.axis_index("tm")
    place = jnp.stack([lax.axis_index("types"), half]).astype(jnp.int32)
    order = list(range(0, n, 2)) + list(range(1, n, 2))[::-1]
    up = [(order[i], order[(i + 1) % n]) for i in range(n)]
    down = [(b, a) for a, b in up]
    up_one, down_one, ends = first(counts, mark_value, basis, overall)
    enter = lax.ppermute(ends, "tm", [(0, 1)])
    up_two, down_two = second(counts, mark_value, enter, basis)
    lag, power = lag_tables(bins, basis, overall, tile)
    chunks = [up_one, up_two, down_one, down_two]
    states = None
    for step in range(n):
        ahead = None
        if step < n - 1:
            ahead = [
                lax.ppermute(chunks[j], "types", up if j < STREAMS // 2 else down)
                for j in (0, 2, 1, 3)
            ]
            ahead = [ahead[0], ahead[2], ahead[1], ahead[3]]
        states = build_states(states, chunks, lag, power, step, n, tile)
        chunks = ahead
    mine, other, rate = rows(
        place, block_col.reshape(-1), row_fill, states, excite, counts, base_rate, overall, n
    )
    swap = [(0, 1), (1, 0)]
    rate = rate.reshape(2, -1)
    got = lax.ppermute(other, "tm", swap)
    rate_got = lax.ppermute(lax.dynamic_index_in_dim(rate, 1 - half, 0, False), "tm", swap)
    grad = (mine.astype(jnp.float32) + got.astype(jnp.float32)).astype(jnp.bfloat16)
    return grad, lax.dynamic_index_in_dim(rate, half, 0, False) + rate_got


def solution(mesh):
    return jax.shard_map(
        shards,
        mesh=mesh,
        in_specs=(
            P(("parts", "tm"), "types"),
            P(("parts", "tm"), "types"),
            P("types"),
            P(None, "types", None, None, None),
            P(),
            P(),
        ),
        out_specs=(P("parts", "types", None, "tm", None), P(("parts", "types", "tm"))),
        check_vma=False,
    )
```

time: 136 us -> 104 us (0.76)
  blocking collectives: 32.3 us -> 0 us
  waiting for transfers between devices: 45.4 us -> 13.3 us
  starting transfers between devices: 2.97 us -> 32.8 us
  local copies, waits for them, and re-layouts: 7.08 us -> 21.2 us
  between operations: 14.2 us -> 0.92 us
  Pallas kernels: 25.1 us -> 28.9 us
  other arithmetic: 8.31 us -> 6.95 us
    all_gather x1 -> x0, waiting for transfers between devices: 41.5 us -> none  [shards(): gathered = lax.all_gather(impact, 'types')]
    all_gather x1 -> x0, blocking collectives: 32.3 us -> none  [shards(): entering = lax.all_gather(lax.ppermute(ends, 'tm', [(0, 1)]), 'types')]
    ppermute x1 -> x29, starting transfers between devices: 2.36 us -> 32.2 us  [the longest x28 29.9 us: shards(): lax.ppermute(chunks[j], 'types', up if j < STREAMS // 2 else down)]
    unnamed x17 -> x21, local copies, waits for them, and re-layouts: 6.22 us -> 20.3 us
    pallas_call x1 -> x10, Pallas kernels: 2.02 us -> 12.1 us  [the longest x8 11.3 us: build_states(): pl.pallas_call(functools.partial(states_kernel, basis, step, tile), in_sp...]
    ppermute x1 -> x29, waiting for transfers between devices: 0.01 us -> 9.41 us  [the longest x28 9.41 us: shards(): lax.ppermute(chunks[j], 'types', up if j < STREAMS // 2 else down)]
    pallas_call x1, Pallas kernels: 23.1 us -> 16.8 us  [rows(): pl.pallas_call(functools.partial(rows_kernel, basis, slots, brows, overal...]
  transfers between devices with their start and end apart: 4 -> 31, of which waited for: 2 -> 8; matrix products, arithmetic and copies ran while one was open for 2% -> 3% of each run, Pallas kernels for 0% -> 10%
where the time goes in v2:
time: 104 us
  starting transfers between devices  32.8 us (32%)
  Pallas kernels  28.9 us (28%)
  local copies, waits for them, and re-layouts  21.2 us (20%)
  waiting for transfers between devices  13.3 us (13%)
  other arithmetic  6.95 us (7%)
    ppermute x28, starting transfers between devices, shards(): lax.ppermute(chunks[j], 'types', up if j < STREAMS // 2 else down)  29.9 us
    unnamed x21, local copies, waits for them, and re-layouts  20.3 us
    pallas_call x1, Pallas kernels, rows(): pl.pallas_call(functools.partial(rows_kernel, basis, slots, brows, overal...  16.8 us
    pallas_call x8, Pallas kernels, build_states(): pl.pallas_call(functools.partial(states_kernel, basis, step, tile), in_sp...  11.3 us
    ppermute x28, waiting for transfers between devices, shards(): lax.ppermute(chunks[j], 'types', up if j < STREAMS // 2 else down)  9.41 us
    convert_element_type x1, other arithmetic, shards(): (mine.astype(jnp.float32) + got.astype(jnp.float32)).astype(jnp.bfloat16)  5.05 us
    ppermute x1, waiting for transfers between devices, shards(): lax.ppermute(lax.dynamic_index_in_dim(rate, 1 - half, 0, False), 'tm', swap)  3.87 us
    ppermute x1, starting transfers between devices, shards(): enter = lax.ppermute(ends, 'tm', [(0, 1)])  2.35 us
  transfers between devices with their start and end apart: 31, of which 8 were waited for; matrix products, arithmetic and copies ran while one was open for 3% of the time, Pallas kernels for 10%

profile of v2, /device:TPU:0, one launch (start us, length us, event | category | flops | bytes accessed | tf_op | source)
XLA Modules:
  0.0 104.0 jit_solution(11228091124766999016)
XLA Ops:
  3.7 2.4 %collective-permute-start.7 = (f32[4,1024]{1,0:T(4,128)S(1)}, f32[4,1024]{1,0:T(4,128)S(1)}, u32[]{:S(2)}, u32[]{:S(2)}) collective-permute-start(f32[4,1024]{1,0:T(4,128)S(1)} %get-tuple-element.11), channel_id=1, source_target_pairs={{0,1},{2,3},{4,5},{6,7},{8,9},{10,11},{12,13},{14,15},{16,17},{18,... | collective-permute-start | bytes 49160 | tf_op jit(solution)/shard_map/ppermute | solution.py:241
  6.0 2.5 %collective-permute-start = (bf16[256,256]{1,0:T(8,128)(2,1)S(1)}, bf16[256,256]{1,0:T(8,128)(2,1)S(1)}, u32[]{:S(2)}, u32[]{:S(2)}) collective-permute-start(bf16[256,256]{1,0:T(8,128)(2,1)S(1)} %get-tuple-element.10.refs_0_), channel_id=1, source_target_pairs={{0,4},{4,8},{8,12},{12,14},{14,10},{10,6},{6,2},{2,0},{1,5},{5,9},... | collective-permute-start | bytes 393224 | tf_op jit(solution)/shard_map/ppermute | solution.py:250
  8.6 2.0 %collective-permute-start.22 = (bf16[272,256]{1,0:T(8,128)(2,1)S(1)}, bf16[272,256]{1,0:T(8,128)(2,1)S(1)}, u32[]{:S(2)}, u32[]{:S(2)}) collective-permute-start(bf16[272,256]{1,0:T(8,128)(2,1)S(1)} %get-tuple-element.14.refs_3_), channel_id=1, source_target_pairs={{4,0},{8,4},{12,8},{14,12},{10,14},{6,10},{2,6},{0,2},{5,1},{9,5},... | collective-permute-start | bytes 417800 | tf_op jit(solution)/shard_map/ppermute | solution.py:250
  12.0 2.5 %collective-permute-start.1 = (bf16[256,256]{1,0:T(8,128)(2,1)S(1)}, bf16[256,256]{1,0:T(8,128)(2,1)S(1)}, u32[]{:S(2)}, u32[]{:S(2)}) collective-permute-start(bf16[256,256]{1,0:T(8,128)(2,1)S(1)} %collective-permute-done.refs_0_), channel_id=1, source_target_pairs={{0,4},{4,8},{8,12},{12,14},{14,10},{10,6},{6,2},{2,0},{1,5},{5,9},... | collective-permute-start | bytes 393224 | tf_op jit(solution)/shard_map/ppermute | solution.py:250
  14.7 3.0 %collective-permute-done.22.refs_3_ = bf16[272,256]{1,0:T(8,128)(2,1)S(1)} collective-permute-done((bf16[272,256]{1,0:T(8,128)(2,1)S(1)}, bf16[272,256]{1,0:T(8,128)(2,1)S(1)}, u32[]{:S(2)}, u32[]{:S(2)}) %collective-permute-start.22) | collective-permute-done | bytes 139296 | tf_op jit(solution)/shard_map/ppermute | solution.py:250
  17.7 2.0 %collective-permute-start.9 = (bf16[272,256]{1,0:T(8,128)(2,1)S(1)}, bf16[272,256]{1,0:T(8,128)(2,1)S(1)}, u32[]{:S(2)}, u32[]{:S(2)}) collective-permute-start(bf16[272,256]{1,0:T(8,128)(2,1)S(1)} %collective-permute-done.8.refs_1_), channel_id=1, source_target_pairs={{0,4},{4,8},{8,12},{12,14},{14,10},{10,6},{6,2},{2,0},{1,5},{5,9},... | collective-permute-start | bytes 417800 | tf_op jit(solution)/shard_map/ppermute | solution.py:250
  21.1 1.8 %collective-permute-start.2 = (bf16[256,256]{1,0:T(8,128)(2,1)S(1)}, bf16[256,256]{1,0:T(8,128)(2,1)S(1)}, u32[]{:S(2)}, u32[]{:S(2)}) collective-permute-start(bf16[256,256]{1,0:T(8,128)(2,1)S(1)} %collective-permute-done.1.refs_0_), channel_id=1, source_target_pairs={{0,4},{4,8},{8,12},{12,14},{14,10},{10,6},{6,2},{2,0},{1,5},{5,9},... | collective-permute-start | bytes 393224 | tf_op jit(solution)/shard_map/ppermute | solution.py:250
  22.9 1.5 %collective-permute-done.9.refs_1_ = bf16[272,256]{1,0:T(8,128)(2,1)S(1)} collective-permute-done((bf16[272,256]{1,0:T(8,128)(2,1)S(1)}, bf16[272,256]{1,0:T(8,128)(2,1)S(1)}, u32[]{:S(2)}, u32[]{:S(2)}) %collective-permute-start.9) | collective-permute-done | bytes 139296 | tf_op jit(solution)/shard_map/ppermute | solution.py:250
  24.3 1.6 %collective-permute-start.10 = (bf16[272,256]{1,0:T(8,128)(2,1)S(1)}, bf16[272,256]{1,0:T(8,128)(2,1)S(1)}, u32[]{:S(2)}, u32[]{:S(2)}) collective-permute-start(bf16[272,256]{1,0:T(8,128)(2,1)S(1)} %collective-permute-done.9.refs_1_), channel_id=1, source_target_pairs={{0,4},{4,8},{8,12},{12,14},{14,10},{10,6},{6,2},{2,0},{1,5},{5,9},... | collective-permute-start | bytes 417800 | tf_op jit(solution)/shard_map/ppermute | solution.py:250
  30.5 2.0 %collective-permute-start.11 = (bf16[272,256]{1,0:T(8,128)(2,1)S(1)}, bf16[272,256]{1,0:T(8,128)(2,1)S(1)}, u32[]{:S(2)}, u32[]{:S(2)}) collective-permute-start(bf16[272,256]{1,0:T(8,128)(2,1)S(1)} %collective-permute-done.10.refs_1_), channel_id=1, source_target_pairs={{0,4},{4,8},{8,12},{12,14},{14,10},{10,6},{6,2},{2,0},{1,5},{5,9},... | collective-permute-start | bytes 417800 | tf_op jit(solution)/shard_map/ppermute | solution.py:250
  33.0 1.7 %collective-permute-done.18.refs_2_ = bf16[256,256]{1,0:T(8,128)(2,1)S(1)} collective-permute-done((bf16[256,256]{1,0:T(8,128)(2,1)S(1)}, bf16[256,256]{1,0:T(8,128)(2,1)S(1)}, u32[]{:S(2)}, u32[]{:S(2)}) %collective-permute-start.18) | collective-permute-done | bytes 131104 | tf_op jit(solution)/shard_map/ppermute | solution.py:250
  35.2 1.5 %collective-permute-start.4 = (bf16[256,256]{1,0:T(8,128)(2,1)S(1)}, bf16[256,256]{1,0:T(8,128)(2,1)S(1)}, u32[]{:S(2)}, u32[]{:S(2)}) collective-permute-start(bf16[256,256]{1,0:T(8,128)(2,1)S(1)} %collective-permute-done.3.refs_0_), channel_id=1, source_target_pairs={{0,4},{4,8},{8,12},{12,14},{14,10},{10,6},{6,2},{2,0},{1,5},{5,9},... | collective-permute-start | bytes 393224 | tf_op jit(solution)/shard_map/ppermute | solution.py:250
  39.0 1.4 %states.8.refs_6_ = bf16[64,256,512]{2,1,0:T(8,128)(2,1)S(1)} custom-call(bf16[256,256]{1,0:T(8,128)(2,1)S(1)} %get-tuple-element.10.refs_0_, bf16[272,256]{1,0:T(8,128)(2,1)S(1)} %get-tuple-element.12.refs_1_, bf16[256,256]{1,0:T(8,128)(2,1)S(1)} %get-tuple-element.13.refs_2_, bf16[272,256]{1,0:T(8,128)(2,1)S(1)} %get-tuple-element.14.refs_3_, ...), custom_call_target="tpu_custom_call" | custom-call | flops 536870912 | bytes 4194304 | tf_op jit(solution)/shard_map/states/pallas_call | solution.py:123
  40.4 5.7 %copy-done = bf16[64,256,512]{2,1,0:T(8,128)(2,1)} copy-done((bf16[64,256,512]{2,1,0:T(8,128)(2,1)}, bf16[64,256,512]{2,1,0:T(8,128)(2,1)S(1)}, u32[]{:S(2)}) %copy-start) | copy-done | bytes 16777240
  46.1 1.4 %collective-permute-start.20 = (bf16[256,256]{1,0:T(8,128)(2,1)S(1)}, bf16[256,256]{1,0:T(8,128)(2,1)S(1)}, u32[]{:S(2)}, u32[]{:S(2)}) collective-permute-start(bf16[256,256]{1,0:T(8,128)(2,1)S(1)} %collective-permute-done.19.refs_2_), channel_id=1, source_target_pairs={{4,0},{8,4},{12,8},{14,12},{10,14},{6,10},{2,6},{0,2},{5,1},{9,5},... | collective-permute-start | bytes 393224 | tf_op jit(solution)/shard_map/ppermute | solution.py:250
  50.2 5.8 %copy-done.1 = bf16[64,256,512]{2,1,0:T(8,128)(2,1)S(1)} copy-done((bf16[64,256,512]{2,1,0:T(8,128)(2,1)S(1)}, bf16[64,256,512]{2,1,0:T(8,128)(2,1)}, u32[]{:S(2)}) %copy-start.1) | copy-done | bytes 16777240
  58.8 1.4 %states.11.refs_6_ = bf16[64,256,512]{2,1,0:T(8,128)(2,1)S(1)} custom-call(bf16[256,256]{1,0:T(8,128)(2,1)S(1)} %collective-permute-done.2.refs_0_, bf16[272,256]{1,0:T(8,128)(2,1)S(1)} %collective-permute-done.10.refs_1_, bf16[256,256]{1,0:T(8,128)(2,1)S(1)} %collective-permute-done.17.refs_2_, ...), custom_call_target="tpu_custom_call", output_to_operand_aliasing={{}: (6, {})} | custom-call | flops 536870912 | bytes 4194304 | tf_op jit(solution)/shard_map/states/pallas_call | solution.py:123
  60.2 1.5 %collective-permute-start.21 = (bf16[256,256]{1,0:T(8,128)(2,1)S(1)}, bf16[256,256]{1,0:T(8,128)(2,1)S(1)}, u32[]{:S(2)}, u32[]{:S(2)}) collective-permute-start(bf16[256,256]{1,0:T(8,128)(2,1)S(1)} %collective-permute-done.20.refs_2_), channel_id=1, source_target_pairs={{4,0},{8,4},{12,8},{14,12},{10,14},{6,10},{2,6},{0,2},{5,1},{9,5},... | collective-permute-start | bytes 393224 | tf_op jit(solution)/shard_map/ppermute | solution.py:250
  65.8 1.4 %states.13.refs_6_ = bf16[64,256,512]{2,1,0:T(8,128)(2,1)S(1)} custom-call(bf16[256,256]{1,0:T(8,128)(2,1)S(1)} %collective-permute-done.4.refs_0_, bf16[272,256]{1,0:T(8,128)(2,1)S(1)} %collective-permute-done.12.refs_1_, bf16[256,256]{1,0:T(8,128)(2,1)S(1)} %collective-permute-done.19.refs_2_, ...), custom_call_target="tpu_custom_call", output_to_operand_aliasing={{}: (6, {})} | custom-call | flops 536870912 | bytes 4194304 | tf_op jit(solution)/shard_map/states/pallas_call | solution.py:123
  67.2 1.4 %states.14.refs_6_ = bf16[64,256,512]{2,1,0:T(8,128)(2,1)S(1)} custom-call(bf16[256,256]{1,0:T(8,128)(2,1)S(1)} %collective-permute-done.5.refs_0_, bf16[272,256]{1,0:T(8,128)(2,1)S(1)} %collective-permute-done.13.refs_1_, bf16[256,256]{1,0:T(8,128)(2,1)S(1)} %collective-permute-done.20.refs_2_, ...), custom_call_target="tpu_custom_call", output_to_operand_aliasing={{}: (6, {})} | custom-call | flops 536870912 | bytes 4194304 | tf_op jit(solution)/shard_map/states/pallas_call | solution.py:123
  70.2 5.7 %copy-done.2 = bf16[64,256,512]{2,1,0:T(8,128)(2,1)} copy-done((bf16[64,256,512]{2,1,0:T(8,128)(2,1)}, bf16[64,256,512]{2,1,0:T(8,128)(2,1)S(1)}, u32[]{:S(2)}) %copy-start.2) | copy-done | bytes 16777240
  75.9 16.8 %rows.1 = (bf16[4,8,6,64,128]{4,3,2,1,0:T(8,128)(2,1)S(1)}, bf16[4,8,6,64,128]{4,3,2,1,0:T(8,128)(2,1)}, f32[8,1,128]{2,1,0:T(1,128)S(1)}) custom-call(s32[2]{0:T(128)S(1)} %pad_add_fusion.place_ref, s32[384]{0:T(512)S(1)} %reshape.90.col_ref, s32[64]{0:T(128)S(1)} %copy-done.7, bf16[64,256,512]{2,1,0:T(8,128)(2,1)} %copy-done.2, ...), custom_call_target="tpu_custom_call" | custom-call | tf_op jit(solution)/shard_map/rows/pallas_call | solution.py:203
  94.5 3.9 %collective-permute-done.30 = f32[512]{0:T(512)S(1)} collective-permute-done((f32[512]{0:T(512)S(1)}, f32[512]{0:T(512)S(1)}, u32[]{:S(2)}, u32[]{:S(2)}) %collective-permute-start.30) | collective-permute-done | bytes 2080 | tf_op jit(solution)/shard_map/ppermute | solution.py:262
  99.0 5.0 %add_convert_fusion = bf16[4,8,6,64,128]{4,3,2,1,0:T(8,128)(2,1)} fusion(bf16[4,8,6,64,128]{4,3,2,1,0:T(8,128)(2,1)} %collective-permute-done.29, bf16[4,8,6,64,128]{4,3,2,1,0:T(8,128)(2,1)S(1)} %get-tuple-element.15), kind=kLoop, calls=%fused_computation | loop fusion | flops 6291456 | bytes 9437184 | tf_op jit(solution)/shard_map/convert_element_type | solution.py:263
  (86 shorter events, 27.2 us)
Async XLA Ops:
  8.5 6.2 %collective-permute-start.15 = (bf16[256,256]{1,0:T(8,128)(2,1)S(1)}, bf16[256,256]{1,0:T(8,128)(2,1)S(1)}, u32[]{:S(2)}, u32[]{:S(2)}) collective-permute-start(bf16[256,256]{1,0:T(8,128)(2,1)S(1)} %get-tuple-element.13.refs_2_), channel_id=1, source_target_pairs={{4,0},{8,4},{12,8},{14,12},{10,14},{6,10},{2,6},{0,2},{5,1},{9,5},... | collective-permute-start | bytes 393224 | tf_op jit(solution)/shard_map/ppermute | solution.py:250
  8.6 9.1 %collective-permute-start.22 = (bf16[272,256]{1,0:T(8,128)(2,1)S(1)}, bf16[272,256]{1,0:T(8,128)(2,1)S(1)}, u32[]{:S(2)}, u32[]{:S(2)}) collective-permute-start(bf16[272,256]{1,0:T(8,128)(2,1)S(1)} %get-tuple-element.14.refs_3_), channel_id=1, source_target_pairs={{4,0},{8,4},{12,8},{14,12},{10,14},{6,10},{2,6},{0,2},{5,1},{9,5},... | collective-permute-start | bytes 417800 | tf_op jit(solution)/shard_map/ppermute | solution.py:250
  10.6 7.1 %collective-permute-start.8 = (bf16[272,256]{1,0:T(8,128)(2,1)S(1)}, bf16[272,256]{1,0:T(8,128)(2,1)S(1)}, u32[]{:S(2)}, u32[]{:S(2)}) collective-permute-start(bf16[272,256]{1,0:T(8,128)(2,1)S(1)} %get-tuple-element.12.refs_1_), channel_id=1, source_target_pairs={{0,4},{4,8},{8,12},{12,14},{14,10},{10,6},{6,2},{2,0},{1,5},{5,9},... | collective-permute-start | bytes 417800 | tf_op jit(solution)/shard_map/ppermute | solution.py:250
  12.0 9.0 %collective-permute-start.1 = (bf16[256,256]{1,0:T(8,128)(2,1)S(1)}, bf16[256,256]{1,0:T(8,128)(2,1)S(1)}, u32[]{:S(2)}, u32[]{:S(2)}) collective-permute-start(bf16[256,256]{1,0:T(8,128)(2,1)S(1)} %collective-permute-done.refs_0_), channel_id=1, source_target_pairs={{0,4},{4,8},{8,12},{12,14},{14,10},{10,6},{6,2},{2,0},{1,5},{5,9},... | collective-permute-start | bytes 393224 | tf_op jit(solution)/shard_map/ppermute | solution.py:250
  17.7 8.3 %collective-permute-start.23 = (bf16[272,256]{1,0:T(8,128)(2,1)S(1)}, bf16[272,256]{1,0:T(8,128)(2,1)S(1)}, u32[]{:S(2)}, u32[]{:S(2)}) collective-permute-start(bf16[272,256]{1,0:T(8,128)(2,1)S(1)} %collective-permute-done.22.refs_3_), channel_id=1, source_target_pairs={{4,0},{8,4},{12,8},{14,12},{10,14},{6,10},{2,6},{0,2},{5,1},{9,5},... | collective-permute-start | bytes 417800 | tf_op jit(solution)/shard_map/ppermute | solution.py:250
  17.7 6.6 %collective-permute-start.9 = (bf16[272,256]{1,0:T(8,128)(2,1)S(1)}, bf16[272,256]{1,0:T(8,128)(2,1)S(1)}, u32[]{:S(2)}, u32[]{:S(2)}) collective-permute-start(bf16[272,256]{1,0:T(8,128)(2,1)S(1)} %collective-permute-done.8.refs_1_), channel_id=1, source_target_pairs={{0,4},{4,8},{8,12},{12,14},{14,10},{10,6},{6,2},{2,0},{1,5},{5,9},... | collective-permute-start | bytes 417800 | tf_op jit(solution)/shard_map/ppermute | solution.py:250
  20.8 6.4 %collective-permute-start.17 = (bf16[256,256]{1,0:T(8,128)(2,1)S(1)}, bf16[256,256]{1,0:T(8,128)(2,1)S(1)}, u32[]{:S(2)}, u32[]{:S(2)}) collective-permute-start(bf16[256,256]{1,0:T(8,128)(2,1)S(1)} %collective-permute-done.16.refs_2_), channel_id=1, source_target_pairs={{4,0},{8,4},{12,8},{14,12},{10,14},{6,10},{2,6},{0,2},{5,1},{9,5},... | collective-permute-start | bytes 393224 | tf_op jit(solution)/shard_map/ppermute | solution.py:250
  21.1 7.5 %collective-permute-start.2 = (bf16[256,256]{1,0:T(8,128)(2,1)S(1)}, bf16[256,256]{1,0:T(8,128)(2,1)S(1)}, u32[]{:S(2)}, u32[]{:S(2)}) collective-permute-start(bf16[256,256]{1,0:T(8,128)(2,1)S(1)} %collective-permute-done.1.refs_0_), channel_id=1, source_target_pairs={{0,4},{4,8},{8,12},{12,14},{14,10},{10,6},{6,2},{2,0},{1,5},{5,9},... | collective-permute-start | bytes 393224 | tf_op jit(solution)/shard_map/ppermute | solution.py:250
  26.0 6.5 %collective-permute-start.24 = (bf16[272,256]{1,0:T(8,128)(2,1)S(1)}, bf16[272,256]{1,0:T(8,128)(2,1)S(1)}, u32[]{:S(2)}, u32[]{:S(2)}) collective-permute-start(bf16[272,256]{1,0:T(8,128)(2,1)S(1)} %collective-permute-done.23.refs_3_), channel_id=1, source_target_pairs={{4,0},{8,4},{12,8},{14,12},{10,14},{6,10},{2,6},{0,2},{5,1},{9,5},... | collective-permute-start | bytes 417800 | tf_op jit(solution)/shard_map/ppermute | solution.py:250
  27.2 7.4 %collective-permute-start.18 = (bf16[256,256]{1,0:T(8,128)(2,1)S(1)}, bf16[256,256]{1,0:T(8,128)(2,1)S(1)}, u32[]{:S(2)}, u32[]{:S(2)}) collective-permute-start(bf16[256,256]{1,0:T(8,128)(2,1)S(1)} %collective-permute-done.17.refs_2_), channel_id=1, source_target_pairs={{4,0},{8,4},{12,8},{14,12},{10,14},{6,10},{2,6},{0,2},{5,1},{9,5},... | collective-permute-start | bytes 393224 | tf_op jit(solution)/shard_map/ppermute | solution.py:250
  28.6 6.6 %collective-permute-start.3 = (bf16[256,256]{1,0:T(8,128)(2,1)S(1)}, bf16[256,256]{1,0:T(8,128)(2,1)S(1)}, u32[]{:S(2)}, u32[]{:S(2)}) collective-permute-start(bf16[256,256]{1,0:T(8,128)(2,1)S(1)} %collective-permute-done.2.refs_0_), channel_id=1, source_target_pairs={{0,4},{4,8},{8,12},{12,14},{14,10},{10,6},{6,2},{2,0},{1,5},{5,9},... | collective-permute-start | bytes 393224 | tf_op jit(solution)/shard_map/ppermute | solution.py:250
  30.5 6.2 %collective-permute-start.11 = (bf16[272,256]{1,0:T(8,128)(2,1)S(1)}, bf16[272,256]{1,0:T(8,128)(2,1)S(1)}, u32[]{:S(2)}, u32[]{:S(2)}) collective-permute-start(bf16[272,256]{1,0:T(8,128)(2,1)S(1)} %collective-permute-done.10.refs_1_), channel_id=1, source_target_pairs={{0,4},{4,8},{8,12},{12,14},{14,10},{10,6},{6,2},{2,0},{1,5},{5,9},... | collective-permute-start | bytes 417800 | tf_op jit(solution)/shard_map/ppermute | solution.py:250
  34.6 11.5 %collective-permute-start.19 = (bf16[256,256]{1,0:T(8,128)(2,1)S(1)}, bf16[256,256]{1,0:T(8,128)(2,1)S(1)}, u32[]{:S(2)}, u32[]{:S(2)}) collective-permute-start(bf16[256,256]{1,0:T(8,128)(2,1)S(1)} %collective-permute-done.18.refs_2_), channel_id=1, source_target_pairs={{4,0},{8,4},{12,8},{14,12},{10,14},{6,10},{2,6},{0,2},{5,1},{9,5},... | collective-permute-start | bytes 393224 | tf_op jit(solution)/shard_map/ppermute | solution.py:250
  35.2 12.4 %collective-permute-start.4 = (bf16[256,256]{1,0:T(8,128)(2,1)S(1)}, bf16[256,256]{1,0:T(8,128)(2,1)S(1)}, u32[]{:S(2)}, u32[]{:S(2)}) collective-permute-start(bf16[256,256]{1,0:T(8,128)(2,1)S(1)} %collective-permute-done.3.refs_0_), channel_id=1, source_target_pairs={{0,4},{4,8},{8,12},{12,14},{14,10},{10,6},{6,2},{2,0},{1,5},{5,9},... | collective-permute-start | bytes 393224 | tf_op jit(solution)/shard_map/ppermute | solution.py:250
  36.7 11.5 %collective-permute-start.12 = (bf16[272,256]{1,0:T(8,128)(2,1)S(1)}, bf16[272,256]{1,0:T(8,128)(2,1)S(1)}, u32[]{:S(2)}, u32[]{:S(2)}) collective-permute-start(bf16[272,256]{1,0:T(8,128)(2,1)S(1)} %collective-permute-done.11.refs_1_), channel_id=1, source_target_pairs={{0,4},{4,8},{8,12},{12,14},{14,10},{10,6},{6,2},{2,0},{1,5},{5,9},... | collective-permute-start | bytes 417800 | tf_op jit(solution)/shard_map/ppermute | solution.py:250
  38.0 11.5 %collective-permute-start.26 = (bf16[272,256]{1,0:T(8,128)(2,1)S(1)}, bf16[272,256]{1,0:T(8,128)(2,1)S(1)}, u32[]{:S(2)}, u32[]{:S(2)}) collective-permute-start(bf16[272,256]{1,0:T(8,128)(2,1)S(1)} %collective-permute-done.25.refs_3_), channel_id=1, source_target_pairs={{4,0},{8,4},{12,8},{14,12},{10,14},{6,10},{2,6},{0,2},{5,1},{9,5},... | collective-permute-start | bytes 417800 | tf_op jit(solution)/shard_map/ppermute | solution.py:250
  46.1 14.1 %collective-permute-start.20 = (bf16[256,256]{1,0:T(8,128)(2,1)S(1)}, bf16[256,256]{1,0:T(8,128)(2,1)S(1)}, u32[]{:S(2)}, u32[]{:S(2)}) collective-permute-start(bf16[256,256]{1,0:T(8,128)(2,1)S(1)} %collective-permute-done.19.refs_2_), channel_id=1, source_target_pairs={{4,0},{8,4},{12,8},{14,12},{10,14},{6,10},{2,6},{0,2},{5,1},{9,5},... | collective-permute-start | bytes 393224 | tf_op jit(solution)/shard_map/ppermute | solution.py:250
  47.6 14.1 %collective-permute-start.5 = (bf16[256,256]{1,0:T(8,128)(2,1)S(1)}, bf16[256,256]{1,0:T(8,128)(2,1)S(1)}, u32[]{:S(2)}, u32[]{:S(2)}) collective-permute-start(bf16[256,256]{1,0:T(8,128)(2,1)S(1)} %collective-permute-done.4.refs_0_), channel_id=1, source_target_pairs={{0,4},{4,8},{8,12},{12,14},{14,10},{10,6},{6,2},{2,0},{1,5},{5,9},... | collective-permute-start | bytes 393224 | tf_op jit(solution)/shard_map/ppermute | solution.py:250
  48.2 14.1 %collective-permute-start.13 = (bf16[272,256]{1,0:T(8,128)(2,1)S(1)}, bf16[272,256]{1,0:T(8,128)(2,1)S(1)}, u32[]{:S(2)}, u32[]{:S(2)}) collective-permute-start(bf16[272,256]{1,0:T(8,128)(2,1)S(1)} %collective-permute-done.12.refs_1_), channel_id=1, source_target_pairs={{0,4},{4,8},{8,12},{12,14},{14,10},{10,6},{6,2},{2,0},{1,5},{5,9},... | collective-permute-start | bytes 417800 | tf_op jit(solution)/shard_map/ppermute | solution.py:250
  49.5 14.1 %collective-permute-start.27 = (bf16[272,256]{1,0:T(8,128)(2,1)S(1)}, bf16[272,256]{1,0:T(8,128)(2,1)S(1)}, u32[]{:S(2)}, u32[]{:S(2)}) collective-permute-start(bf16[272,256]{1,0:T(8,128)(2,1)S(1)} %collective-permute-done.26.refs_3_), channel_id=1, source_target_pairs={{4,0},{8,4},{12,8},{14,12},{10,14},{6,10},{2,6},{0,2},{5,1},{9,5},... | collective-permute-start | bytes 417800 | tf_op jit(solution)/shard_map/ppermute | solution.py:250
  60.2 8.4 %collective-permute-start.21 = (bf16[256,256]{1,0:T(8,128)(2,1)S(1)}, bf16[256,256]{1,0:T(8,128)(2,1)S(1)}, u32[]{:S(2)}, u32[]{:S(2)}) collective-permute-start(bf16[256,256]{1,0:T(8,128)(2,1)S(1)} %collective-permute-done.20.refs_2_), channel_id=1, source_target_pairs={{4,0},{8,4},{12,8},{14,12},{10,14},{6,10},{2,6},{0,2},{5,1},{9,5},... | collective-permute-start | bytes 393224 | tf_op jit(solution)/shard_map/ppermute | solution.py:250
  61.7 6.9 %collective-permute-start.6 = (bf16[256,256]{1,0:T(8,128)(2,1)S(1)}, bf16[256,256]{1,0:T(8,128)(2,1)S(1)}, u32[]{:S(2)}, u32[]{:S(2)}) collective-permute-start(bf16[256,256]{1,0:T(8,128)(2,1)S(1)} %collective-permute-done.5.refs_0_), channel_id=1, source_target_pairs={{0,4},{4,8},{8,12},{12,14},{14,10},{10,6},{6,2},{2,0},{1,5},{5,9},... | collective-permute-start | bytes 393224 | tf_op jit(solution)/shard_map/ppermute | solution.py:250
  62.3 6.4 %collective-permute-start.14 = (bf16[272,256]{1,0:T(8,128)(2,1)S(1)}, bf16[272,256]{1,0:T(8,128)(2,1)S(1)}, u32[]{:S(2)}, u32[]{:S(2)}) collective-permute-start(bf16[272,256]{1,0:T(8,128)(2,1)S(1)} %collective-permute-done.13.refs_1_), channel_id=1, source_target_pairs={{0,4},{4,8},{8,12},{12,14},{14,10},{10,6},{6,2},{2,0},{1,5},{5,9},... | collective-permute-start | bytes 417800 | tf_op jit(solution)/shard_map/ppermute | solution.py:250
  92.7 6.2 %collective-permute-start.29 = (bf16[4,8,6,64,128]{4,3,2,1,0:T(8,128)(2,1)}, bf16[4,8,6,64,128]{4,3,2,1,0:T(8,128)(2,1)}, u32[]{:S(2)}, u32[]{:S(2)}) collective-permute-start(bf16[4,8,6,64,128]{4,3,2,1,0:T(8,128)(2,1)} %get-tuple-element.16), channel_id=1, source_target_pairs={{0,1},{1,0},{2,3},{3,2},{4,5},{5,4},{6,7},{7,6},{8,9},{9,8},{10,11... | collective-permute-start | bytes 9437192 | tf_op jit(solution)/shard_map/ppermute | solution.py:261
  (17 other events, 95.6 us)

commit v3 on v2

v3 whole, which is shorter than its diff:
```python
import functools
import jax
import jax.numpy as jnp
from jax import lax
from jax.experimental import pallas as pl
from jax.experimental.pallas import tpu as pltpu
from jax.sharding import PartitionSpec as P

STREAMS = 4
CARRY_ROWS = 16
GROUPS = 2


def lag_tables(bins, basis_count, overall, lanes):
    log_decay = -(8.0 ** jnp.arange(basis_count, dtype=jnp.float32)) / (2.0 * overall)
    t = jnp.arange(bins, dtype=jnp.float32)
    lag = t[:, None] - 1.0 - t[None, :]
    weights = jnp.where(
        lag[None] >= 0.0,
        (1.0 - jnp.exp(log_decay))[:, None, None]
        * jnp.exp(jnp.maximum(lag, 0.0)[None] * log_decay[:, None, None]),
        jnp.float32(0.0),
    )
    power = jnp.exp(t[None, :, None] * log_decay[:, None, None])
    return weights.astype(jnp.bfloat16), jnp.broadcast_to(power, (basis_count, bins, lanes))


def impact_of(counts_ref, mark_ref, lanes):
    counts = counts_ref[:, lanes].astype(jnp.float32)
    return (counts * mark_ref[:, lanes].astype(jnp.float32)).astype(jnp.bfloat16)


def first_kernel(basis, overall, counts_ref, mark_ref, up_ref, down_ref, ends_ref):
    bins, types = counts_ref.shape
    lanes = types // STREAMS
    back = (bins - 1 - lax.broadcasted_iota(jnp.int32, (bins, 1), 0)).astype(jnp.float32)
    gains = []
    for b in range(basis):
        rate = (8.0**b) / (2.0 * overall)
        gains.append((1.0 - jnp.exp(jnp.full((bins, 1), -rate, jnp.float32))) * jnp.exp(-rate * back))
    for j in range(STREAMS):
        impact = impact_of(counts_ref, mark_ref, slice(j * lanes, (j + 1) * lanes))
        if j == 0:
            up_ref[...] = impact
        if j == 2:
            down_ref[...] = impact
        impact = impact.astype(jnp.float32)
        for b in range(basis):
            ends_ref[b : b + 1, j * lanes : (j + 1) * lanes] = jnp.sum(
                impact * gains[b], axis=0, keepdims=True
            )


def second_kernel(basis, counts_ref, mark_ref, enter_ref, up_ref, down_ref):
    bins, types = counts_ref.shape
    lanes = types // STREAMS
    for j, out_ref in ((1, up_ref), (3, down_ref)):
        out_ref[:bins] = impact_of(counts_ref, mark_ref, slice(j * lanes, (j + 1) * lanes))
        carry = jnp.concatenate(
            [enter_ref[:, (j - 1) * lanes : j * lanes], enter_ref[:, j * lanes : (j + 1) * lanes]],
            axis=0,
        )
        pad = jnp.zeros((CARRY_ROWS - 2 * basis, lanes), jnp.float32)
        out_ref[bins:] = jnp.concatenate([carry, pad], axis=0).astype(jnp.bfloat16)


def first(counts, mark, basis, overall):
    bins, types = counts.shape
    chunk = jax.ShapeDtypeStruct((bins, types // STREAMS), jnp.bfloat16)
    return pl.pallas_call(
        functools.partial(first_kernel, basis, overall),
        out_shape=[chunk, chunk, jax.ShapeDtypeStruct((basis, types), jnp.float32)],
        compiler_params=pltpu.CompilerParams(vmem_limit_bytes=32 << 20),
        name="first_chunks",
    )(counts, mark)


def second(counts, mark, enter, basis):
    bins, types = counts.shape
    chunk = jax.ShapeDtypeStruct((bins + CARRY_ROWS, types // STREAMS), jnp.bfloat16)
    return pl.pallas_call(
        functools.partial(second_kernel, basis),
        out_shape=[chunk, chunk],
        compiler_params=pltpu.CompilerParams(vmem_limit_bytes=32 << 20),
        name="second_chunks",
    )(counts, mark, enter)


def ring_place(index, n):
    return jnp.where(index % 2 == 0, index // 2, n - 1 - index // 2)


def step_kernel(shape, step, place_ref, col_ref, fill_ref, *refs):
    basis, brows, slots, tile, n = shape
    chunks = refs[:STREAMS]
    lag_ref, power_ref, excite_ref = refs[STREAMS : STREAMS + 3]
    states_ref, total_ref, held = refs[-3:]
    bins, lanes = chunks[0].shape
    per = lanes // tile
    width = STREAMS * per
    own = place_ref[0]
    if step == 0:
        counts_ref, base_ref = refs[STREAMS + 3 : STREAMS + 5]
        for row in range(brows):
            at = slice(row * tile, (row + 1) * tile)
            total_ref[row] = (base_ref[:, at] - counts_ref[:, at].astype(jnp.float32)).T
    for j in range(STREAMS):
        impact = chunks[j][:bins] if j % 2 else chunks[j][...]
        carry = chunks[j | 1][bins:].astype(jnp.float32)
        for b in range(basis):
            state = jnp.dot(lag_ref[b], impact, preferred_element_type=jnp.float32)
            row = (j % 2) * basis + b
            for q in range(per):
                at = slice(q * tile, (q + 1) * tile)
                held[j * per + q, :, b * tile : (b + 1) * tile] = (
                    state[:, at] + power_ref[b] * carry[row : row + 1, at]
                ).astype(jnp.bfloat16)

    @pl.loop(0, brows * slots)
    def _(entry):
        row = entry // slots
        slot = entry - row * slots
        column = col_ref[own * (brows * slots) + entry]
        source = column // width
        block = column - source * width
        ahead = ring_place(source, n) - ring_place(own, n)
        ahead = jnp.where(block < width // 2, -ahead, ahead)
        ahead = jnp.where(ahead < 0, ahead + n, ahead)

        @pl.when((ahead == step) & (slot < fill_ref[own * brows + row]))
        def _():
            state = held[block]
            states_ref[entry] = state
            weight = jnp.concatenate([excite_ref[b, row, slot] for b in range(basis)], axis=1)
            total_ref[row] += lax.dot_general(
                weight, state, (((1,), (1,)), ((), ())), preferred_element_type=jnp.float32
            )


SMEM = pl.BlockSpec(memory_space=pltpu.SMEM)
VMEM = pl.BlockSpec(memory_space=pltpu.VMEM)


def take_step(step, scalars, chunks, lag, power, excite, more, n):
    basis, brows, slots, tile, _ = excite.shape
    bins = lag.shape[1]
    lanes = chunks[0].shape[1]
    before = 3 + STREAMS + 3
    return pl.pallas_call(
        functools.partial(step_kernel, (basis, brows, slots, tile, n), step),
        in_specs=[SMEM] * 3 + [VMEM] * (STREAMS + 5),
        out_specs=[VMEM, VMEM],
        out_shape=[
            jax.ShapeDtypeStruct((brows * slots, bins, basis * tile), jnp.bfloat16),
            jax.ShapeDtypeStruct((brows, tile, bins), jnp.float32),
        ],
        scratch_shapes=[pltpu.VMEM((STREAMS * lanes // tile, bins, basis * tile), jnp.bfloat16)],
        input_output_aliases={} if step == 0 else {before: 0, before + 1: 1},
        compiler_params=pltpu.CompilerParams(vmem_limit_bytes=16 << 20),
        cost_estimate=pl.CostEstimate(
            flops=4 * basis * bins * bins * lanes * STREAMS,
            bytes_accessed=2 * 1024 * 1024,
            transcendentals=0,
        ),
        name="ring_step",
    )(*scalars, *chunks, lag, power, excite, *more)


def products(turned_ref, states_ref, fills, rows, slots, basis, tile, put):
    for r, row in enumerate(rows):
        for s in range(slots):
            grad = jnp.dot(
                turned_ref[row], states_ref[row * slots + s], preferred_element_type=jnp.float32
            )
            grad = jnp.where(s < fills[r], grad, jnp.zeros_like(grad))
            for b in range(basis):
                put(b, r, row, s, grad[:, b * tile : (b + 1) * tile])


def sent_kernel(shape, group, place_ref, fill_ref, *refs):
    basis, brows, slots, tile, overall = shape
    own, half = place_ref[0], place_ref[1]
    part = tile // 2
    if group == 0:
        total_ref, states_ref, out_ref, other_ref, mine_ref, rate_own_ref, rate_sent_ref = refs
        rates = []
        for row in range(brows):
            weighted = (2.0 / overall) * total_ref[row]
            ones = jnp.ones((8, weighted.shape[1]), jnp.float32)
            rates.append(
                lax.dot_general(
                    ones,
                    weighted,
                    (((1,), (1,)), ((), ())),
                    precision=lax.Precision.HIGHEST,
                    preferred_element_type=jnp.float32,
                )[:1]
            )
            weighted = weighted.astype(jnp.bfloat16)
            upper, lower = weighted[:part], weighted[part:]
            mine_ref[row] = jnp.where(half == 0, upper, lower)
            other_ref[row] = jnp.where(half == 0, lower, upper)
        first_half = jnp.concatenate(rates[: brows // 2], axis=0)
        second_half = jnp.concatenate(rates[brows // 2 :], axis=0)
        rate_own_ref[...] = jnp.where(half == 0, first_half, second_half)
        rate_sent_ref[...] = jnp.where(half == 0, second_half, first_half)
    else:
        other_ref, states_ref, out_ref = refs
    count = brows // GROUPS
    rows = range(group * count, (group + 1) * count)
    fills = [fill_ref[own * brows + row] for row in rows]

    def put(b, r, row, s, grad):
        out_ref[b, r, s] = grad.astype(jnp.bfloat16)

    products(other_ref, states_ref, fills, rows, slots, basis, tile, put)


def sent(group, place, fill, given, states, dims, overall):
    basis, brows, slots, tile = dims
    bins = states.shape[1]
    part = tile // 2
    out_shape = [jax.ShapeDtypeStruct((basis, brows // GROUPS, slots, part, tile), jnp.bfloat16)]
    if group == 0:
        out_shape += [jax.ShapeDtypeStruct((brows, part, bins), jnp.bfloat16)] * 2
        out_shape += [jax.ShapeDtypeStruct((brows // 2, tile), jnp.float32)] * 2
    return pl.pallas_call(
        functools.partial(sent_kernel, (basis, brows, slots, tile, overall), group),
        in_specs=[SMEM, SMEM, VMEM, VMEM],
        out_specs=[VMEM] * len(out_shape),
        out_shape=out_shape,
        compiler_params=pltpu.CompilerParams(vmem_limit_bytes=16 << 20),
        name="sent_half",
    )(place, fill, given, states)


def kept_kernel(shape, group, place_ref, fill_ref, mine_ref, states_ref, got_ref, *refs):
    basis, brows, slots, tile = shape
    out_ref, held, sems = refs[-3:]
    own = place_ref[0]
    count = brows // GROUPS
    copies = []
    for r in range(count):
        row = group * count + r

        def put(b, _, row, s, grad, r=r):
            held[b, r, s] = (grad + got_ref[b, r, s].astype(jnp.float32)).astype(jnp.bfloat16)

        products(mine_ref, states_ref, [fill_ref[own * brows + row]], [row], slots, basis, tile, put)
        for b in range(basis):
            copy = pltpu.make_async_copy(held.at[b, r], out_ref.at[b, row], sems.at[b, r])
            copy.start()
            copies.append(copy)
    for copy in copies:
        copy.wait()


def kept(group, place, fill, mine, states, got, out, dims):
    basis, brows, slots, tile = dims
    part = tile // 2
    anywhere = pl.BlockSpec(memory_space=pl.ANY)
    given = [] if out is None else [out]
    return pl.pallas_call(
        functools.partial(kept_kernel, dims, group),
        in_specs=[SMEM, SMEM, VMEM, VMEM, VMEM] + [anywhere] * len(given),
        out_specs=anywhere,
        out_shape=jax.ShapeDtypeStruct((basis, brows, slots, part, tile), jnp.bfloat16),
        scratch_shapes=[
            pltpu.VMEM((basis, brows // GROUPS, slots, part, tile), jnp.bfloat16),
            pltpu.SemaphoreType.DMA((basis, brows // GROUPS)),
        ],
        input_output_aliases={5: 0} if given else {},
        compiler_params=pltpu.CompilerParams(vmem_limit_bytes=16 << 20),
        name="kept_half",
    )(place, fill, mine, states, got, *given)


def shards(counts, mark_value, base_rate, excite, block_col, row_fill):
    basis, brows, slots, tile, _ = excite.shape
    bins = counts.shape[0]
    overall = bins * lax.axis_size("tm")
    n = lax.axis_size("types")
    half = lax.axis_index("tm")
    place = jnp.stack([lax.axis_index("types"), half]).astype(jnp.int32)
    order = list(range(0, n, 2)) + list(range(1, n, 2))[::-1]
    up = [(order[i], order[(i + 1) % n]) for i in range(n)]
    down = [(b, a) for a, b in up]
    up_one, down_one, ends = first(counts, mark_value, basis, overall)
    enter = lax.ppermute(ends, "tm", [(0, 1)])
    up_two, down_two = second(counts, mark_value, enter, basis)
    lag, power = lag_tables(bins, basis, overall, tile)
    chunks = [up_one, up_two, down_one, down_two]
    scalars = (place, block_col.reshape(-1), row_fill)
    more = (counts, base_rate.reshape(1, -1))
    for step in range(n):
        ahead = None
        if step < n - 1:
            ahead = [
                lax.ppermute(chunks[j], "types", up if j < STREAMS // 2 else down)
                for j in (0, 2, 1, 3)
            ]
            ahead = [ahead[0], ahead[2], ahead[1], ahead[3]]
        more = take_step(step, scalars, chunks, lag, power, excite, more, n)
        chunks = ahead
    states, total = more
    dims = (basis, brows, slots, tile)
    swap = [(0, 1), (1, 0)]
    out, other, mine, rate_own, rate_sent = sent(0, place, row_fill, total, states, dims, overall)
    got = [lax.ppermute(out, "tm", swap)]
    rate_got = lax.ppermute(rate_sent, "tm", swap)
    for group in range(1, GROUPS):
        (out,) = sent(group, place, row_fill, other, states, dims, overall)
        got.append(lax.ppermute(out, "tm", swap))
    grad = None
    for group in range(GROUPS):
        grad = kept(group, place, row_fill, mine, states, got[group], grad, dims)
    return grad, (rate_own + rate_got).reshape(-1)


def solution(mesh):
    return jax.shard_map(
        shards,
        mesh=mesh,
        in_specs=(
            P(("parts", "tm"), "types"),
            P(("parts", "tm"), "types"),
            P("types"),
            P(None, "types", None, None, None),
            P(),
            P(),
        ),
        out_specs=(P("parts", "types", None, "tm", None), P(("parts", "types", "tm"))),
        check_vma=False,
    )
```

time: 104 us -> 99.4 us (0.956)
  Pallas kernels: 28.9 us -> 42.6 us
  local copies, waits for them, and re-layouts: 21.2 us -> 8.71 us
  other arithmetic: 6.95 us -> 1.25 us
  waiting for transfers between devices: 13.3 us -> 11.8 us
  starting transfers between devices: 32.8 us -> 34.1 us
    pallas_call x9 -> x12, Pallas kernels: 28.1 us -> 41.8 us  [the longest x8 32.2 us: take_step(): pl.pallas_call(functools.partial(step_kernel, (basis, brows, slots, tile,...]
    unnamed x21 -> x13, local copies, waits for them, and re-layouts: 20.3 us -> 8.39 us
    convert_element_type x1 -> x0, other arithmetic: 5.05 us -> none  [shards(): (mine.astype(jnp.float32) + got.astype(jnp.float32)).astype(jnp.bfloat16)]
    ppermute x28, starting transfers between devices: 29.9 us -> 31 us  [shards(): lax.ppermute(chunks[j], 'types', up if j < STREAMS // 2 else down)]
    ppermute x2 -> x3, waiting for transfers between devices: 3.87 us -> 3.25 us  [the longest x1 3.25 us: shards(): rate_got = lax.ppermute(rate_sent, 'tm', swap)]
  transfers between devices with their start and end apart: 31 -> 32, of which waited for: 8 -> 8; matrix products, arithmetic and copies ran while one was open for 3% -> 2% of each run, Pallas kernels for 10% -> 33%
where the time goes in v3:
time: 99.4 us; the launch traced here: 99.5 us
  Pallas kernels  42.6 us (43%)
  starting transfers between devices  34.1 us (34%)
  waiting for transfers between devices  11.8 us (12%)
  local copies, waits for them, and re-layouts  8.71 us (9%)
  other arithmetic  1.25 us (1%)
  between operations  1.07 us (1%)
    pallas_call x8, Pallas kernels, take_step(): pl.pallas_call(functools.partial(step_kernel, (basis, brows, slots, tile,...  32.2 us
    ppermute x28, starting transfers between devices, shards(): lax.ppermute(chunks[j], 'types', up if j < STREAMS // 2 else down)  31 us
    ppermute x28, waiting for transfers between devices, shards(): lax.ppermute(chunks[j], 'types', up if j < STREAMS // 2 else down)  8.57 us
    unnamed x13, local copies, waits for them, and re-layouts  8.39 us
    pallas_call x2, Pallas kernels, kept(): pl.pallas_call(functools.partial(kept_kernel, dims, group), in_specs=[SME...  5.27 us
    pallas_call x2, Pallas kernels, sent(): pl.pallas_call(functools.partial(sent_kernel, (basis, brows, slots, tile,...  4.34 us
    ppermute x1, waiting for transfers between devices, shards(): rate_got = lax.ppermute(rate_sent, 'tm', swap)  3.25 us
    ppermute x1, starting transfers between devices, shards(): enter = lax.ppermute(ends, 'tm', [(0, 1)])  2.35 us
  transfers between devices with their start and end apart: 32, of which 8 were waited for; matrix products, arithmetic and copies ran while one was open for 2% of the time, Pallas kernels for 33%

profile of v3, /device:TPU:0, one launch (start us, length us, event | category | flops | bytes accessed | tf_op | source)
XLA Modules:
  0.0 99.5 jit_solution(5313571564416600282)
XLA Ops:
  3.7 2.4 %collective-permute-start.7 = (f32[4,1024]{1,0:T(4,128)S(1)}, f32[4,1024]{1,0:T(4,128)S(1)}, u32[]{:S(2)}, u32[]{:S(2)}) collective-permute-start(f32[4,1024]{1,0:T(4,128)S(1)} %get-tuple-element.29), channel_id=1, source_target_pairs={{0,1},{2,3},{4,5},{6,7},{8,9},{10,11},{12,13},{14,15},{16,17},{18,... | collective-permute-start | bytes 49160 | tf_op jit(solution)/shard_map/ppermute | solution.py:289
  6.0 2.5 %collective-permute-start = (bf16[256,256]{1,0:T(8,128)(2,1)S(1)}, bf16[256,256]{1,0:T(8,128)(2,1)S(1)}, u32[]{:S(2)}, u32[]{:S(2)}) collective-permute-start(bf16[256,256]{1,0:T(8,128)(2,1)S(1)} %get-tuple-element.28.refs_0_), channel_id=1, source_target_pairs={{0,4},{4,8},{8,12},{12,14},{14,10},{10,6},{6,2},{2,0},{1,5},{5,9},... | collective-permute-start | bytes 393224 | tf_op jit(solution)/shard_map/ppermute | solution.py:299
  8.7 2.0 %collective-permute-start.22 = (bf16[272,256]{1,0:T(8,128)(2,1)S(1)}, bf16[272,256]{1,0:T(8,128)(2,1)S(1)}, u32[]{:S(2)}, u32[]{:S(2)}) collective-permute-start(bf16[272,256]{1,0:T(8,128)(2,1)S(1)} %get-tuple-element.32.refs_3_), channel_id=1, source_target_pairs={{4,0},{8,4},{12,8},{14,12},{10,14},{6,10},{2,6},{0,2},{5,1},{9,5},... | collective-permute-start | bytes 417800 | tf_op jit(solution)/shard_map/ppermute | solution.py:299
  12.0 2.5 %collective-permute-start.1 = (bf16[256,256]{1,0:T(8,128)(2,1)S(1)}, bf16[256,256]{1,0:T(8,128)(2,1)S(1)}, u32[]{:S(2)}, u32[]{:S(2)}) collective-permute-start(bf16[256,256]{1,0:T(8,128)(2,1)S(1)} %collective-permute-done.refs_0_), channel_id=1, source_target_pairs={{0,4},{4,8},{8,12},{12,14},{14,10},{10,6},{6,2},{2,0},{1,5},{5,9},... | collective-permute-start | bytes 393224 | tf_op jit(solution)/shard_map/ppermute | solution.py:299
  14.7 3.0 %collective-permute-done.22.refs_3_ = bf16[272,256]{1,0:T(8,128)(2,1)S(1)} collective-permute-done((bf16[272,256]{1,0:T(8,128)(2,1)S(1)}, bf16[272,256]{1,0:T(8,128)(2,1)S(1)}, u32[]{:S(2)}, u32[]{:S(2)}) %collective-permute-start.22) | collective-permute-done | bytes 139296 | tf_op jit(solution)/shard_map/ppermute | solution.py:299
  17.7 2.0 %collective-permute-start.9 = (bf16[272,256]{1,0:T(8,128)(2,1)S(1)}, bf16[272,256]{1,0:T(8,128)(2,1)S(1)}, u32[]{:S(2)}, u32[]{:S(2)}) collective-permute-start(bf16[272,256]{1,0:T(8,128)(2,1)S(1)} %collective-permute-done.8.refs_1_), channel_id=1, source_target_pairs={{0,4},{4,8},{8,12},{12,14},{14,10},{10,6},{6,2},{2,0},{1,5},{5,9},... | collective-permute-start | bytes 417800 | tf_op jit(solution)/shard_map/ppermute | solution.py:299
  33.7 2.8 %copy-done = bf16[4,8,6,128,128]{4,3,2,1,0:T(8,128)(2,1)S(1)} copy-done((bf16[4,8,6,128,128]{4,3,2,1,0:T(8,128)(2,1)S(1)}, bf16[4,8,6,128,128]{4,3,2,1,0:T(8,128)(2,1)}, u32[]{:S(2)}) %copy-start) | copy-done | bytes 6291480
  39.0 4.2 %ring_step.8 = (bf16[48,256,512]{2,1,0:T(8,128)(2,1)S(1)}, f32[8,128,256]{2,1,0:T(8,128)S(1)}) custom-call(s32[2]{0:T(128)S(1)} %pad_add_fusion.place_ref, s32[384]{0:T(512)S(1)} %reshape.90.col_ref, s32[64]{0:T(128)S(1)} %copy-done.4, bf16[256,256]{1,0:T(8,128)(2,1)S(1)} %get-tuple-element.28.refs_0_, bf16[272,256]{1,0:T(8,128)(2,1)S(1)} %get-tuple-element.30.refs_1_, ...), custom_call_target="tpu_custom_call" | custom-call | flops 1073741824 | bytes 2097152 | tf_op jit(solution)/shard_map/ring_step/pallas_call | solution.py:149
  43.3 1.8 %collective-permute-start.19 = (bf16[256,256]{1,0:T(8,128)(2,1)S(1)}, bf16[256,256]{1,0:T(8,128)(2,1)S(1)}, u32[]{:S(2)}, u32[]{:S(2)}) collective-permute-start(bf16[256,256]{1,0:T(8,128)(2,1)S(1)} %collective-permute-done.18.refs_2_), channel_id=1, source_target_pairs={{4,0},{8,4},{12,8},{14,12},{10,14},{6,10},{2,6},{0,2},{5,1},{9,5},... | collective-permute-start | bytes 393224 | tf_op jit(solution)/shard_map/ppermute | solution.py:299
  47.4 4.2 %ring_step.9 = (bf16[48,256,512]{2,1,0:T(8,128)(2,1)S(1)}, f32[8,128,256]{2,1,0:T(8,128)S(1)}) custom-call(s32[2]{0:T(128)S(1)} %pad_add_fusion.place_ref, s32[384]{0:T(512)S(1)} %reshape.90.col_ref, s32[64]{0:T(128)S(1)} %copy-done.4, bf16[256,256]{1,0:T(8,128)(2,1)S(1)} %collective-permute-done.refs_0_, ...), custom_call_target="tpu_custom_call", output_to_operand_aliasing={{0}: (10, {}), {1}: (11, {})} | custom-call | flops 1073741824 | bytes 2097152 | tf_op jit(solution)/shard_map/ring_step/pallas_call | solution.py:149
  51.6 4.2 %ring_step.10 = (bf16[48,256,512]{2,1,0:T(8,128)(2,1)S(1)}, f32[8,128,256]{2,1,0:T(8,128)S(1)}) custom-call(s32[2]{0:T(128)S(1)} %pad_add_fusion.place_ref, s32[384]{0:T(512)S(1)} %reshape.90.col_ref, s32[64]{0:T(128)S(1)} %copy-done.4, bf16[256,256]{1,0:T(8,128)(2,1)S(1)} %collective-permute-done.1.refs_0_, ...), custom_call_target="tpu_custom_call", output_to_operand_aliasing={{0}: (10, {}), {1}: (11, {})} | custom-call | flops 1073741824 | bytes 2097152 | tf_op jit(solution)/shard_map/ring_step/pallas_call | solution.py:149
  55.8 2.7 %collective-permute-start.20 = (bf16[256,256]{1,0:T(8,128)(2,1)S(1)}, bf16[256,256]{1,0:T(8,128)(2,1)S(1)}, u32[]{:S(2)}, u32[]{:S(2)}) collective-permute-start(bf16[256,256]{1,0:T(8,128)(2,1)S(1)} %collective-permute-done.19.refs_2_), channel_id=1, source_target_pairs={{4,0},{8,4},{12,8},{14,12},{10,14},{6,10},{2,6},{0,2},{5,1},{9,5},... | collective-permute-start | bytes 393224 | tf_op jit(solution)/shard_map/ppermute | solution.py:299
  58.7 1.9 %collective-permute-start.27 = (bf16[272,256]{1,0:T(8,128)(2,1)S(1)}, bf16[272,256]{1,0:T(8,128)(2,1)S(1)}, u32[]{:S(2)}, u32[]{:S(2)}) collective-permute-start(bf16[272,256]{1,0:T(8,128)(2,1)S(1)} %collective-permute-done.26.refs_3_), channel_id=1, source_target_pairs={{4,0},{8,4},{12,8},{14,12},{10,14},{6,10},{2,6},{0,2},{5,1},{9,5},... | collective-permute-start | bytes 417800 | tf_op jit(solution)/shard_map/ppermute | solution.py:299
  60.6 4.0 %ring_step.11 = (bf16[48,256,512]{2,1,0:T(8,128)(2,1)S(1)}, f32[8,128,256]{2,1,0:T(8,128)S(1)}) custom-call(s32[2]{0:T(128)S(1)} %pad_add_fusion.place_ref, s32[384]{0:T(512)S(1)} %reshape.90.col_ref, s32[64]{0:T(128)S(1)} %copy-done.4, bf16[256,256]{1,0:T(8,128)(2,1)S(1)} %collective-permute-done.2.refs_0_, ...), custom_call_target="tpu_custom_call", output_to_operand_aliasing={{0}: (10, {}), {1}: (11, {})} | custom-call | flops 1073741824 | bytes 2097152 | tf_op jit(solution)/shard_map/ring_step/pallas_call | solution.py:149
  64.5 3.5 %ring_step.12 = (bf16[48,256,512]{2,1,0:T(8,128)(2,1)S(1)}, f32[8,128,256]{2,1,0:T(8,128)S(1)}) custom-call(s32[2]{0:T(128)S(1)} %pad_add_fusion.place_ref, s32[384]{0:T(512)S(1)} %reshape.90.col_ref, s32[64]{0:T(128)S(1)} %copy-done.4, bf16[256,256]{1,0:T(8,128)(2,1)S(1)} %collective-permute-done.3.refs_0_, ...), custom_call_target="tpu_custom_call", output_to_operand_aliasing={{0}: (10, {}), {1}: (11, {})} | custom-call | flops 1073741824 | bytes 2097152 | tf_op jit(solution)/shard_map/ring_step/pallas_call | solution.py:149
  68.1 2.7 %collective-permute-start.21 = (bf16[256,256]{1,0:T(8,128)(2,1)S(1)}, bf16[256,256]{1,0:T(8,128)(2,1)S(1)}, u32[]{:S(2)}, u32[]{:S(2)}) collective-permute-start(bf16[256,256]{1,0:T(8,128)(2,1)S(1)} %collective-permute-done.20.refs_2_), channel_id=1, source_target_pairs={{4,0},{8,4},{12,8},{14,12},{10,14},{6,10},{2,6},{0,2},{5,1},{9,5},... | collective-permute-start | bytes 393224 | tf_op jit(solution)/shard_map/ppermute | solution.py:299
  70.9 2.1 %collective-permute-start.28 = (bf16[272,256]{1,0:T(8,128)(2,1)S(1)}, bf16[272,256]{1,0:T(8,128)(2,1)S(1)}, u32[]{:S(2)}, u32[]{:S(2)}) collective-permute-start(bf16[272,256]{1,0:T(8,128)(2,1)S(1)} %collective-permute-done.27.refs_3_), channel_id=1, source_target_pairs={{4,0},{8,4},{12,8},{14,12},{10,14},{6,10},{2,6},{0,2},{5,1},{9,5},... | collective-permute-start | bytes 417800 | tf_op jit(solution)/shard_map/ppermute | solution.py:299
  73.0 4.0 %ring_step.13 = (bf16[48,256,512]{2,1,0:T(8,128)(2,1)S(1)}, f32[8,128,256]{2,1,0:T(8,128)S(1)}) custom-call(s32[2]{0:T(128)S(1)} %pad_add_fusion.place_ref, s32[384]{0:T(512)S(1)} %reshape.90.col_ref, s32[64]{0:T(128)S(1)} %copy-done.4, bf16[256,256]{1,0:T(8,128)(2,1)S(1)} %collective-permute-done.4.refs_0_, ...), custom_call_target="tpu_custom_call", output_to_operand_aliasing={{0}: (10, {}), {1}: (11, {})} | custom-call | flops 1073741824 | bytes 2097152 | tf_op jit(solution)/shard_map/ring_step/pallas_call | solution.py:149
  77.0 4.2 %ring_step.14 = (bf16[48,256,512]{2,1,0:T(8,128)(2,1)S(1)}, f32[8,128,256]{2,1,0:T(8,128)S(1)}) custom-call(s32[2]{0:T(128)S(1)} %pad_add_fusion.place_ref, s32[384]{0:T(512)S(1)} %reshape.90.col_ref, s32[64]{0:T(128)S(1)} %copy-done.4, bf16[256,256]{1,0:T(8,128)(2,1)S(1)} %collective-permute-done.5.refs_0_, ...), custom_call_target="tpu_custom_call", output_to_operand_aliasing={{0}: (10, {}), {1}: (11, {})} | custom-call | flops 1073741824 | bytes 2097152 | tf_op jit(solution)/shard_map/ring_step/pallas_call | solution.py:149
  81.2 4.0 %ring_step.15 = (bf16[48,256,512]{2,1,0:T(8,128)(2,1)S(1)}, f32[8,128,256]{2,1,0:T(8,128)S(1)}) custom-call(s32[2]{0:T(128)S(1)} %pad_add_fusion.place_ref, s32[384]{0:T(512)S(1)} %reshape.90.col_ref, s32[64]{0:T(128)S(1)} %copy-done.4, bf16[256,256]{1,0:T(8,128)(2,1)S(1)} %collective-permute-done.6.refs_0_, ...), custom_call_target="tpu_custom_call", output_to_operand_aliasing={{0}: (10, {}), {1}: (11, {})} | custom-call | flops 1073741824 | bytes 2097152 | tf_op jit(solution)/shard_map/ring_step/pallas_call | solution.py:149
  85.2 2.6 %sent_half.2 = (bf16[4,4,6,64,128]{4,3,2,1,0:T(8,128)(2,1)S(1)}, bf16[8,64,256]{2,1,0:T(8,128)(2,1)S(1)}, bf16[8,64,256]{2,1,0:T(8,128)(2,1)S(1)}, f32[4,128]{1,0:T(4,128)S(1)}, f32[4,128]{1,0:T(4,128)S(1)}) custom-call(s32[2]{0:T(128)S(1)} %pad_add_fusion.place_ref, s32[64]{0:T(128)S(1)} %copy-done.4, f32[8,128,256]{2,1,0:T(8,128)S(1)} %get-tuple-element.47.refs_0_, ...), custom_call_target="tpu_custom_call" | custom-call | tf_op jit(solution)/shard_map/sent_half/pallas_call | solution.py:227
  90.2 3.2 %collective-permute-done.31 = f32[4,128]{1,0:T(4,128)S(1)} collective-permute-done((f32[4,128]{1,0:T(4,128)S(1)}, f32[4,128]{1,0:T(4,128)S(1)}, u32[]{:S(2)}, u32[]{:S(2)}) %collective-permute-start.31) | collective-permute-done | bytes 2080 | tf_op jit(solution)/shard_map/ppermute | solution.py:310
  94.1 2.6 %kept_half.2.refs_0_ = bf16[4,8,6,64,128]{4,3,2,1,0:T(8,128)(2,1)} custom-call(s32[2]{0:T(128)S(1)} %pad_add_fusion.place_ref, s32[64]{0:T(128)S(1)} %copy-done.4, bf16[8,64,256]{2,1,0:T(8,128)(2,1)S(1)} %get-tuple-element.49.mine_ref, bf16[48,256,512]{2,1,0:T(8,128)(2,1)S(1)} %get-tuple-element.48.refs_1_.states_ref, ...), custom_call_target="tpu_custom_call" | custom-call | tf_op jit(solution)/shard_map/kept_half/pallas_call | solution.py:263
  96.7 2.6 %kept_half.3 = bf16[4,8,6,64,128]{4,3,2,1,0:T(8,128)(2,1)} custom-call(s32[2]{0:T(128)S(1)} %pad_add_fusion.place_ref, s32[64]{0:T(128)S(1)} %copy-done.4, bf16[8,64,256]{2,1,0:T(8,128)(2,1)S(1)} %get-tuple-element.49.mine_ref, bf16[48,256,512]{2,1,0:T(8,128)(2,1)S(1)} %get-tuple-element.48.refs_1_.states_ref, ...), custom_call_target="tpu_custom_call", output_to_operand_aliasing={{}: (5, {})} | custom-call | tf_op jit(solution)/shard_map/kept_half/pallas_call | solution.py:263
  (77 shorter events, 27.0 us)
Async XLA Ops:
  8.7 9.0 %collective-permute-start.22 = (bf16[272,256]{1,0:T(8,128)(2,1)S(1)}, bf16[272,256]{1,0:T(8,128)(2,1)S(1)}, u32[]{:S(2)}, u32[]{:S(2)}) collective-permute-start(bf16[272,256]{1,0:T(8,128)(2,1)S(1)} %get-tuple-element.32.refs_3_), channel_id=1, source_target_pairs={{4,0},{8,4},{12,8},{14,12},{10,14},{6,10},{2,6},{0,2},{5,1},{9,5},... | collective-permute-start | bytes 417800 | tf_op jit(solution)/shard_map/ppermute | solution.py:299
  10.7 7.0 %collective-permute-start.8 = (bf16[272,256]{1,0:T(8,128)(2,1)S(1)}, bf16[272,256]{1,0:T(8,128)(2,1)S(1)}, u32[]{:S(2)}, u32[]{:S(2)}) collective-permute-start(bf16[272,256]{1,0:T(8,128)(2,1)S(1)} %get-tuple-element.30.refs_1_), channel_id=1, source_target_pairs={{0,4},{4,8},{8,12},{12,14},{14,10},{10,6},{6,2},{2,0},{1,5},{5,9},... | collective-permute-start | bytes 417800 | tf_op jit(solution)/shard_map/ppermute | solution.py:299
  12.0 9.0 %collective-permute-start.1 = (bf16[256,256]{1,0:T(8,128)(2,1)S(1)}, bf16[256,256]{1,0:T(8,128)(2,1)S(1)}, u32[]{:S(2)}, u32[]{:S(2)}) collective-permute-start(bf16[256,256]{1,0:T(8,128)(2,1)S(1)} %collective-permute-done.refs_0_), channel_id=1, source_target_pairs={{0,4},{4,8},{8,12},{12,14},{14,10},{10,6},{6,2},{2,0},{1,5},{5,9},... | collective-permute-start | bytes 393224 | tf_op jit(solution)/shard_map/ppermute | solution.py:299
  17.7 8.3 %collective-permute-start.23 = (bf16[272,256]{1,0:T(8,128)(2,1)S(1)}, bf16[272,256]{1,0:T(8,128)(2,1)S(1)}, u32[]{:S(2)}, u32[]{:S(2)}) collective-permute-start(bf16[272,256]{1,0:T(8,128)(2,1)S(1)} %collective-permute-done.22.refs_3_), channel_id=1, source_target_pairs={{4,0},{8,4},{12,8},{14,12},{10,14},{6,10},{2,6},{0,2},{5,1},{9,5},... | collective-permute-start | bytes 417800 | tf_op jit(solution)/shard_map/ppermute | solution.py:299
  17.7 6.6 %collective-permute-start.9 = (bf16[272,256]{1,0:T(8,128)(2,1)S(1)}, bf16[272,256]{1,0:T(8,128)(2,1)S(1)}, u32[]{:S(2)}, u32[]{:S(2)}) collective-permute-start(bf16[272,256]{1,0:T(8,128)(2,1)S(1)} %collective-permute-done.8.refs_1_), channel_id=1, source_target_pairs={{0,4},{4,8},{8,12},{12,14},{14,10},{10,6},{6,2},{2,0},{1,5},{5,9},... | collective-permute-start | bytes 417800 | tf_op jit(solution)/shard_map/ppermute | solution.py:299
  20.7 6.4 %collective-permute-start.17 = (bf16[256,256]{1,0:T(8,128)(2,1)S(1)}, bf16[256,256]{1,0:T(8,128)(2,1)S(1)}, u32[]{:S(2)}, u32[]{:S(2)}) collective-permute-start(bf16[256,256]{1,0:T(8,128)(2,1)S(1)} %collective-permute-done.16.refs_2_), channel_id=1, source_target_pairs={{4,0},{8,4},{12,8},{14,12},{10,14},{6,10},{2,6},{0,2},{5,1},{9,5},... | collective-permute-start | bytes 393224 | tf_op jit(solution)/shard_map/ppermute | solution.py:299
  21.1 7.2 %collective-permute-start.2 = (bf16[256,256]{1,0:T(8,128)(2,1)S(1)}, bf16[256,256]{1,0:T(8,128)(2,1)S(1)}, u32[]{:S(2)}, u32[]{:S(2)}) collective-permute-start(bf16[256,256]{1,0:T(8,128)(2,1)S(1)} %collective-permute-done.1.refs_0_), channel_id=1, source_target_pairs={{0,4},{4,8},{8,12},{12,14},{14,10},{10,6},{6,2},{2,0},{1,5},{5,9},... | collective-permute-start | bytes 393224 | tf_op jit(solution)/shard_map/ppermute | solution.py:299
  27.1 16.2 %collective-permute-start.18 = (bf16[256,256]{1,0:T(8,128)(2,1)S(1)}, bf16[256,256]{1,0:T(8,128)(2,1)S(1)}, u32[]{:S(2)}, u32[]{:S(2)}) collective-permute-start(bf16[256,256]{1,0:T(8,128)(2,1)S(1)} %collective-permute-done.17.refs_2_), channel_id=1, source_target_pairs={{4,0},{8,4},{12,8},{14,12},{10,14},{6,10},{2,6},{0,2},{5,1},{9,5},... | collective-permute-start | bytes 393224 | tf_op jit(solution)/shard_map/ppermute | solution.py:299
  28.3 16.8 %collective-permute-start.3 = (bf16[256,256]{1,0:T(8,128)(2,1)S(1)}, bf16[256,256]{1,0:T(8,128)(2,1)S(1)}, u32[]{:S(2)}, u32[]{:S(2)}) collective-permute-start(bf16[256,256]{1,0:T(8,128)(2,1)S(1)} %collective-permute-done.2.refs_0_), channel_id=1, source_target_pairs={{0,4},{4,8},{8,12},{12,14},{14,10},{10,6},{6,2},{2,0},{1,5},{5,9},... | collective-permute-start | bytes 393224 | tf_op jit(solution)/shard_map/ppermute | solution.py:299
  30.5 14.9 %collective-permute-start.11 = (bf16[272,256]{1,0:T(8,128)(2,1)S(1)}, bf16[272,256]{1,0:T(8,128)(2,1)S(1)}, u32[]{:S(2)}, u32[]{:S(2)}) collective-permute-start(bf16[272,256]{1,0:T(8,128)(2,1)S(1)} %collective-permute-done.10.refs_1_), channel_id=1, source_target_pairs={{0,4},{4,8},{8,12},{12,14},{14,10},{10,6},{6,2},{2,0},{1,5},{5,9},... | collective-permute-start | bytes 417800 | tf_op jit(solution)/shard_map/ppermute | solution.py:299
  32.1 14.9 %collective-permute-start.25 = (bf16[272,256]{1,0:T(8,128)(2,1)S(1)}, bf16[272,256]{1,0:T(8,128)(2,1)S(1)}, u32[]{:S(2)}, u32[]{:S(2)}) collective-permute-start(bf16[272,256]{1,0:T(8,128)(2,1)S(1)} %collective-permute-done.24.refs_3_), channel_id=1, source_target_pairs={{4,0},{8,4},{12,8},{14,12},{10,14},{6,10},{2,6},{0,2},{5,1},{9,5},... | collective-permute-start | bytes 417800 | tf_op jit(solution)/shard_map/ppermute | solution.py:299
  43.3 12.5 %collective-permute-start.19 = (bf16[256,256]{1,0:T(8,128)(2,1)S(1)}, bf16[256,256]{1,0:T(8,128)(2,1)S(1)}, u32[]{:S(2)}, u32[]{:S(2)}) collective-permute-start(bf16[256,256]{1,0:T(8,128)(2,1)S(1)} %collective-permute-done.18.refs_2_), channel_id=1, source_target_pairs={{4,0},{8,4},{12,8},{14,12},{10,14},{6,10},{2,6},{0,2},{5,1},{9,5},... | collective-permute-start | bytes 393224 | tf_op jit(solution)/shard_map/ppermute | solution.py:299
  45.1 13.4 %collective-permute-start.4 = (bf16[256,256]{1,0:T(8,128)(2,1)S(1)}, bf16[256,256]{1,0:T(8,128)(2,1)S(1)}, u32[]{:S(2)}, u32[]{:S(2)}) collective-permute-start(bf16[256,256]{1,0:T(8,128)(2,1)S(1)} %collective-permute-done.3.refs_0_), channel_id=1, source_target_pairs={{0,4},{4,8},{8,12},{12,14},{14,10},{10,6},{6,2},{2,0},{1,5},{5,9},... | collective-permute-start | bytes 393224 | tf_op jit(solution)/shard_map/ppermute | solution.py:299
  45.4 13.1 %collective-permute-start.12 = (bf16[272,256]{1,0:T(8,128)(2,1)S(1)}, bf16[272,256]{1,0:T(8,128)(2,1)S(1)}, u32[]{:S(2)}, u32[]{:S(2)}) collective-permute-start(bf16[272,256]{1,0:T(8,128)(2,1)S(1)} %collective-permute-done.11.refs_1_), channel_id=1, source_target_pairs={{0,4},{4,8},{8,12},{12,14},{14,10},{10,6},{6,2},{2,0},{1,5},{5,9},... | collective-permute-start | bytes 417800 | tf_op jit(solution)/shard_map/ppermute | solution.py:299
  47.0 11.6 %collective-permute-start.26 = (bf16[272,256]{1,0:T(8,128)(2,1)S(1)}, bf16[272,256]{1,0:T(8,128)(2,1)S(1)}, u32[]{:S(2)}, u32[]{:S(2)}) collective-permute-start(bf16[272,256]{1,0:T(8,128)(2,1)S(1)} %collective-permute-done.25.refs_3_), channel_id=1, source_target_pairs={{4,0},{8,4},{12,8},{14,12},{10,14},{6,10},{2,6},{0,2},{5,1},{9,5},... | collective-permute-start | bytes 417800 | tf_op jit(solution)/shard_map/ppermute | solution.py:299
  55.8 12.2 %collective-permute-start.20 = (bf16[256,256]{1,0:T(8,128)(2,1)S(1)}, bf16[256,256]{1,0:T(8,128)(2,1)S(1)}, u32[]{:S(2)}, u32[]{:S(2)}) collective-permute-start(bf16[256,256]{1,0:T(8,128)(2,1)S(1)} %collective-permute-done.19.refs_2_), channel_id=1, source_target_pairs={{4,0},{8,4},{12,8},{14,12},{10,14},{6,10},{2,6},{0,2},{5,1},{9,5},... | collective-permute-start | bytes 393224 | tf_op jit(solution)/shard_map/ppermute | solution.py:299
  58.5 12.3 %collective-permute-start.5 = (bf16[256,256]{1,0:T(8,128)(2,1)S(1)}, bf16[256,256]{1,0:T(8,128)(2,1)S(1)}, u32[]{:S(2)}, u32[]{:S(2)}) collective-permute-start(bf16[256,256]{1,0:T(8,128)(2,1)S(1)} %collective-permute-done.4.refs_0_), channel_id=1, source_target_pairs={{0,4},{4,8},{8,12},{12,14},{14,10},{10,6},{6,2},{2,0},{1,5},{5,9},... | collective-permute-start | bytes 393224 | tf_op jit(solution)/shard_map/ppermute | solution.py:299
  58.5 12.3 %collective-permute-start.13 = (bf16[272,256]{1,0:T(8,128)(2,1)S(1)}, bf16[272,256]{1,0:T(8,128)(2,1)S(1)}, u32[]{:S(2)}, u32[]{:S(2)}) collective-permute-start(bf16[272,256]{1,0:T(8,128)(2,1)S(1)} %collective-permute-done.12.refs_1_), channel_id=1, source_target_pairs={{0,4},{4,8},{8,12},{12,14},{14,10},{10,6},{6,2},{2,0},{1,5},{5,9},... | collective-permute-start | bytes 417800 | tf_op jit(solution)/shard_map/ppermute | solution.py:299
  58.7 12.3 %collective-permute-start.27 = (bf16[272,256]{1,0:T(8,128)(2,1)S(1)}, bf16[272,256]{1,0:T(8,128)(2,1)S(1)}, u32[]{:S(2)}, u32[]{:S(2)}) collective-permute-start(bf16[272,256]{1,0:T(8,128)(2,1)S(1)} %collective-permute-done.26.refs_3_), channel_id=1, source_target_pairs={{4,0},{8,4},{12,8},{14,12},{10,14},{6,10},{2,6},{0,2},{5,1},{9,5},... | collective-permute-start | bytes 417800 | tf_op jit(solution)/shard_map/ppermute | solution.py:299
  68.1 13.1 %collective-permute-start.21 = (bf16[256,256]{1,0:T(8,128)(2,1)S(1)}, bf16[256,256]{1,0:T(8,128)(2,1)S(1)}, u32[]{:S(2)}, u32[]{:S(2)}) collective-permute-start(bf16[256,256]{1,0:T(8,128)(2,1)S(1)} %collective-permute-done.20.refs_2_), channel_id=1, source_target_pairs={{4,0},{8,4},{12,8},{14,12},{10,14},{6,10},{2,6},{0,2},{5,1},{9,5},... | collective-permute-start | bytes 393224 | tf_op jit(solution)/shard_map/ppermute | solution.py:299
  70.7 10.4 %collective-permute-start.6 = (bf16[256,256]{1,0:T(8,128)(2,1)S(1)}, bf16[256,256]{1,0:T(8,128)(2,1)S(1)}, u32[]{:S(2)}, u32[]{:S(2)}) collective-permute-start(bf16[256,256]{1,0:T(8,128)(2,1)S(1)} %collective-permute-done.5.refs_0_), channel_id=1, source_target_pairs={{0,4},{4,8},{8,12},{12,14},{14,10},{10,6},{6,2},{2,0},{1,5},{5,9},... | collective-permute-start | bytes 393224 | tf_op jit(solution)/shard_map/ppermute | solution.py:299
  70.7 10.4 %collective-permute-start.14 = (bf16[272,256]{1,0:T(8,128)(2,1)S(1)}, bf16[272,256]{1,0:T(8,128)(2,1)S(1)}, u32[]{:S(2)}, u32[]{:S(2)}) collective-permute-start(bf16[272,256]{1,0:T(8,128)(2,1)S(1)} %collective-permute-done.13.refs_1_), channel_id=1, source_target_pairs={{0,4},{4,8},{8,12},{12,14},{14,10},{10,6},{6,2},{2,0},{1,5},{5,9},... | collective-permute-start | bytes 417800 | tf_op jit(solution)/shard_map/ppermute | solution.py:299
  70.9 10.2 %collective-permute-start.28 = (bf16[272,256]{1,0:T(8,128)(2,1)S(1)}, bf16[272,256]{1,0:T(8,128)(2,1)S(1)}, u32[]{:S(2)}, u32[]{:S(2)}) collective-permute-start(bf16[272,256]{1,0:T(8,128)(2,1)S(1)} %collective-permute-done.27.refs_3_), channel_id=1, source_target_pairs={{4,0},{8,4},{12,8},{14,12},{10,14},{6,10},{2,6},{0,2},{5,1},{9,5},... | collective-permute-start | bytes 417800 | tf_op jit(solution)/shard_map/ppermute | solution.py:299
  89.6 7.1 %collective-permute-start.29 = (bf16[4,4,6,64,128]{4,3,2,1,0:T(8,128)(2,1)S(1)}, bf16[4,4,6,64,128]{4,3,2,1,0:T(8,128)(2,1)S(1)}, u32[]{:S(2)}, u32[]{:S(2)}) collective-permute-start(bf16[4,4,6,64,128]{4,3,2,1,0:T(8,128)(2,1)S(1)} %sent_half.3), channel_id=1, source_target_pairs={{0,1},{1,0},{2,3},{3,2},{4,5},{5,4},{6,7},{7,6},{8,9},{9,8},{10,11... | collective-permute-start | bytes 4718600 | tf_op jit(solution)/shard_map/ppermute | solution.py:313
  (14 other events, 52.7 us)

commit v4 on v3

--- a/solution.py
+++ b/solution.py
@@ -90,15 +90,59 @@
     return jnp.where(index % 2 == 0, index // 2, n - 1 - index // 2)
 
 
-def step_kernel(shape, step, place_ref, col_ref, fill_ref, *refs):
+SMEM = pl.BlockSpec(memory_space=pltpu.SMEM)
+VMEM = pl.BlockSpec(memory_space=pltpu.VMEM)
+
+
+def plan_kernel(shape, place_ref, col_ref, fill_ref, plan_ref):
+    brows, slots, width, n, most = shape
+    own = place_ref[0]
+    entries = brows * slots
+    tail = n * (most + 1)
+    plan_ref[tail] = place_ref[1]
+    for step in range(n):
+        plan_ref[step * (most + 1)] = 0
+
+    @pl.loop(0, brows)
+    def _(row):
+        fill = fill_ref[own * brows + row]
+        plan_ref[tail + 1 + row] = fill
+
+        @pl.loop(0, fill)
+        def _(slot):
+            column = col_ref[own * entries + row * slots + slot]
+            source = lax.div(column, width)
+            block = lax.rem(column, width)
+            ahead = ring_place(source, n) - ring_place(own, n)
+            ahead = jnp.where(block < width // 2, -ahead, ahead)
+            ahead = jnp.where(ahead < 0, ahead + n, ahead)
+            base = ahead * (most + 1)
+            count = plan_ref[base] + 1
+            plan_ref[base] = count
+            plan_ref[base + count] = (row * 256 + slot) * 256 + block
+
+
+def make_plan(place, cols, fill, dims, width, n):
+    _, brows, slots, _ = dims
+    most = 2 * max(2, brows * slots // n)
+    return pl.pallas_call(
+        functools.partial(plan_kernel, (brows, slots, width, n, most)),
+        in_specs=[SMEM] * 3,
+        out_specs=SMEM,
+        out_shape=jax.ShapeDtypeStruct((n * (most + 1) + 1 + brows,), jnp.int32),
+        name="plan",
+    )(place, cols, fill)
+
+
+def step_kernel(shape, step, plan_ref, *refs):
     basis, brows, slots, tile, n = shape
     chunks = refs[:STREAMS]
     lag_ref, power_ref, excite_ref = refs[STREAMS : STREAMS + 3]
-    states_ref, total_ref, held = refs[-3:]
+    states_ref, total_ref, built_ref, held = refs[-4:]
     bins, lanes = chunks[0].shape
     per = lanes // tile
-    width = STREAMS * per
-    own = place_ref[0]
+    built_ref[...] = jnp.zeros_like(built_ref)
+    most = (plan_ref.shape[0] - 1 - brows) // n - 1
     if step == 0:
         counts_ref, base_ref = refs[STREAMS + 3 : STREAMS + 5]
         for row in range(brows):
@@ -116,43 +160,33 @@
                     state[:, at] + power_ref[b] * carry[row : row + 1, at]
                 ).astype(jnp.bfloat16)
 
-    @pl.loop(0, brows * slots)
-    def _(entry):
-        row = entry // slots
-        slot = entry - row * slots
-        column = col_ref[own * (brows * slots) + entry]
-        source = column // width
-        block = column - source * width
-        ahead = ring_place(source, n) - ring_place(own, n)
-        ahead = jnp.where(block < width // 2, -ahead, ahead)
-        ahead = jnp.where(ahead < 0, ahead + n, ahead)
-
-        @pl.when((ahead == step) & (slot < fill_ref[own * brows + row]))
-        def _():
-            state = held[block]
-            states_ref[entry] = state
-            weight = jnp.concatenate([excite_ref[b, row, slot] for b in range(basis)], axis=1)
-            total_ref[row] += lax.dot_general(
-                weight, state, (((1,), (1,)), ((), ())), preferred_element_type=jnp.float32
-            )
-
-
-SMEM = pl.BlockSpec(memory_space=pltpu.SMEM)
-VMEM = pl.BlockSpec(memory_space=pltpu.VMEM)
-
-
-def take_step(step, scalars, chunks, lag, power, excite, more, n):
+    @pl.loop(0, plan_ref[step * (most + 1)])
+    def _(k):
+        code = plan_ref[step * (most + 1) + 1 + k]
+        block = code & 255
+        slot = (code >> 8) & 255
+        row = code >> 16
+        state = held[block]
+        states_ref[row * slots + slot] = state
+        weight = jnp.concatenate([excite_ref[b, row, slot] for b in range(basis)], axis=1)
+        total_ref[row] += lax.dot_general(
+            weight, state, (((1,), (1,)), ((), ())), preferred_element_type=jnp.float32
+        )
+
+
+def take_step(step, plan, chunks, lag, power, excite, more, n):
     basis, brows, slots, tile, _ = excite.shape
     bins = lag.shape[1]
     lanes = chunks[0].shape[1]
-    before = 3 + STREAMS + 3
+    before = 1 + STREAMS + 3
     return pl.pallas_call(
         functools.partial(step_kernel, (basis, brows, slots, tile, n), step),
-        in_specs=[SMEM] * 3 + [VMEM] * (STREAMS + 5),
-        out_specs=[VMEM, VMEM],
+        in_specs=[SMEM] + [VMEM] * (STREAMS + 5),
+        out_specs=[VMEM, VMEM, VMEM],
         out_shape=[
             jax.ShapeDtypeStruct((brows * slots, bins, basis * tile), jnp.bfloat16),
             jax.ShapeDtypeStruct((brows, tile, bins), jnp.float32),
+            jax.ShapeDtypeStruct((8, tile), jnp.float32),
         ],
         scratch_shapes=[pltpu.VMEM((STREAMS * lanes // tile, bins, basis * tile), jnp.bfloat16)],
         input_output_aliases={} if step == 0 else {before: 0, before + 1: 1},
@@ -163,7 +197,7 @@
             transcendentals=0,
         ),
         name="ring_step",
-    )(*scalars, *chunks, lag, power, excite, *more)
+    )(plan, *chunks, lag, power, excite, *more)
 
 
 def products(turned_ref, states_ref, fills, rows, slots, basis, tile, put):
@@ -177,9 +211,10 @@
                 put(b, r, row, s, grad[:, b * tile : (b + 1) * tile])
 
 
-def sent_kernel(shape, group, place_ref, fill_ref, *refs):
+def sent_kernel(shape, group, plan_ref, *refs):
     basis, brows, slots, tile, overall = shape
-    own, half = place_ref[0], place_ref[1]
+    tail = plan_ref.shape[0] - 1 - brows
+    half = plan_ref[tail]
     part = tile // 2
     if group == 0:
         total_ref, states_ref, out_ref, other_ref, mine_ref, rate_own_ref, rate_sent_ref = refs
@@ -208,7 +243,7 @@
         other_ref, states_ref, out_ref = refs
     count = brows // GROUPS
     rows = range(group * count, (group + 1) * count)
-    fills = [fill_ref[own * brows + row] for row in rows]
+    fills = [plan_ref[tail + 1 + row] for row in rows]
 
     def put(b, r, row, s, grad):
         out_ref[b, r, s] = grad.astype(jnp.bfloat16)
@@ -216,7 +251,7 @@
     products(other_ref, states_ref, fills, rows, slots, basis, tile, put)
 
 
-def sent(group, place, fill, given, states, dims, overall):
+def sent(group, plan, given, states, dims, overall):
     basis, brows, slots, tile = dims
     bins = states.shape[1]
     part = tile // 2
@@ -226,18 +261,18 @@
         out_shape += [jax.ShapeDtypeStruct((brows // 2, tile), jnp.float32)] * 2
     return pl.pallas_call(
         functools.partial(sent_kernel, (basis, brows, slots, tile, overall), group),
-        in_specs=[SMEM, SMEM, VMEM, VMEM],
+        in_specs=[SMEM, VMEM, VMEM],
         out_specs=[VMEM] * len(out_shape),
         out_shape=out_shape,
         compiler_params=pltpu.CompilerParams(vmem_limit_bytes=16 << 20),
         name="sent_half",
-    )(place, fill, given, states)
-
-
-def kept_kernel(shape, group, place_ref, fill_ref, mine_ref, states_ref, got_ref, *refs):
+    )(plan, given, states)
+
+
+def kept_kernel(shape, group, plan_ref, mine_ref, states_ref, got_ref, *refs):
     basis, brows, slots, tile = shape
     out_ref, held, sems = refs[-3:]
-    own = place_ref[0]
+    tail = plan_ref.shape[0] - 1 - brows
     count = brows // GROUPS
     copies = []
     for r in range(count):
@@ -246,7 +281,7 @@
         def put(b, _, row, s, grad, r=r):
             held[b, r, s] = (grad + got_ref[b, r, s].astype(jnp.float32)).astype(jnp.bfloat16)
 
-        products(mine_ref, states_ref, [fill_ref[own * brows + row]], [row], slots, basis, tile, put)
+        products(mine_ref, states_ref, [plan_ref[tail + 1 + row]], [row], slots, basis, tile, put)
         for b in range(basis):
             copy = pltpu.make_async_copy(held.at[b, r], out_ref.at[b, row], sems.at[b, r])
             copy.start()
@@ -255,24 +290,24 @@
         copy.wait()
 
 
-def kept(group, place, fill, mine, states, got, out, dims):
+def kept(group, plan, mine, states, got, out, dims):
     basis, brows, slots, tile = dims
     part = tile // 2
     anywhere = pl.BlockSpec(memory_space=pl.ANY)
     given = [] if out is None else [out]
     return pl.pallas_call(
         functools.partial(kept_kernel, dims, group),
-        in_specs=[SMEM, SMEM, VMEM, VMEM, VMEM] + [anywhere] * len(given),
+        in_specs=[SMEM, VMEM, VMEM, VMEM] + [anywhere] * len(given),
         out_specs=anywhere,
         out_shape=jax.ShapeDtypeStruct((basis, brows, slots, part, tile), jnp.bfloat16),
         scratch_shapes=[
             pltpu.VMEM((basis, brows // GROUPS, slots, part, tile), jnp.bfloat16),
             pltpu.SemaphoreType.DMA((basis, brows // GROUPS)),
         ],
-        input_output_aliases={5: 0} if given else {},
+        input_output_aliases={4: 0} if given else {},
         compiler_params=pltpu.CompilerParams(vmem_limit_bytes=16 << 20),
         name="kept_half",
-    )(place, fill, mine, states, got, *given)
+    )(plan, mine, states, got, *given)
 
 
 def shards(counts, mark_value, base_rate, excite, block_col, row_fill):
@@ -290,7 +325,8 @@
     up_two, down_two = second(counts, mark_value, enter, basis)
     lag, power = lag_tables(bins, basis, overall, tile)
     chunks = [up_one, up_two, down_one, down_two]
-    scalars = (place, block_col.reshape(-1), row_fill)
+    dims = (basis, brows, slots, tile)
+    plan = make_plan(place, block_col.reshape(-1), row_fill, dims, counts.shape[1] // tile, n)
     more = (counts, base_rate.reshape(1, -1))
     for step in range(n):
         ahead = None
@@ -300,20 +336,21 @@
                 for j in (0, 2, 1, 3)
             ]
             ahead = [ahead[0], ahead[2], ahead[1], ahead[3]]
-        more = take_step(step, scalars, chunks, lag, power, excite, more, n)
+        *more, built = take_step(step, plan, chunks, lag, power, excite, more, n)
+        if step < n - 1:
+            ahead = [lax.optimization_barrier((chunk, built))[0] for chunk in ahead]
         chunks = ahead
     states, total = more
-    dims = (basis, brows, slots, tile)
     swap = [(0, 1), (1, 0)]
-    out, other, mine, rate_own, rate_sent = sent(0, place, row_fill, total, states, dims, overall)
+    out, other, mine, rate_own, rate_sent = sent(0, plan, total, states, dims, overall)
     got = [lax.ppermute(out, "tm", swap)]
     rate_got = lax.ppermute(rate_sent, "tm", swap)
     for group in range(1, GROUPS):
-        (out,) = sent(group, place, row_fill, other, states, dims, overall)
+        (out,) = sent(group, plan, other, states, dims, overall)
         got.append(lax.ppermute(out, "tm", swap))
     grad = None
     for group in range(GROUPS):
-        grad = kept(group, place, row_fill, mine, states, got[group], grad, dims)
+        grad = kept(group, plan, mine, states, got[group], grad, dims)
     return grad, (rate_own + rate_got).reshape(-1)
 
 

time: 99.4 us -> 88.9 us (0.89); the launches traced: 99.5 us -> 88 us
  Pallas kernels: 42.6 us -> 35.6 us
  waiting for transfers between devices: 11.8 us -> 5.51 us
  local copies, waits for them, and re-layouts: 8.71 us -> 11.6 us
  starting transfers between devices: 34.1 us -> 32.5 us
    pallas_call x8, Pallas kernels: 32.2 us -> 23 us  [take_step(): pl.pallas_call(functools.partial(step_kernel, (basis, brows, slots, tile,...]
    ppermute x28, waiting for transfers between devices: 8.57 us -> 2.25 us  [shards(): lax.ppermute(chunks[j], 'types', up if j < STREAMS // 2 else down)]
    unnamed x13 -> x17, local copies, waits for them, and re-layouts: 8.39 us -> 10.7 us
    pallas_call x0 -> x1, Pallas kernels: none -> 2.19 us  [make_plan(): pl.pallas_call(functools.partial(plan_kernel, (brows, slots, width, n, mo...]
    ppermute x28, starting transfers between devices: 31 us -> 29.5 us  [shards(): lax.ppermute(chunks[j], 'types', up if j < STREAMS // 2 else down)]
  transfers between devices with their start and end apart: 32 -> 32, of which waited for: 8 -> 3; matrix products, arithmetic and copies ran while one was open for 2% -> 4% of each run, Pallas kernels for 33% -> 30%
where the time goes in v4:
time: 88.9 us; the launch traced here: 88 us
  Pallas kernels  35.6 us (40%)
  starting transfers between devices  32.5 us (37%)
  local copies, waits for them, and re-layouts  11.6 us (13%)
  waiting for transfers between devices  5.51 us (6%)
  other arithmetic  1.79 us (2%)
  between operations  0.95 us (1%)
    ppermute x28, starting transfers between devices, shards(): lax.ppermute(chunks[j], 'types', up if j < STREAMS // 2 else down)  29.5 us
    pallas_call x8, Pallas kernels, take_step(): pl.pallas_call(functools.partial(step_kernel, (basis, brows, slots, tile,...  23 us
    unnamed x17, local copies, waits for them, and re-layouts  10.7 us
    pallas_call x2, Pallas kernels, kept(): pl.pallas_call(functools.partial(kept_kernel, dims, group), in_specs=[SME...  5.27 us
    pallas_call x2, Pallas kernels, sent(): pl.pallas_call(functools.partial(sent_kernel, (basis, brows, slots, tile,...  4.33 us
    ppermute x1, waiting for transfers between devices, shards(): rate_got = lax.ppermute(rate_sent, 'tm', swap)  3.25 us
    ppermute x1, starting transfers between devices, shards(): enter = lax.ppermute(ends, 'tm', [(0, 1)])  2.35 us
    ppermute x28, waiting for transfers between devices, shards(): lax.ppermute(chunks[j], 'types', up if j < STREAMS // 2 else down)  2.25 us
  transfers between devices with their start and end apart: 32, of which 3 were waited for; matrix products, arithmetic and copies ran while one was open for 4% of the time, Pallas kernels for 30%

profile of v4, /device:TPU:0, one launch (start us, length us, event | category | flops | bytes accessed | tf_op | source)
XLA Modules:
  0.0 88.0 jit_solution(6140770286127201139)
XLA Ops:
  3.7 2.4 %collective-permute-start.1 = (f32[4,1024]{1,0:T(4,128)S(1)}, f32[4,1024]{1,0:T(4,128)S(1)}, u32[]{:S(2)}, u32[]{:S(2)}) collective-permute-start(f32[4,1024]{1,0:T(4,128)S(1)} %get-tuple-element.64), channel_id=1, source_target_pairs={{0,1},{2,3},{4,5},{6,7},{8,9},{10,11},{12,13},{14,15},{16,17},{18,... | collective-permute-start | bytes 49160 | tf_op jit(solution)/shard_map/ppermute | solution.py:324
  6.0 2.4 %collective-permute-start.4 = (bf16[256,256]{1,0:T(8,128)(2,1)S(1)}, bf16[256,256]{1,0:T(8,128)(2,1)S(1)}, u32[]{:S(2)}, u32[]{:S(2)}) collective-permute-start(bf16[256,256]{1,0:T(8,128)(2,1)S(1)} %get-tuple-element.66.refs_2_), channel_id=1, source_target_pairs={{4,0},{8,4},{12,8},{14,12},{10,14},{6,10},{2,6},{0,2},{5,1},{9,5},... | collective-permute-start | bytes 393224 | tf_op jit(solution)/shard_map/ppermute | solution.py:335
  15.7 2.2 %plan.1.plan_ref = s32[113]{0:T(128)} custom-call(s32[2]{0:T(128)} %pad_add_fusion.place_ref, s32[384]{0:T(512)} %reshape.90.col_ref, s32[64]{0:T(128)} %fill_ref.1), custom_call_target="tpu_custom_call" | custom-call | tf_op jit(solution)/shard_map/plan/pallas_call | solution.py:128
  18.1 2.8 %copy-done = bf16[4,8,6,128,128]{4,3,2,1,0:T(8,128)(2,1)S(1)} copy-done((bf16[4,8,6,128,128]{4,3,2,1,0:T(8,128)(2,1)S(1)}, bf16[4,8,6,128,128]{4,3,2,1,0:T(8,128)(2,1)}, u32[]{:S(2)}) %copy-start) | copy-done | bytes 6291480
  23.4 3.3 %ring_step.8 = (bf16[48,256,512]{2,1,0:T(8,128)(2,1)S(1)}, f32[8,128,256]{2,1,0:T(8,128)S(1)}, f32[8,128]{1,0:T(8,128)}) custom-call(s32[113]{0:T(128)S(1)} %copy-done.6, bf16[256,256]{1,0:T(8,128)(2,1)S(1)} %get-tuple-element.63.refs_0_, bf16[272,256]{1,0:T(8,128)(2,1)S(1)} %get-tuple-element.65.refs_1_, bf16[256,256]{1,0:T(8,128)(2,1)S(1)} %get-tuple-element.66.refs_2_, ...), custom_call_target="tpu_custom_call" | custom-call | flops 1073741824 | bytes 2097152 | tf_op jit(solution)/shard_map/ring_step/pallas_call | solution.py:182
  30.8 2.6 %ring_step.9 = (bf16[48,256,512]{2,1,0:T(8,128)(2,1)S(1)}, f32[8,128,256]{2,1,0:T(8,128)S(1)}, f32[8,128]{1,0:T(8,128)}) custom-call(s32[113]{0:T(128)S(1)} %copy-done.6, bf16[256,256]{1,0:T(8,128)(2,1)S(1)} %collective-permute-done.refs_0_, bf16[272,256]{1,0:T(8,128)(2,1)S(1)} %collective-permute-done.3.refs_1_, ...), custom_call_target="tpu_custom_call", output_to_operand_aliasing={{0}: (8, {}), {1}: (9, {})} | custom-call | flops 1073741824 | bytes 2097152 | tf_op jit(solution)/shard_map/ring_step/pallas_call | solution.py:182
  33.4 2.1 %collective-permute-start.13 = (bf16[272,256]{1,0:T(8,128)(2,1)S(1)}, bf16[272,256]{1,0:T(8,128)(2,1)S(1)}, u32[]{:S(2)}, u32[]{:S(2)}) collective-permute-start(bf16[272,256]{1,0:T(8,128)(2,1)S(1)} %collective-permute-done.9.refs_3_), channel_id=1, source_target_pairs={{4,0},{8,4},{12,8},{14,12},{10,14},{6,10},{2,6},{0,2},{5,1},{9,5},... | collective-permute-start | bytes 417800 | tf_op jit(solution)/shard_map/ppermute | solution.py:335
  35.5 2.0 %collective-permute-start.12 = (bf16[256,256]{1,0:T(8,128)(2,1)S(1)}, bf16[256,256]{1,0:T(8,128)(2,1)S(1)}, u32[]{:S(2)}, u32[]{:S(2)}) collective-permute-start(bf16[256,256]{1,0:T(8,128)(2,1)S(1)} %collective-permute-done.8.refs_2_), channel_id=1, source_target_pairs={{4,0},{8,4},{12,8},{14,12},{10,14},{6,10},{2,6},{0,2},{5,1},{9,5},... | collective-permute-start | bytes 393224 | tf_op jit(solution)/shard_map/ppermute | solution.py:335
  37.6 3.3 %ring_step.10 = (bf16[48,256,512]{2,1,0:T(8,128)(2,1)S(1)}, f32[8,128,256]{2,1,0:T(8,128)S(1)}, f32[8,128]{1,0:T(8,128)}) custom-call(s32[113]{0:T(128)S(1)} %copy-done.6, bf16[256,256]{1,0:T(8,128)(2,1)S(1)} %collective-permute-done.2.refs_0_, bf16[272,256]{1,0:T(8,128)(2,1)S(1)} %collective-permute-done.7.refs_1_, ...), custom_call_target="tpu_custom_call", output_to_operand_aliasing={{0}: (8, {}), {1}: (9, {})} | custom-call | flops 1073741824 | bytes 2097152 | tf_op jit(solution)/shard_map/ring_step/pallas_call | solution.py:182
  40.8 2.0 %collective-permute-start.17 = (bf16[272,256]{1,0:T(8,128)(2,1)S(1)}, bf16[272,256]{1,0:T(8,128)(2,1)S(1)}, u32[]{:S(2)}, u32[]{:S(2)}) collective-permute-start(bf16[272,256]{1,0:T(8,128)(2,1)S(1)} %collective-permute-done.13.refs_3_), channel_id=1, source_target_pairs={{4,0},{8,4},{12,8},{14,12},{10,14},{6,10},{2,6},{0,2},{5,1},{9,5},... | collective-permute-start | bytes 417800 | tf_op jit(solution)/shard_map/ppermute | solution.py:335
  42.9 2.0 %collective-permute-start.16 = (bf16[256,256]{1,0:T(8,128)(2,1)S(1)}, bf16[256,256]{1,0:T(8,128)(2,1)S(1)}, u32[]{:S(2)}, u32[]{:S(2)}) collective-permute-start(bf16[256,256]{1,0:T(8,128)(2,1)S(1)} %collective-permute-done.12.refs_2_), channel_id=1, source_target_pairs={{4,0},{8,4},{12,8},{14,12},{10,14},{6,10},{2,6},{0,2},{5,1},{9,5},... | collective-permute-start | bytes 393224 | tf_op jit(solution)/shard_map/ppermute | solution.py:335
  44.9 2.6 %ring_step.11 = (bf16[48,256,512]{2,1,0:T(8,128)(2,1)S(1)}, f32[8,128,256]{2,1,0:T(8,128)S(1)}, f32[8,128]{1,0:T(8,128)}) custom-call(s32[113]{0:T(128)S(1)} %copy-done.6, bf16[256,256]{1,0:T(8,128)(2,1)S(1)} %collective-permute-done.6.refs_0_, bf16[272,256]{1,0:T(8,128)(2,1)S(1)} %collective-permute-done.11.refs_1_, ...), custom_call_target="tpu_custom_call", output_to_operand_aliasing={{0}: (8, {}), {1}: (9, {})} | custom-call | flops 1073741824 | bytes 2097152 | tf_op jit(solution)/shard_map/ring_step/pallas_call | solution.py:182
  47.5 2.0 %collective-permute-start.21 = (bf16[272,256]{1,0:T(8,128)(2,1)S(1)}, bf16[272,256]{1,0:T(8,128)(2,1)S(1)}, u32[]{:S(2)}, u32[]{:S(2)}) collective-permute-start(bf16[272,256]{1,0:T(8,128)(2,1)S(1)} %collective-permute-done.17.refs_3_), channel_id=1, source_target_pairs={{4,0},{8,4},{12,8},{14,12},{10,14},{6,10},{2,6},{0,2},{5,1},{9,5},... | collective-permute-start | bytes 417800 | tf_op jit(solution)/shard_map/ppermute | solution.py:335
  49.5 2.0 %collective-permute-start.20 = (bf16[256,256]{1,0:T(8,128)(2,1)S(1)}, bf16[256,256]{1,0:T(8,128)(2,1)S(1)}, u32[]{:S(2)}, u32[]{:S(2)}) collective-permute-start(bf16[256,256]{1,0:T(8,128)(2,1)S(1)} %collective-permute-done.16.refs_2_), channel_id=1, source_target_pairs={{4,0},{8,4},{12,8},{14,12},{10,14},{6,10},{2,6},{0,2},{5,1},{9,5},... | collective-permute-start | bytes 393224 | tf_op jit(solution)/shard_map/ppermute | solution.py:335
  51.8 2.8 %ring_step.12 = (bf16[48,256,512]{2,1,0:T(8,128)(2,1)S(1)}, f32[8,128,256]{2,1,0:T(8,128)S(1)}, f32[8,128]{1,0:T(8,128)}) custom-call(s32[113]{0:T(128)S(1)} %copy-done.6, bf16[256,256]{1,0:T(8,128)(2,1)S(1)} %collective-permute-done.10.refs_0_, bf16[272,256]{1,0:T(8,128)(2,1)S(1)} %collective-permute-done.15.refs_1_, ...), custom_call_target="tpu_custom_call", output_to_operand_aliasing={{0}: (8, {}), {1}: (9, {})} | custom-call | flops 1073741824 | bytes 2097152 | tf_op jit(solution)/shard_map/ring_step/pallas_call | solution.py:182
  58.7 2.6 %ring_step.13 = (bf16[48,256,512]{2,1,0:T(8,128)(2,1)S(1)}, f32[8,128,256]{2,1,0:T(8,128)S(1)}, f32[8,128]{1,0:T(8,128)}) custom-call(s32[113]{0:T(128)S(1)} %copy-done.6, bf16[256,256]{1,0:T(8,128)(2,1)S(1)} %collective-permute-done.14.refs_0_, bf16[272,256]{1,0:T(8,128)(2,1)S(1)} %collective-permute-done.19.refs_1_, ...), custom_call_target="tpu_custom_call", output_to_operand_aliasing={{0}: (8, {}), {1}: (9, {})} | custom-call | flops 1073741824 | bytes 2097152 | tf_op jit(solution)/shard_map/ring_step/pallas_call | solution.py:182
  61.3 2.4 %collective-permute-start.28 = (bf16[272,256]{1,0:T(8,128)(2,1)S(1)}, bf16[272,256]{1,0:T(8,128)(2,1)S(1)}, u32[]{:S(2)}, u32[]{:S(2)}) collective-permute-start(bf16[272,256]{1,0:T(8,128)(2,1)S(1)} %collective-permute-done.25.refs_3_), channel_id=1, source_target_pairs={{4,0},{8,4},{12,8},{14,12},{10,14},{6,10},{2,6},{0,2},{5,1},{9,5},... | collective-permute-start | bytes 417800 | tf_op jit(solution)/shard_map/ppermute | solution.py:335
  63.6 2.0 %collective-permute-start.27 = (bf16[256,256]{1,0:T(8,128)(2,1)S(1)}, bf16[256,256]{1,0:T(8,128)(2,1)S(1)}, u32[]{:S(2)}, u32[]{:S(2)}) collective-permute-start(bf16[256,256]{1,0:T(8,128)(2,1)S(1)} %collective-permute-done.24.refs_2_), channel_id=1, source_target_pairs={{4,0},{8,4},{12,8},{14,12},{10,14},{6,10},{2,6},{0,2},{5,1},{9,5},... | collective-permute-start | bytes 393224 | tf_op jit(solution)/shard_map/ppermute | solution.py:335
  65.7 3.0 %ring_step.14 = (bf16[48,256,512]{2,1,0:T(8,128)(2,1)S(1)}, f32[8,128,256]{2,1,0:T(8,128)S(1)}, f32[8,128]{1,0:T(8,128)}) custom-call(s32[113]{0:T(128)S(1)} %copy-done.6, bf16[256,256]{1,0:T(8,128)(2,1)S(1)} %collective-permute-done.18.refs_0_, bf16[272,256]{1,0:T(8,128)(2,1)S(1)} %collective-permute-done.23.refs_1_, ...), custom_call_target="tpu_custom_call", output_to_operand_aliasing={{0}: (8, {}), {1}: (9, {})} | custom-call | flops 1073741824 | bytes 2097152 | tf_op jit(solution)/shard_map/ring_step/pallas_call | solution.py:182
  70.6 3.0 %ring_step.15 = (bf16[48,256,512]{2,1,0:T(8,128)(2,1)S(1)}, f32[8,128,256]{2,1,0:T(8,128)S(1)}, f32[8,128]{1,0:T(8,128)}) custom-call(s32[113]{0:T(128)S(1)} %copy-done.6, bf16[256,256]{1,0:T(8,128)(2,1)S(1)} %collective-permute-done.22.refs_0_, bf16[272,256]{1,0:T(8,128)(2,1)S(1)} %collective-permute-done.26.refs_1_, ...), custom_call_target="tpu_custom_call", output_to_operand_aliasing={{0}: (8, {}), {1}: (9, {})} | custom-call | flops 1073741824 | bytes 2097152 | tf_op jit(solution)/shard_map/ring_step/pallas_call | solution.py:182
  73.6 2.6 %sent_half.2 = (bf16[4,4,6,64,128]{4,3,2,1,0:T(8,128)(2,1)S(1)}, bf16[8,64,256]{2,1,0:T(8,128)(2,1)S(1)}, bf16[8,64,256]{2,1,0:T(8,128)(2,1)S(1)}, f32[4,128]{1,0:T(4,128)S(1)}, f32[4,128]{1,0:T(4,128)S(1)}) custom-call(s32[113]{0:T(128)S(1)} %copy-done.6, f32[8,128,256]{2,1,0:T(8,128)S(1)} %get-tuple-element.117.refs_0_, ...), custom_call_target="tpu_custom_call" | custom-call | tf_op jit(solution)/shard_map/sent_half/pallas_call | solution.py:262
  78.7 3.3 %collective-permute-done.31 = f32[4,128]{1,0:T(4,128)S(1)} collective-permute-done((f32[4,128]{1,0:T(4,128)S(1)}, f32[4,128]{1,0:T(4,128)S(1)}, u32[]{:S(2)}, u32[]{:S(2)}) %collective-permute-start.31) | collective-permute-done | bytes 2080 | tf_op jit(solution)/shard_map/ppermute | solution.py:347
  82.5 2.6 %kept_half.2.refs_0_ = bf16[4,8,6,64,128]{4,3,2,1,0:T(8,128)(2,1)} custom-call(s32[113]{0:T(128)S(1)} %copy-done.6, bf16[8,64,256]{2,1,0:T(8,128)(2,1)S(1)} %get-tuple-element.119.mine_ref, bf16[48,256,512]{2,1,0:T(8,128)(2,1)S(1)} %get-tuple-element.118.refs_1_.states_ref, bf16[4,4,6,64,128]{4,3,2,1,0:T(8,128)(2,1)S(1)} %collective-permute-done.30.got_ref), custom_call_target="tpu_custom_call" | custom-call | tf_op jit(solution)/shard_map/kept_half/pallas_call | solution.py:298
  85.2 2.6 %kept_half.3 = bf16[4,8,6,64,128]{4,3,2,1,0:T(8,128)(2,1)} custom-call(s32[113]{0:T(128)S(1)} %copy-done.6, bf16[8,64,256]{2,1,0:T(8,128)(2,1)S(1)} %get-tuple-element.119.mine_ref, bf16[48,256,512]{2,1,0:T(8,128)(2,1)S(1)} %get-tuple-element.118.refs_1_.states_ref, ...), custom_call_target="tpu_custom_call", output_to_operand_aliasing={{}: (4, {})} | custom-call | tf_op jit(solution)/shard_map/kept_half/pallas_call | solution.py:298
  (82 shorter events, 26.8 us)
Async XLA Ops:
  6.0 22.8 %collective-permute-start.4 = (bf16[256,256]{1,0:T(8,128)(2,1)S(1)}, bf16[256,256]{1,0:T(8,128)(2,1)S(1)}, u32[]{:S(2)}, u32[]{:S(2)}) collective-permute-start(bf16[256,256]{1,0:T(8,128)(2,1)S(1)} %get-tuple-element.66.refs_2_), channel_id=1, source_target_pairs={{4,0},{8,4},{12,8},{14,12},{10,14},{6,10},{2,6},{0,2},{5,1},{9,5},... | collective-permute-start | bytes 393224 | tf_op jit(solution)/shard_map/ppermute | solution.py:335
  8.4 20.4 %collective-permute-start = (bf16[256,256]{1,0:T(8,128)(2,1)S(1)}, bf16[256,256]{1,0:T(8,128)(2,1)S(1)}, u32[]{:S(2)}, u32[]{:S(2)}) collective-permute-start(bf16[256,256]{1,0:T(8,128)(2,1)S(1)} %get-tuple-element.63.refs_0_), channel_id=1, source_target_pairs={{0,4},{4,8},{8,12},{12,14},{14,10},{10,6},{6,2},{2,0},{1,5},{5,9},... | collective-permute-start | bytes 393224 | tf_op jit(solution)/shard_map/ppermute | solution.py:335
  11.5 15.2 %collective-permute-start.5 = (bf16[272,256]{1,0:T(8,128)(2,1)S(1)}, bf16[272,256]{1,0:T(8,128)(2,1)S(1)}, u32[]{:S(2)}, u32[]{:S(2)}) collective-permute-start(bf16[272,256]{1,0:T(8,128)(2,1)S(1)} %get-tuple-element.67.refs_3_), channel_id=1, source_target_pairs={{4,0},{8,4},{12,8},{14,12},{10,14},{6,10},{2,6},{0,2},{5,1},{9,5},... | collective-permute-start | bytes 417800 | tf_op jit(solution)/shard_map/ppermute | solution.py:335
  13.5 14.7 %collective-permute-start.3 = (bf16[272,256]{1,0:T(8,128)(2,1)S(1)}, bf16[272,256]{1,0:T(8,128)(2,1)S(1)}, u32[]{:S(2)}, u32[]{:S(2)}) collective-permute-start(bf16[272,256]{1,0:T(8,128)(2,1)S(1)} %get-tuple-element.65.refs_1_), channel_id=1, source_target_pairs={{0,4},{4,8},{8,12},{12,14},{14,10},{10,6},{6,2},{2,0},{1,5},{5,9},... | collective-permute-start | bytes 417800 | tf_op jit(solution)/shard_map/ppermute | solution.py:335
  26.7 6.6 %collective-permute-start.9 = (bf16[272,256]{1,0:T(8,128)(2,1)S(1)}, bf16[272,256]{1,0:T(8,128)(2,1)S(1)}, u32[]{:S(2)}, u32[]{:S(2)}) collective-permute-start(bf16[272,256]{1,0:T(8,128)(2,1)S(1)} %collective-permute-done.5.refs_3_), channel_id=1, source_target_pairs={{4,0},{8,4},{12,8},{14,12},{10,14},{6,10},{2,6},{0,2},{5,1},{9,5},... | collective-permute-start | bytes 417800 | tf_op jit(solution)/shard_map/ppermute | solution.py:335
  28.2 7.3 %collective-permute-start.7 = (bf16[272,256]{1,0:T(8,128)(2,1)S(1)}, bf16[272,256]{1,0:T(8,128)(2,1)S(1)}, u32[]{:S(2)}, u32[]{:S(2)}) collective-permute-start(bf16[272,256]{1,0:T(8,128)(2,1)S(1)} %collective-permute-done.3.refs_1_), channel_id=1, source_target_pairs={{0,4},{4,8},{8,12},{12,14},{14,10},{10,6},{6,2},{2,0},{1,5},{5,9},... | collective-permute-start | bytes 417800 | tf_op jit(solution)/shard_map/ppermute | solution.py:335
  28.8 6.7 %collective-permute-start.8 = (bf16[256,256]{1,0:T(8,128)(2,1)S(1)}, bf16[256,256]{1,0:T(8,128)(2,1)S(1)}, u32[]{:S(2)}, u32[]{:S(2)}) collective-permute-start(bf16[256,256]{1,0:T(8,128)(2,1)S(1)} %collective-permute-done.4.refs_2_), channel_id=1, source_target_pairs={{4,0},{8,4},{12,8},{14,12},{10,14},{6,10},{2,6},{0,2},{5,1},{9,5},... | collective-permute-start | bytes 393224 | tf_op jit(solution)/shard_map/ppermute | solution.py:335
  33.4 7.5 %collective-permute-start.13 = (bf16[272,256]{1,0:T(8,128)(2,1)S(1)}, bf16[272,256]{1,0:T(8,128)(2,1)S(1)}, u32[]{:S(2)}, u32[]{:S(2)}) collective-permute-start(bf16[272,256]{1,0:T(8,128)(2,1)S(1)} %collective-permute-done.9.refs_3_), channel_id=1, source_target_pairs={{4,0},{8,4},{12,8},{14,12},{10,14},{6,10},{2,6},{0,2},{5,1},{9,5},... | collective-permute-start | bytes 417800 | tf_op jit(solution)/shard_map/ppermute | solution.py:335
  35.5 7.3 %collective-permute-start.11 = (bf16[272,256]{1,0:T(8,128)(2,1)S(1)}, bf16[272,256]{1,0:T(8,128)(2,1)S(1)}, u32[]{:S(2)}, u32[]{:S(2)}) collective-permute-start(bf16[272,256]{1,0:T(8,128)(2,1)S(1)} %collective-permute-done.7.refs_1_), channel_id=1, source_target_pairs={{0,4},{4,8},{8,12},{12,14},{14,10},{10,6},{6,2},{2,0},{1,5},{5,9},... | collective-permute-start | bytes 417800 | tf_op jit(solution)/shard_map/ppermute | solution.py:335
  35.5 7.4 %collective-permute-start.12 = (bf16[256,256]{1,0:T(8,128)(2,1)S(1)}, bf16[256,256]{1,0:T(8,128)(2,1)S(1)}, u32[]{:S(2)}, u32[]{:S(2)}) collective-permute-start(bf16[256,256]{1,0:T(8,128)(2,1)S(1)} %collective-permute-done.8.refs_2_), channel_id=1, source_target_pairs={{4,0},{8,4},{12,8},{14,12},{10,14},{6,10},{2,6},{0,2},{5,1},{9,5},... | collective-permute-start | bytes 393224 | tf_op jit(solution)/shard_map/ppermute | solution.py:335
  37.5 7.3 %collective-permute-start.6 = (bf16[256,256]{1,0:T(8,128)(2,1)S(1)}, bf16[256,256]{1,0:T(8,128)(2,1)S(1)}, u32[]{:S(2)}, u32[]{:S(2)}) collective-permute-start(bf16[256,256]{1,0:T(8,128)(2,1)S(1)} %collective-permute-done.2.refs_0_), channel_id=1, source_target_pairs={{0,4},{4,8},{8,12},{12,14},{14,10},{10,6},{6,2},{2,0},{1,5},{5,9},... | collective-permute-start | bytes 393224 | tf_op jit(solution)/shard_map/ppermute | solution.py:335
  40.8 6.6 %collective-permute-start.17 = (bf16[272,256]{1,0:T(8,128)(2,1)S(1)}, bf16[272,256]{1,0:T(8,128)(2,1)S(1)}, u32[]{:S(2)}, u32[]{:S(2)}) collective-permute-start(bf16[272,256]{1,0:T(8,128)(2,1)S(1)} %collective-permute-done.13.refs_3_), channel_id=1, source_target_pairs={{4,0},{8,4},{12,8},{14,12},{10,14},{6,10},{2,6},{0,2},{5,1},{9,5},... | collective-permute-start | bytes 417800 | tf_op jit(solution)/shard_map/ppermute | solution.py:335
  44.9 6.9 %collective-permute-start.10 = (bf16[256,256]{1,0:T(8,128)(2,1)S(1)}, bf16[256,256]{1,0:T(8,128)(2,1)S(1)}, u32[]{:S(2)}, u32[]{:S(2)}) collective-permute-start(bf16[256,256]{1,0:T(8,128)(2,1)S(1)} %collective-permute-done.6.refs_0_), channel_id=1, source_target_pairs={{0,4},{4,8},{8,12},{12,14},{14,10},{10,6},{6,2},{2,0},{1,5},{5,9},... | collective-permute-start | bytes 393224 | tf_op jit(solution)/shard_map/ppermute | solution.py:335
  47.5 7.1 %collective-permute-start.21 = (bf16[272,256]{1,0:T(8,128)(2,1)S(1)}, bf16[272,256]{1,0:T(8,128)(2,1)S(1)}, u32[]{:S(2)}, u32[]{:S(2)}) collective-permute-start(bf16[272,256]{1,0:T(8,128)(2,1)S(1)} %collective-permute-done.17.refs_3_), channel_id=1, source_target_pairs={{4,0},{8,4},{12,8},{14,12},{10,14},{6,10},{2,6},{0,2},{5,1},{9,5},... | collective-permute-start | bytes 417800 | tf_op jit(solution)/shard_map/ppermute | solution.py:335
  49.5 6.7 %collective-permute-start.19 = (bf16[272,256]{1,0:T(8,128)(2,1)S(1)}, bf16[272,256]{1,0:T(8,128)(2,1)S(1)}, u32[]{:S(2)}, u32[]{:S(2)}) collective-permute-start(bf16[272,256]{1,0:T(8,128)(2,1)S(1)} %collective-permute-done.15.refs_1_), channel_id=1, source_target_pairs={{0,4},{4,8},{8,12},{12,14},{14,10},{10,6},{6,2},{2,0},{1,5},{5,9},... | collective-permute-start | bytes 417800 | tf_op jit(solution)/shard_map/ppermute | solution.py:335
  49.5 7.1 %collective-permute-start.20 = (bf16[256,256]{1,0:T(8,128)(2,1)S(1)}, bf16[256,256]{1,0:T(8,128)(2,1)S(1)}, u32[]{:S(2)}, u32[]{:S(2)}) collective-permute-start(bf16[256,256]{1,0:T(8,128)(2,1)S(1)} %collective-permute-done.16.refs_2_), channel_id=1, source_target_pairs={{4,0},{8,4},{12,8},{14,12},{10,14},{6,10},{2,6},{0,2},{5,1},{9,5},... | collective-permute-start | bytes 393224 | tf_op jit(solution)/shard_map/ppermute | solution.py:335
  51.8 6.8 %collective-permute-start.14 = (bf16[256,256]{1,0:T(8,128)(2,1)S(1)}, bf16[256,256]{1,0:T(8,128)(2,1)S(1)}, u32[]{:S(2)}, u32[]{:S(2)}) collective-permute-start(bf16[256,256]{1,0:T(8,128)(2,1)S(1)} %collective-permute-done.10.refs_0_), channel_id=1, source_target_pairs={{0,4},{4,8},{8,12},{12,14},{14,10},{10,6},{6,2},{2,0},{1,5},{5,9},... | collective-permute-start | bytes 393224 | tf_op jit(solution)/shard_map/ppermute | solution.py:335
  54.6 6.7 %collective-permute-start.25 = (bf16[272,256]{1,0:T(8,128)(2,1)S(1)}, bf16[272,256]{1,0:T(8,128)(2,1)S(1)}, u32[]{:S(2)}, u32[]{:S(2)}) collective-permute-start(bf16[272,256]{1,0:T(8,128)(2,1)S(1)} %collective-permute-done.21.refs_3_), channel_id=1, source_target_pairs={{4,0},{8,4},{12,8},{14,12},{10,14},{6,10},{2,6},{0,2},{5,1},{9,5},... | collective-permute-start | bytes 417800 | tf_op jit(solution)/shard_map/ppermute | solution.py:335
  56.1 7.5 %collective-permute-start.23 = (bf16[272,256]{1,0:T(8,128)(2,1)S(1)}, bf16[272,256]{1,0:T(8,128)(2,1)S(1)}, u32[]{:S(2)}, u32[]{:S(2)}) collective-permute-start(bf16[272,256]{1,0:T(8,128)(2,1)S(1)} %collective-permute-done.19.refs_1_), channel_id=1, source_target_pairs={{0,4},{4,8},{8,12},{12,14},{14,10},{10,6},{6,2},{2,0},{1,5},{5,9},... | collective-permute-start | bytes 417800 | tf_op jit(solution)/shard_map/ppermute | solution.py:335
  56.7 7.0 %collective-permute-start.24 = (bf16[256,256]{1,0:T(8,128)(2,1)S(1)}, bf16[256,256]{1,0:T(8,128)(2,1)S(1)}, u32[]{:S(2)}, u32[]{:S(2)}) collective-permute-start(bf16[256,256]{1,0:T(8,128)(2,1)S(1)} %collective-permute-done.20.refs_2_), channel_id=1, source_target_pairs={{4,0},{8,4},{12,8},{14,12},{10,14},{6,10},{2,6},{0,2},{5,1},{9,5},... | collective-permute-start | bytes 393224 | tf_op jit(solution)/shard_map/ppermute | solution.py:335
  58.6 7.1 %collective-permute-start.18 = (bf16[256,256]{1,0:T(8,128)(2,1)S(1)}, bf16[256,256]{1,0:T(8,128)(2,1)S(1)}, u32[]{:S(2)}, u32[]{:S(2)}) collective-permute-start(bf16[256,256]{1,0:T(8,128)(2,1)S(1)} %collective-permute-done.14.refs_0_), channel_id=1, source_target_pairs={{0,4},{4,8},{8,12},{12,14},{14,10},{10,6},{6,2},{2,0},{1,5},{5,9},... | collective-permute-start | bytes 393224 | tf_op jit(solution)/shard_map/ppermute | solution.py:335
  61.3 9.4 %collective-permute-start.28 = (bf16[272,256]{1,0:T(8,128)(2,1)S(1)}, bf16[272,256]{1,0:T(8,128)(2,1)S(1)}, u32[]{:S(2)}, u32[]{:S(2)}) collective-permute-start(bf16[272,256]{1,0:T(8,128)(2,1)S(1)} %collective-permute-done.25.refs_3_), channel_id=1, source_target_pairs={{4,0},{8,4},{12,8},{14,12},{10,14},{6,10},{2,6},{0,2},{5,1},{9,5},... | collective-permute-start | bytes 417800 | tf_op jit(solution)/shard_map/ppermute | solution.py:335
  63.6 7.0 %collective-permute-start.26 = (bf16[272,256]{1,0:T(8,128)(2,1)S(1)}, bf16[272,256]{1,0:T(8,128)(2,1)S(1)}, u32[]{:S(2)}, u32[]{:S(2)}) collective-permute-start(bf16[272,256]{1,0:T(8,128)(2,1)S(1)} %collective-permute-done.23.refs_1_), channel_id=1, source_target_pairs={{0,4},{4,8},{8,12},{12,14},{14,10},{10,6},{6,2},{2,0},{1,5},{5,9},... | collective-permute-start | bytes 417800 | tf_op jit(solution)/shard_map/ppermute | solution.py:335
  78.0 7.1 %collective-permute-start.29 = (bf16[4,4,6,64,128]{4,3,2,1,0:T(8,128)(2,1)S(1)}, bf16[4,4,6,64,128]{4,3,2,1,0:T(8,128)(2,1)S(1)}, u32[]{:S(2)}, u32[]{:S(2)}) collective-permute-start(bf16[4,4,6,64,128]{4,3,2,1,0:T(8,128)(2,1)S(1)} %sent_half.3), channel_id=1, source_target_pairs={{0,1},{1,0},{2,3},{3,2},{4,5},{5,4},{6,7},{7,6},{8,9},{9,8},{10,11... | collective-permute-start | bytes 4718600 | tf_op jit(solution)/shard_map/ppermute | solution.py:350
  (16 other events, 53.7 us)

commit v5 on v0

v5 whole, which is shorter than its diff:
```python
import functools
import jax
import jax.numpy as jnp
from jax import lax
from jax.experimental import pallas as pl
from jax.experimental.pallas import tpu as pltpu
from jax.sharding import PartitionSpec as P

GROUPS = 2
LATE = 3
SMEM = pl.BlockSpec(memory_space=pltpu.SMEM)
VMEM = pl.BlockSpec(memory_space=pltpu.VMEM)
ANYWHERE = pl.BlockSpec(memory_space=pl.ANY)
PARAMS = pltpu.CompilerParams(vmem_limit_bytes=16 << 20)


def lag_tables(bins, basis_count, overall, lanes):
    log_decay = -(8.0 ** jnp.arange(basis_count, dtype=jnp.float32)) / (2.0 * overall)
    t = jnp.arange(bins, dtype=jnp.float32)
    lag = t[:, None] - 1.0 - t[None, :]
    weights = jnp.where(
        lag[None] >= 0.0,
        (1.0 - jnp.exp(log_decay))[:, None, None]
        * jnp.exp(jnp.maximum(lag, 0.0)[None] * log_decay[:, None, None]),
        jnp.float32(0.0),
    )
    power = jnp.exp(t[None, :, None] * log_decay[:, None, None])
    return weights.astype(jnp.bfloat16), jnp.broadcast_to(power, (basis_count, bins, lanes))


def impact_kernel(
    basis, tile, overall, counts_hbm, mark_hbm, up_ref, down_ref, ends_ref, counts, mark, sems
):
    bins, types = counts.shape
    parts = sems.shape[1]
    lanes = types // parts
    copies = []
    for j in range(parts):
        at = pl.ds(j * lanes, lanes)
        copies.append(
            (
                pltpu.make_async_copy(counts_hbm.at[:, at], counts.at[:, at], sems.at[0, j]),
                pltpu.make_async_copy(mark_hbm.at[:, at], mark.at[:, at], sems.at[1, j]),
            )
        )
        for copy in copies[-1]:
            copy.start()
    back = (bins - 1 - lax.broadcasted_iota(jnp.int32, (bins, tile), 0)).astype(jnp.float32)
    gains = []
    for b in range(basis):
        rate = (8.0**b) / (2.0 * overall)
        gains.append((1.0 - jnp.exp(jnp.full((bins, tile), -rate, jnp.float32))) * jnp.exp(-rate * back))
    half = types // tile // 2
    for j in range(parts):
        for copy in copies[j]:
            copy.wait()
        for block in range(j * lanes // tile, (j + 1) * lanes // tile):
            at = slice(block * tile, (block + 1) * tile)
            impact = counts[:, at].astype(jnp.float32) * mark[:, at].astype(jnp.float32)
            impact = impact.astype(jnp.bfloat16)
            out_ref = up_ref if block < half else down_ref
            out_ref[block % half * bins : (block % half + 1) * bins] = impact
            impact = impact.astype(jnp.float32)
            for b in range(basis):
                ends_ref[b : b + 1, at] = jnp.sum(impact * gains[b], axis=0, keepdims=True)
    rest = up_ref.shape[0] - half * bins
    for out_ref in (up_ref, down_ref):
        out_ref[half * bins :] = jnp.zeros((rest, tile), jnp.bfloat16)


def impact_chunks(counts, mark, dims, overall):
    basis, _, _, tile = dims
    bins, types = counts.shape
    half = types // tile // 2
    carry = -(-half * basis // 16) * 16
    chunk = jax.ShapeDtypeStruct((half * bins + carry, tile), jnp.bfloat16)
    return pl.pallas_call(
        functools.partial(impact_kernel, basis, tile, overall),
        in_specs=[ANYWHERE, ANYWHERE],
        out_specs=[VMEM, VMEM, VMEM],
        out_shape=[chunk, chunk, jax.ShapeDtypeStruct((basis, types), jnp.float32)],
        scratch_shapes=[
            pltpu.VMEM((bins, types), jnp.int32),
            pltpu.VMEM((bins, types), jnp.bfloat16),
            pltpu.SemaphoreType.DMA((2, 2)),
        ],
        compiler_params=pltpu.CompilerParams(vmem_limit_bytes=56 << 20),
        name="impact_chunks",
    )(counts, mark)


def carry_kernel(basis, bins, enter_ref, _, __, up_ref, down_ref, held, sems):
    rows, tile = up_ref.shape
    half = enter_ref.shape[1] // tile // 2
    rest = rows - half * bins
    copies = []
    for d, out_ref in enumerate((up_ref, down_ref)):
        carry = [
            enter_ref[:, (d * half + q) * tile : (d * half + q + 1) * tile] for q in range(half)
        ]
        if rest > half * basis:
            carry.append(jnp.zeros((rest - half * basis, tile), jnp.float32))
        held[d] = jnp.concatenate(carry, axis=0).astype(jnp.bfloat16)
        copies.append(
            pltpu.make_async_copy(held.at[d], out_ref.at[pl.ds(half * bins, rest)], sems.at[d])
        )
        copies[-1].start()
    for copy in copies:
        copy.wait()


def add_carry(enter, up, down, basis, bins):
    chunk = jax.ShapeDtypeStruct(up.shape, up.dtype)
    rows, tile = up.shape
    return pl.pallas_call(
        functools.partial(carry_kernel, basis, bins),
        in_specs=[VMEM, ANYWHERE, ANYWHERE],
        out_specs=[ANYWHERE, ANYWHERE],
        out_shape=[chunk, chunk],
        scratch_shapes=[
            pltpu.VMEM((2, rows % bins, tile), jnp.bfloat16),
            pltpu.SemaphoreType.DMA((2,)),
        ],
        input_output_aliases={1: 0, 2: 1},
        compiler_params=PARAMS,
        name="carry_rows",
    )(enter, up, down)


def ring_place(index, n):
    return jnp.where(index % 2 == 0, index // 2, n - 1 - index // 2)


def code_of(row, slot, block):
    return (row * 256 + slot) * 256 + block


def plan_kernel(shape, place_ref, col_ref, fill_ref, plan_ref):
    brows, slots, width, n, most = shape
    own = place_ref[0]
    entries = brows * slots
    tail = n * (most + 1)
    plan_ref[tail] = place_ref[1]
    for step in range(n):
        plan_ref[step * (most + 1)] = 0

    @pl.loop(0, brows)
    def _(row):
        fill = fill_ref[own * brows + row]
        plan_ref[tail + 1 + row] = fill

        @pl.loop(0, fill)
        def _(slot):
            column = col_ref[own * entries + row * slots + slot]
            source = lax.div(column, width)
            block = lax.rem(column, width)
            ahead = ring_place(source, n) - ring_place(own, n)
            ahead = jnp.where(block < width // 2, -ahead, ahead)
            ahead = jnp.where(ahead < 0, ahead + n, ahead)
            base = ahead * (most + 1)
            count = plan_ref[base] + 1
            plan_ref[base] = count
            plan_ref[base + count] = code_of(row, slot, block)

    for step in range(n):
        base = step * (most + 1)
        count = plan_ref[base]

        @pl.when(lax.rem(count, 2) == 1)
        def _(base=base, count=count):
            plan_ref[base + count + 1] = code_of(brows, 0, 0)


def make_plan(place, cols, fill, dims, width, n):
    _, brows, slots, _ = dims
    most = 2 * max(2, brows * slots // n)
    return pl.pallas_call(
        functools.partial(plan_kernel, (brows, slots, width, n, most)),
        in_specs=[SMEM] * 3,
        out_specs=SMEM,
        out_shape=jax.ShapeDtypeStruct((n * (most + 1) + 1 + brows,), jnp.int32),
        name="plan",
    )(place, cols, fill)


def start_kernel(tile, counts_ref, base_ref, total_ref):
    for row in range(total_ref.shape[0] - 1):
        at = slice(row * tile, (row + 1) * tile)
        total_ref[row] = (base_ref[:, at] - counts_ref[:, at].astype(jnp.float32)).T
    total_ref[total_ref.shape[0] - 1] = jnp.zeros(total_ref.shape[1:], jnp.float32)


def start_total(counts, base_rate, dims):
    _, brows, _, tile = dims
    return pl.pallas_call(
        functools.partial(start_kernel, tile),
        in_specs=[VMEM, VMEM],
        out_specs=VMEM,
        out_shape=jax.ShapeDtypeStruct((brows + 1, tile, counts.shape[0]), jnp.float32),
        compiler_params=PARAMS,
        name="base_less_counts",
    )(counts, base_rate)


def step_kernel(dims, n, step, plan_ref, up_ref, down_ref, lag_ref, power_ref, excite_ref, *refs):
    basis, brows, slots, tile = dims
    total_in, states_ref, total_ref, built_ref, impact, carry, held, sems = refs[-8:]
    bins = lag_ref.shape[1]
    half = impact.shape[0] // 2
    most = (plan_ref.shape[0] - 1 - brows) // n - 1
    built_ref[...] = jnp.zeros_like(built_ref)
    total_ref[...] = total_in[...]
    pairs = (plan_ref[step * (most + 1)] + 1) // 2

    def entry_at(place):
        code = plan_ref[step * (most + 1) + 1 + place]
        return code >> 16, (code >> 8) & 255, code & 255

    def copy_at(place):
        row, slot, _ = entry_at(place)
        return pltpu.make_async_copy(
            held.at[place], states_ref.at[row * slots + slot], sems.at[place]
        )

    for d, chunk in enumerate((up_ref, down_ref)):
        rows = chunk[half * bins :].astype(jnp.float32)
        for q in range(half):
            impact[d * half + q] = chunk[q * bins : (q + 1) * bins]
            carry[d * half + q, :basis] = rows[q * basis : (q + 1) * basis]

    @pl.loop(0, pairs)
    def _(k):
        found = [entry_at(2 * k + i) for i in range(2)]
        both = jnp.concatenate([impact[block] for _, _, block in found], axis=1)
        enter = [carry[block] for _, _, block in found]
        built = [[], []]
        for b in range(basis):
            state = jnp.dot(lag_ref[b], both, preferred_element_type=jnp.float32)
            for i in range(2):
                built[i].append(
                    (
                        state[:, i * tile : (i + 1) * tile] + power_ref[b] * enter[i][b : b + 1]
                    ).astype(jnp.bfloat16)
                )
        for i, (row, slot, _) in enumerate(found):
            state = jnp.concatenate(built[i], axis=1)
            held[2 * k + i] = state
            copy_at(2 * k + i).start()
            inside = jnp.minimum(row, brows - 1)
            weight = jnp.concatenate([excite_ref[b, inside, slot] for b in range(basis)], axis=1)
            total_ref[row] += lax.dot_general(
                weight, state, (((1,), (1,)), ((), ())), preferred_element_type=jnp.float32
            )

    @pl.loop(0, 2 * pairs)
    def _(place):
        copy_at(place).wait()


def take_step(step, plan, chunks, lag, power, excite, states, total, dims, n):
    basis, brows, slots, tile = dims
    bins = lag.shape[1]
    half = chunks[0].shape[0] // bins
    most = (plan.shape[0] - 1 - brows) // n - 1
    given = [total] if states is None else [states, total]
    return pl.pallas_call(
        functools.partial(step_kernel, dims, n, step),
        in_specs=[SMEM] + [VMEM] * 5 + [ANYWHERE] * (len(given) - 1) + [VMEM],
        out_specs=[ANYWHERE, VMEM, VMEM],
        out_shape=[
            jax.ShapeDtypeStruct((brows * slots + 1, bins, basis * tile), jnp.bfloat16),
            jax.ShapeDtypeStruct(total.shape, total.dtype),
            jax.ShapeDtypeStruct((8, tile), jnp.float32),
        ],
        scratch_shapes=[
            pltpu.VMEM((2 * half, bins, tile), jnp.bfloat16),
            pltpu.VMEM((2 * half, 8, tile), jnp.float32),
            pltpu.VMEM((most, bins, basis * tile), jnp.bfloat16),
            pltpu.SemaphoreType.DMA((most,)),
        ],
        input_output_aliases={} if states is None else {6: 0},
        compiler_params=PARAMS,
        cost_estimate=pl.CostEstimate(
            flops=8 * basis * bins * bins * tile * 4,
            bytes_accessed=4 * 1024 * 1024,
            transcendentals=0,
        ),
        name="ring_step",
    )(plan, *chunks, lag, power, excite, *given)


def products(turned_ref, states_ref, plan_ref, rows, dims, put):
    basis, brows, slots, tile = dims
    tail = plan_ref.shape[0] - 1 - brows
    for r, row in enumerate(rows):
        fill = plan_ref[tail + 1 + row]
        for s in range(slots):
            grad = jnp.dot(
                turned_ref[row], states_ref[row * slots + s], preferred_element_type=jnp.float32
            )
            grad = jnp.where(s < fill, grad, jnp.zeros_like(grad))
            for b in range(basis):
                put(b, r, s, grad[:, b * tile : (b + 1) * tile])


def rows_of(group, dims):
    count = dims[1] // GROUPS
    return range(group * count, (group + 1) * count)


def halves_kernel(dims, overall, plan_ref, total_ref, states_ref, out_ref, *refs):
    _, brows, _, tile = dims
    sent_ref, kept_ref, rate_sent_ref, rate_kept_ref = refs
    half = plan_ref[plan_ref.shape[0] - 1 - brows]
    part = tile // 2
    rates = []
    for row in range(brows):
        weighted = (2.0 / overall) * total_ref[row]
        rates.append(
            lax.dot_general(
                jnp.ones((8, weighted.shape[1]), jnp.float32),
                weighted,
                (((1,), (1,)), ((), ())),
                precision=lax.Precision.HIGHEST,
                preferred_element_type=jnp.float32,
            )[:1]
        )
        weighted = weighted.astype(jnp.bfloat16)
        upper, lower = weighted[:part], weighted[part:]
        kept_ref[row] = jnp.where(half == 0, upper, lower)
        sent_ref[row] = jnp.where(half == 0, lower, upper)
    first_half = jnp.concatenate(rates[: brows // 2], axis=0)
    second_half = jnp.concatenate(rates[brows // 2 :], axis=0)
    rate_kept_ref[...] = jnp.where(half == 0, first_half, second_half)
    rate_sent_ref[...] = jnp.where(half == 0, second_half, first_half)
    store_kernel(dims, 0, plan_ref, sent_ref, states_ref, out_ref)


def store_kernel(dims, group, plan_ref, turned_ref, states_ref, out_ref):
    def put(b, r, s, grad):
        out_ref[b, r, s] = grad.astype(out_ref.dtype)

    products(turned_ref, states_ref, plan_ref, rows_of(group, dims), dims, put)


def group_shape(dims, dtype):
    basis, brows, slots, tile = dims
    return jax.ShapeDtypeStruct((basis, brows // GROUPS, slots, tile // 2, tile), dtype)


def halves(plan, total, states, dims, overall):
    _, brows, _, tile = dims
    turned = jax.ShapeDtypeStruct((brows, tile // 2, total.shape[2]), jnp.bfloat16)
    rate = jax.ShapeDtypeStruct((brows // 2, tile), jnp.float32)
    return pl.pallas_call(
        functools.partial(halves_kernel, dims, overall),
        in_specs=[SMEM, VMEM, VMEM],
        out_specs=[VMEM] * 5,
        out_shape=[group_shape(dims, jnp.bfloat16), turned, turned, rate, rate],
        compiler_params=PARAMS,
        name="weighted_halves",
    )(plan, total, states)


def store_products(group, plan, turned, states, dims, dtype):
    return pl.pallas_call(
        functools.partial(store_kernel, dims, group),
        in_specs=[SMEM, VMEM, VMEM],
        out_specs=VMEM,
        out_shape=group_shape(dims, dtype),
        compiler_params=PARAMS,
        name="products",
    )(plan, turned, states)


def out_copies(dims, group, r, held, out_ref, sems):
    row = rows_of(group, dims)[r]
    return [
        pltpu.make_async_copy(held.at[b, r], out_ref.at[b, row], sems.at[b, r])
        for b in range(dims[0])
    ]


def kept_kernel(dims, group, plan_ref, turned_ref, states_ref, got_ref, out_ref, held, sems):
    copies = []
    for r, row in enumerate(rows_of(group, dims)):

        def put(b, _, s, grad, r=r):
            held[b, r, s] = (grad + got_ref[b, r, s].astype(jnp.float32)).astype(jnp.bfloat16)

        products(turned_ref, states_ref, plan_ref, [row], dims, put)
        for copy in out_copies(dims, group, r, held, out_ref, sems):
            copy.start()
            copies.append(copy)
    for copy in copies:
        copy.wait()


def add_kernel(
    dims, group, own_ref, got_ref, rate_ref, rate_got_ref, _, out_ref, rate_out_ref, held, sems
):
    basis, brows, _, _ = dims
    rate_out_ref[...] = rate_ref[...] + rate_got_ref[...]
    copies = []
    for r in range(brows // GROUPS):
        for b in range(basis):
            held[b, r] = (own_ref[b, r] + got_ref[b, r].astype(jnp.float32)).astype(jnp.bfloat16)
        for copy in out_copies(dims, group, r, held, out_ref, sems):
            copy.start()
            copies.append(copy)
    for copy in copies:
        copy.wait()


def finish(dims, plan, turned, states, own, got, rate, rate_got):
    basis, brows, slots, tile = dims
    whole = jax.ShapeDtypeStruct((basis, brows, slots, tile // 2, tile), jnp.bfloat16)
    scratch = [
        pltpu.VMEM(group_shape(dims, jnp.bfloat16).shape, jnp.bfloat16),
        pltpu.SemaphoreType.DMA((basis, brows // GROUPS)),
    ]
    grad = pl.pallas_call(
        functools.partial(kept_kernel, dims, 0),
        in_specs=[SMEM, VMEM, VMEM, VMEM],
        out_specs=ANYWHERE,
        out_shape=whole,
        scratch_shapes=scratch,
        compiler_params=PARAMS,
        name="kept_half",
    )(plan, turned, states, got[0])
    return pl.pallas_call(
        functools.partial(add_kernel, dims, 1),
        in_specs=[VMEM] * 4 + [ANYWHERE],
        out_specs=[ANYWHERE, VMEM],
        out_shape=[whole, jax.ShapeDtypeStruct(rate.shape, rate.dtype)],
        scratch_shapes=scratch,
        input_output_aliases={4: 0},
        compiler_params=PARAMS,
        name="add_received",
    )(own, got[1], rate, rate_got, grad)


def shards(counts, mark_value, base_rate, excite, block_col, row_fill):
    dims = excite.shape[:4]
    basis, _, _, tile = dims
    bins = counts.shape[0]
    overall = bins * lax.axis_size("tm")
    n = lax.axis_size("types")
    place = jnp.stack([lax.axis_index("types"), lax.axis_index("tm")]).astype(jnp.int32)
    order = list(range(0, n, 2)) + list(range(1, n, 2))[::-1]
    up = [(order[i], order[(i + 1) % n]) for i in range(n)]
    down = [(b, a) for a, b in up]
    swap = [(0, 1), (1, 0)]

    *chunks, ends = impact_chunks(counts, mark_value, dims, overall)
    enter = lax.ppermute(ends, "tm", [(0, 1)])
    chunks = add_carry(enter, *chunks, basis, bins)
    lag, power = lag_tables(bins, basis, overall, tile)
    plan = make_plan(place, block_col.reshape(-1), row_fill, dims, counts.shape[1] // tile, n)
    total = start_total(counts, base_rate.reshape(1, -1), dims)
    states = None
    built = []
    for step in range(n):
        ahead = None
        if step < n - 1:
            if step >= LATE - 1:
                chunks = [
                    lax.optimization_barrier((chunk, built[step - LATE + 1]))[0] for chunk in chunks
                ]
            ahead = [lax.ppermute(chunks[0], "types", up), lax.ppermute(chunks[1], "types", down)]
        states, total, done = take_step(
            step, plan, chunks, lag, power, excite, states, total, dims, n
        )
        built.append(done)
        chunks = ahead
    out, sent, kept, rate_sent, rate_kept = halves(plan, total, states, dims, overall)
    got = [lax.ppermute(out, "tm", swap)]
    rate_got = lax.ppermute(rate_sent, "tm", swap)
    got.append(
        lax.ppermute(store_products(1, plan, sent, states, dims, jnp.bfloat16), "tm", swap)
    )
    own = store_products(1, plan, kept, states, dims, jnp.float32)
    grad, rate = finish(dims, plan, kept, states, own, got, rate_kept, rate_got)
    return grad, rate.reshape(-1)


def solution(mesh):
    return jax.shard_map(
        shards,
        mesh=mesh,
        in_specs=(
            P(("parts", "tm"), "types"),
            P(("parts", "tm"), "types"),
            P("types"),
            P(None, "types", None, None, None),
            P(),
            P(),
        ),
        out_specs=(P("parts", "types", None, "tm", None), P(("parts", "types", "tm"))),
        check_vma=False,
    )
```

time: 444 us -> 83.7 us (0.19)
  waiting for transfers between devices: 282 us -> 11.1 us
  local copies, waits for them, and re-layouts: 97.9 us -> 4.4 us
  Pallas kernels: 0 us -> 45.8 us
  matrix products: 21.1 us -> 0 us
  between operations: 14.9 us -> 1.07 us
  starting transfers between devices: 7.34 us -> 19.1 us
  other arithmetic: 12.9 us -> 1.24 us
  blocking collectives: 6.22 us -> 0 us
    all_to_all x1 -> x0, waiting for transfers between devices: 273 us -> none  [shards(): lax.all_to_all(outgoing, 'types', split_axis=2, concat_axis=2, tiled=True)]
    pallas_call x0 -> x17, Pallas kernels: none -> 45.8 us  [the longest x8 29.3 us: take_step(): pl.pallas_call(functools.partial(step_kernel, dims, n, step), in_specs=[S...]
    gather x4 -> x0, local copies, waits for them, and re-layouts: 45.4 us -> none  [the longest x2 23 us: shards(): jnp.take(state_bf, local_block, axis=2)]
    dot_general x3 -> x0, matrix products: 21.1 us -> none  [the longest x1 10.5 us: shards(): jnp.einsum('tip,btisq->bispq', weighted_bf, stacked, preferred_element_ty...]
    ppermute x0 -> x18, starting transfers between devices: none -> 19.1 us  [the longest x7 14.4 us: shards(): lax.ppermute(chunks[0], 'types', up)]
    reshape x4 -> x1, local copies, waits for them, and re-layouts: 17.1 us -> 0.72 us  [shards(): block_col.reshape(-1)]
    ppermute x0 -> x18, waiting for transfers between devices: none -> 11.1 us  [the longest x7 9.84 us: shards(): lax.ppermute(chunks[0], 'types', up)]
    all_to_all x1 -> x0, local copies, waits for them, and re-layouts: 10.6 us -> none  [shards(): lax.all_to_all(outgoing, 'types', split_axis=2, concat_axis=2, tiled=True)]
  transfers between devices with their start and end apart: 2 -> 18, of which waited for: 2 -> 7; matrix products, arithmetic and copies ran while one was open for 0% -> 3% of each run, Pallas kernels for 0% -> 41%
where the time goes in v5:
time: 83.7 us; the launch traced here: 82.7 us
  Pallas kernels  45.8 us (55%)
  starting transfers between devices  19.1 us (23%)
  waiting for transfers between devices  11.1 us (13%)
  local copies, waits for them, and re-layouts  4.4 us (5%)
  other arithmetic  1.24 us (1%)
  between operations  1.07 us (1%)
    pallas_call x8, Pallas kernels, take_step(): pl.pallas_call(functools.partial(step_kernel, dims, n, step), in_specs=[S...  29.3 us
    ppermute x7, starting transfers between devices, shards(): lax.ppermute(chunks[0], 'types', up)  14.4 us
    ppermute x7, waiting for transfers between devices, shards(): lax.ppermute(chunks[0], 'types', up)  9.84 us
    pallas_call x2, Pallas kernels, store_products(): pl.pallas_call(functools.partial(store_kernel, dims, group), in_specs=[SM...  3.49 us
    unnamed x11, local copies, waits for them, and re-layouts  3.49 us
    pallas_call x1, Pallas kernels, finish(): pl.pallas_call(functools.partial(kept_kernel, dims, 0), in_specs=[SMEM, V...  2.7 us
    pallas_call x1, Pallas kernels, halves(): pl.pallas_call(functools.partial(halves_kernel, dims, overall), in_specs=...  2.59 us
    pallas_call x1, Pallas kernels, impact_chunks(): pl.pallas_call(functools.partial(impact_kernel, basis, tile, overall), in...  2.56 us
  transfers between devices with their start and end apart: 18, of which 7 were waited for; matrix products, arithmetic and copies ran while one was open for 3% of the time, Pallas kernels for 41%

profile of v5, /device:TPU:0, one launch (start us, length us, event | category | flops | bytes accessed | tf_op | source)
XLA Modules:
  0.0 82.7 jit_solution(11423385569172044658)
XLA Ops:
  0.7 2.6 %impact_chunks.1 = (bf16[1040,128]{1,0:T(8,128)(2,1)}, bf16[1040,128]{1,0:T(8,128)(2,1)}, f32[4,1024]{1,0:T(4,128)}) custom-call(s32[256,1024]{1,0:T(8,128)} %counts_ref.1, bf16[256,1024]{1,0:T(8,128)(2,1)} %mark_hbm.1), custom_call_target="tpu_custom_call" | custom-call | tf_op jit(solution)/shard_map/impact_chunks/pallas_call | solution.py:77
  3.2 2.4 %collective-permute-start = (f32[4,1024]{1,0:T(4,128)}, f32[4,1024]{1,0:T(4,128)S(1)}, u32[]{:S(2)}, u32[]{:S(2)}) collective-permute-start(f32[4,1024]{1,0:T(4,128)} %get-tuple-element.45), channel_id=1, source_target_pairs={{0,1},{2,3},{4,5},{6,7},{8,9},{10,11},{12,13},{14,15},{16,17},{18,... | collective-permute-start | bytes 49160 | tf_op jit(solution)/shard_map/ppermute | solution.py:456
  7.2 2.5 %collective-permute-start.1 = (bf16[1040,128]{1,0:T(8,128)(2,1)}, bf16[1040,128]{1,0:T(8,128)(2,1)S(1)}, u32[]{:S(2)}, u32[]{:S(2)}) collective-permute-start(bf16[1040,128]{1,0:T(8,128)(2,1)} %get-tuple-element.48.up_ref), channel_id=1, source_target_pairs={{0,4},{4,8},{8,12},{12,14},{14,10},{10,6},{6,2},{2,0},{1,5},{5,9},... | collective-permute-start | bytes 798728 | tf_op jit(solution)/shard_map/ppermute | solution.py:470
  11.5 2.2 %plan.1.plan_ref = s32[113]{0:T(128)} custom-call(s32[2]{0:T(128)} %pad_add_fusion.place_ref, s32[384]{0:T(512)} %reshape.90.col_ref, s32[64]{0:T(128)} %fill_ref.1), custom_call_target="tpu_custom_call" | custom-call | tf_op jit(solution)/shard_map/plan/pallas_call | solution.py:177
  14.1 2.7 %collective-permute-done.1.up_ref = bf16[1040,128]{1,0:T(8,128)(2,1)S(1)} collective-permute-done((bf16[1040,128]{1,0:T(8,128)(2,1)}, bf16[1040,128]{1,0:T(8,128)(2,1)S(1)}, u32[]{:S(2)}, u32[]{:S(2)}) %collective-permute-start.1) | collective-permute-done | bytes 266272 | tf_op jit(solution)/shard_map/ppermute | solution.py:470
  16.8 1.8 %collective-permute-start.2 = (bf16[1040,128]{1,0:T(8,128)(2,1)S(1)}, bf16[1040,128]{1,0:T(8,128)(2,1)S(1)}, u32[]{:S(2)}, u32[]{:S(2)}) collective-permute-start(bf16[1040,128]{1,0:T(8,128)(2,1)S(1)} %collective-permute-done.1.up_ref), channel_id=1, source_target_pairs={{0,4},{4,8},{8,12},{12,14},{14,10},{10,6},{6,2},{2,0},{1,5},{5,9},... | collective-permute-start | bytes 798728 | tf_op jit(solution)/shard_map/ppermute | solution.py:470
  19.1 2.8 %copy-done = bf16[4,8,6,128,128]{4,3,2,1,0:T(8,128)(2,1)S(1)} copy-done((bf16[4,8,6,128,128]{4,3,2,1,0:T(8,128)(2,1)S(1)}, bf16[4,8,6,128,128]{4,3,2,1,0:T(8,128)(2,1)}, u32[]{:S(2)}) %copy-start) | copy-done | bytes 6291480
  22.5 3.7 %ring_step.8 = (bf16[49,256,512]{2,1,0:T(8,128)(2,1)S(1)}, f32[9,128,256]{2,1,0:T(8,128)S(1)}, f32[8,128]{1,0:T(8,128)}) custom-call(s32[113]{0:T(128)S(1)} %copy-done.2, bf16[1040,128]{1,0:T(8,128)(2,1)} %get-tuple-element.48.up_ref, bf16[1040,128]{1,0:T(8,128)(2,1)} %get-tuple-element.49.down_ref, bf16[4,256,256]{2,1,0:T(8,128)(2,1)S(1)} %select_convert_fusion.lag_ref, ...), custom_call_target="tpu_custom_call" | custom-call | flops 1073741824 | bytes 4194304 | tf_op jit(solution)/shard_map/ring_step/pallas_call | solution.py:266
  28.3 3.2 %ring_step.9 = (bf16[49,256,512]{2,1,0:T(8,128)(2,1)S(1)}, f32[9,128,256]{2,1,0:T(8,128)S(1)}, f32[8,128]{1,0:T(8,128)}) custom-call(s32[113]{0:T(128)S(1)} %copy-done.2, bf16[1040,128]{1,0:T(8,128)(2,1)S(1)} %collective-permute-done.1.up_ref, bf16[1040,128]{1,0:T(8,128)(2,1)S(1)} %collective-permute-done.4.down_ref, ...), custom_call_target="tpu_custom_call", output_to_operand_aliasing={{0}: (6, {})} | custom-call | flops 1073741824 | bytes 4194304 | tf_op jit(solution)/shard_map/ring_step/pallas_call | solution.py:266
  31.5 2.2 %collective-permute-done.3.up_ref = bf16[1040,128]{1,0:T(8,128)(2,1)S(1)} collective-permute-done((bf16[1040,128]{1,0:T(8,128)(2,1)S(1)}, bf16[1040,128]{1,0:T(8,128)(2,1)S(1)}, u32[]{:S(2)}, u32[]{:S(2)}) %collective-permute-start.3) | collective-permute-done | bytes 266272 | tf_op jit(solution)/shard_map/ppermute | solution.py:470
  36.1 3.2 %ring_step.10 = (bf16[49,256,512]{2,1,0:T(8,128)(2,1)S(1)}, f32[9,128,256]{2,1,0:T(8,128)S(1)}, f32[8,128]{1,0:T(8,128)}) custom-call(s32[113]{0:T(128)S(1)} %copy-done.2, bf16[1040,128]{1,0:T(8,128)(2,1)S(1)} %collective-permute-done.2.up_ref, bf16[1040,128]{1,0:T(8,128)(2,1)S(1)} %collective-permute-done.6.down_ref, ...), custom_call_target="tpu_custom_call", output_to_operand_aliasing={{0}: (6, {})} | custom-call | flops 1073741824 | bytes 4194304 | tf_op jit(solution)/shard_map/ring_step/pallas_call | solution.py:266
  41.0 2.1 %collective-permute-start.7 = (bf16[1040,128]{1,0:T(8,128)(2,1)S(1)}, bf16[1040,128]{1,0:T(8,128)(2,1)S(1)}, u32[]{:S(2)}, u32[]{:S(2)}) collective-permute-start(bf16[1040,128]{1,0:T(8,128)(2,1)S(1)} %collective-permute-done.5.up_ref), channel_id=1, source_target_pairs={{0,4},{4,8},{8,12},{12,14},{14,10},{10,6},{6,2},{2,0},{1,5},{5,9},... | collective-permute-start | bytes 798728 | tf_op jit(solution)/shard_map/ppermute | solution.py:470
  43.0 3.2 %ring_step.11 = (bf16[49,256,512]{2,1,0:T(8,128)(2,1)S(1)}, f32[9,128,256]{2,1,0:T(8,128)S(1)}, f32[8,128]{1,0:T(8,128)}) custom-call(s32[113]{0:T(128)S(1)} %copy-done.2, bf16[1040,128]{1,0:T(8,128)(2,1)S(1)} %collective-permute-done.3.up_ref, bf16[1040,128]{1,0:T(8,128)(2,1)S(1)} %collective-permute-done.8.down_ref, ...), custom_call_target="tpu_custom_call", output_to_operand_aliasing={{0}: (6, {})} | custom-call | flops 1073741824 | bytes 4194304 | tf_op jit(solution)/shard_map/ring_step/pallas_call | solution.py:266
  48.0 2.2 %collective-permute-start.9 = (bf16[1040,128]{1,0:T(8,128)(2,1)S(1)}, bf16[1040,128]{1,0:T(8,128)(2,1)S(1)}, u32[]{:S(2)}, u32[]{:S(2)}) collective-permute-start(bf16[1040,128]{1,0:T(8,128)(2,1)S(1)} %collective-permute-done.7.up_ref), channel_id=1, source_target_pairs={{0,4},{4,8},{8,12},{12,14},{14,10},{10,6},{6,2},{2,0},{1,5},{5,9},... | collective-permute-start | bytes 798728 | tf_op jit(solution)/shard_map/ppermute | solution.py:470
  50.2 4.2 %ring_step.12 = (bf16[49,256,512]{2,1,0:T(8,128)(2,1)S(1)}, f32[9,128,256]{2,1,0:T(8,128)S(1)}, f32[8,128]{1,0:T(8,128)}) custom-call(s32[113]{0:T(128)S(1)} %copy-done.2, bf16[1040,128]{1,0:T(8,128)(2,1)S(1)} %collective-permute-done.5.up_ref, bf16[1040,128]{1,0:T(8,128)(2,1)S(1)} %collective-permute-done.10.down_ref, ...), custom_call_target="tpu_custom_call", output_to_operand_aliasing={{0}: (6, {})} | custom-call | flops 1073741824 | bytes 4194304 | tf_op jit(solution)/shard_map/ring_step/pallas_call | solution.py:266
  55.8 3.4 %collective-permute-start.11 = (bf16[1040,128]{1,0:T(8,128)(2,1)S(1)}, bf16[1040,128]{1,0:T(8,128)(2,1)S(1)}, u32[]{:S(2)}, u32[]{:S(2)}) collective-permute-start(bf16[1040,128]{1,0:T(8,128)(2,1)S(1)} %collective-permute-done.9.up_ref), channel_id=1, source_target_pairs={{0,4},{4,8},{8,12},{12,14},{14,10},{10,6},{6,2},{2,0},{1,5},{5,9},... | collective-permute-start | bytes 798728 | tf_op jit(solution)/shard_map/ppermute | solution.py:470
  59.3 4.2 %ring_step.13 = (bf16[49,256,512]{2,1,0:T(8,128)(2,1)S(1)}, f32[9,128,256]{2,1,0:T(8,128)S(1)}, f32[8,128]{1,0:T(8,128)}) custom-call(s32[113]{0:T(128)S(1)} %copy-done.2, bf16[1040,128]{1,0:T(8,128)(2,1)S(1)} %collective-permute-done.7.up_ref, bf16[1040,128]{1,0:T(8,128)(2,1)S(1)} %collective-permute-done.12.down_ref, ...), custom_call_target="tpu_custom_call", output_to_operand_aliasing={{0}: (6, {})} | custom-call | flops 1073741824 | bytes 4194304 | tf_op jit(solution)/shard_map/ring_step/pallas_call | solution.py:266
  63.4 3.2 %ring_step.14 = (bf16[49,256,512]{2,1,0:T(8,128)(2,1)S(1)}, f32[9,128,256]{2,1,0:T(8,128)S(1)}, f32[8,128]{1,0:T(8,128)}) custom-call(s32[113]{0:T(128)S(1)} %copy-done.2, bf16[1040,128]{1,0:T(8,128)(2,1)S(1)} %collective-permute-done.9.up_ref, bf16[1040,128]{1,0:T(8,128)(2,1)S(1)} %collective-permute-done.13.down_ref, ...), custom_call_target="tpu_custom_call", output_to_operand_aliasing={{0}: (6, {})} | custom-call | flops 1073741824 | bytes 4194304 | tf_op jit(solution)/shard_map/ring_step/pallas_call | solution.py:266
  66.7 4.3 %ring_step.15 = (bf16[49,256,512]{2,1,0:T(8,128)(2,1)S(1)}, f32[9,128,256]{2,1,0:T(8,128)S(1)}, f32[8,128]{1,0:T(8,128)}) custom-call(s32[113]{0:T(128)S(1)} %copy-done.2, bf16[1040,128]{1,0:T(8,128)(2,1)S(1)} %collective-permute-done.11.up_ref, bf16[1040,128]{1,0:T(8,128)(2,1)S(1)} %collective-permute-done.14.down_ref, ...), custom_call_target="tpu_custom_call", output_to_operand_aliasing={{0}: (6, {})} | custom-call | flops 1073741824 | bytes 4194304 | tf_op jit(solution)/shard_map/ring_step/pallas_call | solution.py:266
  71.0 2.6 %weighted_halves.1 = (bf16[4,4,6,64,128]{4,3,2,1,0:T(8,128)(2,1)S(1)}, bf16[8,64,256]{2,1,0:T(8,128)(2,1)S(1)}, bf16[8,64,256]{2,1,0:T(8,128)(2,1)S(1)}, f32[4,128]{1,0:T(4,128)S(1)}, f32[4,128]{1,0:T(4,128)S(1)}) custom-call(s32[113]{0:T(128)S(1)} %copy-done.2, f32[9,128,256]{2,1,0:T(8,128)S(1)} %get-tuple-element.79.total_ref, ...), custom_call_target="tpu_custom_call" | custom-call | tf_op jit(solution)/shard_map/weighted_halves/pallas_call | solution.py:355
  73.7 1.7 %products.3 = bf16[4,4,6,64,128]{4,3,2,1,0:T(8,128)(2,1)S(1)} custom-call(s32[113]{0:T(128)S(1)} %copy-done.2, bf16[8,64,256]{2,1,0:T(8,128)(2,1)S(1)} %get-tuple-element.82.turned_ref, bf16[49,256,512]{2,1,0:T(8,128)(2,1)S(1)} %get-tuple-element.80.states_ref), custom_call_target="tpu_custom_call" | custom-call | tf_op jit(solution)/shard_map/products/pallas_call | solution.py:366
  76.1 1.7 %products.2.own_ref = f32[4,4,6,64,128]{4,3,2,1,0:T(8,128)S(1)} custom-call(s32[113]{0:T(128)S(1)} %copy-done.2, bf16[8,64,256]{2,1,0:T(8,128)(2,1)S(1)} %get-tuple-element.81.turned_ref, bf16[49,256,512]{2,1,0:T(8,128)(2,1)S(1)} %get-tuple-element.80.states_ref), custom_call_target="tpu_custom_call" | custom-call | tf_op jit(solution)/shard_map/products/pallas_call | solution.py:366
  77.9 2.7 %kept_half.1._ = bf16[4,8,6,64,128]{4,3,2,1,0:T(8,128)(2,1)} custom-call(s32[113]{0:T(128)S(1)} %copy-done.2, bf16[8,64,256]{2,1,0:T(8,128)(2,1)S(1)} %get-tuple-element.81.turned_ref, bf16[49,256,512]{2,1,0:T(8,128)(2,1)S(1)} %get-tuple-element.80.states_ref, bf16[4,4,6,64,128]{4,3,2,1,0:T(8,128)(2,1)S(1)} %collective-permute-done.17.got_ref), custom_call_target="tpu_custom_call" | custom-call | tf_op jit(solution)/shard_map/kept_half/pallas_call | solution.py:422
  80.6 2.0 %add_received.1 = (bf16[4,8,6,64,128]{4,3,2,1,0:T(8,128)(2,1)}, f32[4,128]{1,0:T(4,128)}) custom-call(f32[4,4,6,64,128]{4,3,2,1,0:T(8,128)S(1)} %products.2.own_ref, bf16[4,4,6,64,128]{4,3,2,1,0:T(8,128)(2,1)S(1)} %collective-permute-done.15.got_ref, f32[4,128]{1,0:T(4,128)S(1)} %get-tuple-element.83.rate_ref, ...), custom_call_target="tpu_custom_call", output_to_operand_aliasing={{0}: (4, {})} | custom-call | tf_op jit(solution)/shard_map/add_received/pallas_call | solution.py:431
  (49 shorter events, 14.8 us)
Async XLA Ops:
  0.6 10.5 %copy-start.1 = (s32[256,1024]{1,0:T(8,128)S(1)}, s32[256,1024]{1,0:T(8,128)}, u32[]{:S(2)}) copy-start(s32[256,1024]{1,0:T(8,128)} %counts_ref.1) | copy-start | bytes 3145732
  0.6 9.7 %copy-start.4 = (s32[64,6]{0,1:T(8,128)S(1)}, s32[64,6]{0,1:T(8,128)}, u32[]{:S(2)}) copy-start(s32[64,6]{0,1:T(8,128)} %param.10) | copy-start | bytes 4612
  0.7 10.5 %copy-start.3 = (f32[1024]{0:T(1024)S(1)}, f32[1024]{0:T(1024)}, u32[]{:S(2)}) copy-start(f32[1024]{0:T(1024)} %param.8) | copy-start | bytes 12292
  3.2 3.4 %collective-permute-start = (f32[4,1024]{1,0:T(4,128)}, f32[4,1024]{1,0:T(4,128)S(1)}, u32[]{:S(2)}, u32[]{:S(2)}) collective-permute-start(f32[4,1024]{1,0:T(4,128)} %get-tuple-element.45), channel_id=1, source_target_pairs={{0,1},{2,3},{4,5},{6,7},{8,9},{10,11},{12,13},{14,15},{16,17},{18,... | collective-permute-start | bytes 49160 | tf_op jit(solution)/shard_map/ppermute | solution.py:456
  7.2 9.5 %collective-permute-start.1 = (bf16[1040,128]{1,0:T(8,128)(2,1)}, bf16[1040,128]{1,0:T(8,128)(2,1)S(1)}, u32[]{:S(2)}, u32[]{:S(2)}) collective-permute-start(bf16[1040,128]{1,0:T(8,128)(2,1)} %get-tuple-element.48.up_ref), channel_id=1, source_target_pairs={{0,4},{4,8},{8,12},{12,14},{14,10},{10,6},{6,2},{2,0},{1,5},{5,9},... | collective-permute-start | bytes 798728 | tf_op jit(solution)/shard_map/ppermute | solution.py:470
  9.7 8.9 %collective-permute-start.4 = (bf16[1040,128]{1,0:T(8,128)(2,1)}, bf16[1040,128]{1,0:T(8,128)(2,1)S(1)}, u32[]{:S(2)}, u32[]{:S(2)}) collective-permute-start(bf16[1040,128]{1,0:T(8,128)(2,1)} %get-tuple-element.49.down_ref), channel_id=1, source_target_pairs={{4,0},{8,4},{12,8},{14,12},{10,14},{6,10},{2,6},{0,2},{5,1},{9,5},... | collective-permute-start | bytes 798728 | tf_op jit(solution)/shard_map/ppermute | solution.py:470
  16.8 9.4 %collective-permute-start.2 = (bf16[1040,128]{1,0:T(8,128)(2,1)S(1)}, bf16[1040,128]{1,0:T(8,128)(2,1)S(1)}, u32[]{:S(2)}, u32[]{:S(2)}) collective-permute-start(bf16[1040,128]{1,0:T(8,128)(2,1)S(1)} %collective-permute-done.1.up_ref), channel_id=1, source_target_pairs={{0,4},{4,8},{8,12},{12,14},{14,10},{10,6},{6,2},{2,0},{1,5},{5,9},... | collective-permute-start | bytes 798728 | tf_op jit(solution)/shard_map/ppermute | solution.py:470
  18.6 8.6 %collective-permute-start.6 = (bf16[1040,128]{1,0:T(8,128)(2,1)S(1)}, bf16[1040,128]{1,0:T(8,128)(2,1)S(1)}, u32[]{:S(2)}, u32[]{:S(2)}) collective-permute-start(bf16[1040,128]{1,0:T(8,128)(2,1)S(1)} %collective-permute-done.4.down_ref), channel_id=1, source_target_pairs={{4,0},{8,4},{12,8},{14,12},{10,14},{6,10},{2,6},{0,2},{5,1},{9,5},... | collective-permute-start | bytes 798728 | tf_op jit(solution)/shard_map/ppermute | solution.py:470
  19.1 2.8 %copy-start = (bf16[4,8,6,128,128]{4,3,2,1,0:T(8,128)(2,1)S(1)}, bf16[4,8,6,128,128]{4,3,2,1,0:T(8,128)(2,1)}, u32[]{:S(2)}) copy-start(bf16[4,8,6,128,128]{4,3,2,1,0:T(8,128)(2,1)} %excite_ref.15) | copy-start | bytes 18874372
  21.9 0.6 copy-start.2
  26.2 7.6 %collective-permute-start.3 = (bf16[1040,128]{1,0:T(8,128)(2,1)S(1)}, bf16[1040,128]{1,0:T(8,128)(2,1)S(1)}, u32[]{:S(2)}, u32[]{:S(2)}) collective-permute-start(bf16[1040,128]{1,0:T(8,128)(2,1)S(1)} %collective-permute-done.2.up_ref), channel_id=1, source_target_pairs={{0,4},{4,8},{8,12},{12,14},{14,10},{10,6},{6,2},{2,0},{1,5},{5,9},... | collective-permute-start | bytes 798728 | tf_op jit(solution)/shard_map/ppermute | solution.py:470
  27.1 8.7 %collective-permute-start.8 = (bf16[1040,128]{1,0:T(8,128)(2,1)S(1)}, bf16[1040,128]{1,0:T(8,128)(2,1)S(1)}, u32[]{:S(2)}, u32[]{:S(2)}) collective-permute-start(bf16[1040,128]{1,0:T(8,128)(2,1)S(1)} %collective-permute-done.6.down_ref), channel_id=1, source_target_pairs={{4,0},{8,4},{12,8},{14,12},{10,14},{6,10},{2,6},{0,2},{5,1},{9,5},... | collective-permute-start | bytes 798728 | tf_op jit(solution)/shard_map/ppermute | solution.py:470
  33.8 7.2 %collective-permute-start.5 = (bf16[1040,128]{1,0:T(8,128)(2,1)S(1)}, bf16[1040,128]{1,0:T(8,128)(2,1)S(1)}, u32[]{:S(2)}, u32[]{:S(2)}) collective-permute-start(bf16[1040,128]{1,0:T(8,128)(2,1)S(1)} %collective-permute-done.3.up_ref), channel_id=1, source_target_pairs={{0,4},{4,8},{8,12},{12,14},{14,10},{10,6},{6,2},{2,0},{1,5},{5,9},... | collective-permute-start | bytes 798728 | tf_op jit(solution)/shard_map/ppermute | solution.py:470
  35.8 7.2 %collective-permute-start.10 = (bf16[1040,128]{1,0:T(8,128)(2,1)S(1)}, bf16[1040,128]{1,0:T(8,128)(2,1)S(1)}, u32[]{:S(2)}, u32[]{:S(2)}) collective-permute-start(bf16[1040,128]{1,0:T(8,128)(2,1)S(1)} %collective-permute-done.8.down_ref), channel_id=1, source_target_pairs={{4,0},{8,4},{12,8},{14,12},{10,14},{6,10},{2,6},{0,2},{5,1},{9,5},... | collective-permute-start | bytes 798728 | tf_op jit(solution)/shard_map/ppermute | solution.py:470
  41.0 7.0 %collective-permute-start.7 = (bf16[1040,128]{1,0:T(8,128)(2,1)S(1)}, bf16[1040,128]{1,0:T(8,128)(2,1)S(1)}, u32[]{:S(2)}, u32[]{:S(2)}) collective-permute-start(bf16[1040,128]{1,0:T(8,128)(2,1)S(1)} %collective-permute-done.5.up_ref), channel_id=1, source_target_pairs={{0,4},{4,8},{8,12},{12,14},{14,10},{10,6},{6,2},{2,0},{1,5},{5,9},... | collective-permute-start | bytes 798728 | tf_op jit(solution)/shard_map/ppermute | solution.py:470
  43.0 7.1 %collective-permute-start.12 = (bf16[1040,128]{1,0:T(8,128)(2,1)S(1)}, bf16[1040,128]{1,0:T(8,128)(2,1)S(1)}, u32[]{:S(2)}, u32[]{:S(2)}) collective-permute-start(bf16[1040,128]{1,0:T(8,128)(2,1)S(1)} %collective-permute-done.10.down_ref), channel_id=1, source_target_pairs={{4,0},{8,4},{12,8},{14,12},{10,14},{6,10},{2,6},{0,2},{5,1},{9,5},... | collective-permute-start | bytes 798728 | tf_op jit(solution)/shard_map/ppermute | solution.py:470
  48.0 7.8 %collective-permute-start.9 = (bf16[1040,128]{1,0:T(8,128)(2,1)S(1)}, bf16[1040,128]{1,0:T(8,128)(2,1)S(1)}, u32[]{:S(2)}, u32[]{:S(2)}) collective-permute-start(bf16[1040,128]{1,0:T(8,128)(2,1)S(1)} %collective-permute-done.7.up_ref), channel_id=1, source_target_pairs={{0,4},{4,8},{8,12},{12,14},{14,10},{10,6},{6,2},{2,0},{1,5},{5,9},... | collective-permute-start | bytes 798728 | tf_op jit(solution)/shard_map/ppermute | solution.py:470
  50.2 9.1 %collective-permute-start.13 = (bf16[1040,128]{1,0:T(8,128)(2,1)S(1)}, bf16[1040,128]{1,0:T(8,128)(2,1)S(1)}, u32[]{:S(2)}, u32[]{:S(2)}) collective-permute-start(bf16[1040,128]{1,0:T(8,128)(2,1)S(1)} %collective-permute-done.12.down_ref), channel_id=1, source_target_pairs={{4,0},{8,4},{12,8},{14,12},{10,14},{6,10},{2,6},{0,2},{5,1},{9,5},... | collective-permute-start | bytes 798728 | tf_op jit(solution)/shard_map/ppermute | solution.py:470
  55.8 10.8 %collective-permute-start.11 = (bf16[1040,128]{1,0:T(8,128)(2,1)S(1)}, bf16[1040,128]{1,0:T(8,128)(2,1)S(1)}, u32[]{:S(2)}, u32[]{:S(2)}) collective-permute-start(bf16[1040,128]{1,0:T(8,128)(2,1)S(1)} %collective-permute-done.9.up_ref), channel_id=1, source_target_pairs={{0,4},{4,8},{8,12},{12,14},{14,10},{10,6},{6,2},{2,0},{1,5},{5,9},... | collective-permute-start | bytes 798728 | tf_op jit(solution)/shard_map/ppermute | solution.py:470
  59.3 7.4 %collective-permute-start.14 = (bf16[1040,128]{1,0:T(8,128)(2,1)S(1)}, bf16[1040,128]{1,0:T(8,128)(2,1)S(1)}, u32[]{:S(2)}, u32[]{:S(2)}) collective-permute-start(bf16[1040,128]{1,0:T(8,128)(2,1)S(1)} %collective-permute-done.13.down_ref), channel_id=1, source_target_pairs={{4,0},{8,4},{12,8},{14,12},{10,14},{6,10},{2,6},{0,2},{5,1},{9,5},... | collective-permute-start | bytes 798728 | tf_op jit(solution)/shard_map/ppermute | solution.py:470
  73.6 4.2 %collective-permute-start.17 = (bf16[4,4,6,64,128]{4,3,2,1,0:T(8,128)(2,1)S(1)}, bf16[4,4,6,64,128]{4,3,2,1,0:T(8,128)(2,1)S(1)}, u32[]{:S(2)}, u32[]{:S(2)}) collective-permute-start(bf16[4,4,6,64,128]{4,3,2,1,0:T(8,128)(2,1)S(1)} %get-tuple-element.85), channel_id=1, source_target_pairs={{0,1},{1,0},{2,3},{3,2},{4,5},{5,4},{6,7},{7,6},{8,9},{9,8},{10,11... | collective-permute-start | bytes 4718600 | tf_op jit(solution)/shard_map/ppermute | solution.py:477
  75.5 5.1 %collective-permute-start.15 = (bf16[4,4,6,64,128]{4,3,2,1,0:T(8,128)(2,1)S(1)}, bf16[4,4,6,64,128]{4,3,2,1,0:T(8,128)(2,1)S(1)}, u32[]{:S(2)}, u32[]{:S(2)}) collective-permute-start(bf16[4,4,6,64,128]{4,3,2,1,0:T(8,128)(2,1)S(1)} %products.3), channel_id=1, source_target_pairs={{0,1},{1,0},{2,3},{3,2},{4,5},{5,4},{6,7},{7,6},{8,9},{9,8},{10,11... | collective-permute-start | bytes 4718600 | tf_op jit(solution)/shard_map/ppermute | solution.py:480
  76.0 4.6 %collective-permute-start.16 = (f32[4,128]{1,0:T(4,128)S(1)}, f32[4,128]{1,0:T(4,128)S(1)}, u32[]{:S(2)}, u32[]{:S(2)}) collective-permute-start(f32[4,128]{1,0:T(4,128)S(1)} %get-tuple-element.84), channel_id=1, source_target_pairs={{0,1},{1,0},{2,3},{3,2},{4,5},{5,4},{6,7},{7,6},{8,9},{9,8},{10,11... | collective-permute-start | bytes 6152 | tf_op jit(solution)/shard_map/ppermute | solution.py:478

commit v6 on v5

v6 whole, which is shorter than its diff:
```python
import functools
import jax
import jax.numpy as jnp
from jax import lax
from jax.experimental import pallas as pl
from jax.experimental.pallas import tpu as pltpu
from jax.sharding import PartitionSpec as P

GROUPS = 2
SMEM = pl.BlockSpec(memory_space=pltpu.SMEM)
VMEM = pl.BlockSpec(memory_space=pltpu.VMEM)
ANYWHERE = pl.BlockSpec(memory_space=pl.ANY)
PARAMS = pltpu.CompilerParams(vmem_limit_bytes=16 << 20)


def lag_tables(bins, basis_count, overall, lanes):
    log_decay = -(8.0 ** jnp.arange(basis_count, dtype=jnp.float32)) / (2.0 * overall)
    t = jnp.arange(bins, dtype=jnp.float32)
    lag = t[:, None] - 1.0 - t[None, :]
    weights = jnp.where(
        lag[None] >= 0.0,
        (1.0 - jnp.exp(log_decay))[:, None, None]
        * jnp.exp(jnp.maximum(lag, 0.0)[None] * log_decay[:, None, None]),
        jnp.float32(0.0),
    )
    power = jnp.exp(t[None, :, None] * log_decay[:, None, None])
    return weights.astype(jnp.bfloat16), jnp.broadcast_to(power, (basis_count, bins, lanes))


def load_lanes(first, count, parts, counts_hbm, mark_hbm, counts, mark, sems):
    lanes = count // parts
    copies = []
    for j in range(parts):
        at = pl.ds(first + j * lanes, lanes)
        to = pl.ds(j * lanes, lanes)
        copies.append(
            (
                pltpu.make_async_copy(counts_hbm.at[:, at], counts.at[:, to], sems.at[0, j]),
                pltpu.make_async_copy(mark_hbm.at[:, at], mark.at[:, to], sems.at[1, j]),
            )
        )
        for copy in copies[-1]:
            copy.start()
    return copies


def impact_of(counts, mark, at):
    impact = counts[:, at].astype(jnp.float32) * mark[:, at].astype(jnp.float32)
    return impact.astype(jnp.bfloat16)


def first_kernel(counts_hbm, mark_hbm, out_ref, counts, mark, sems):
    bins, lanes = counts.shape
    tile = out_ref.shape[1]
    parts = sems.shape[1]
    copies = load_lanes(0, lanes, parts, counts_hbm, mark_hbm, counts, mark, sems)
    for j in range(parts):
        for copy in copies[j]:
            copy.wait()
        for q in range(j * lanes // parts // tile, (j + 1) * lanes // parts // tile):
            at = slice(q * tile, (q + 1) * tile)
            out_ref[q * bins : (q + 1) * bins] = impact_of(counts, mark, at)


def second_kernel(
    basis, tile, overall, counts_hbm, mark_hbm, out_ref, ends_ref, counts, mark, sems
):
    bins, types = counts.shape
    parts = sems.shape[1]
    lanes = types // parts
    copies = load_lanes(0, types, parts, counts_hbm, mark_hbm, counts, mark, sems)
    back = (bins - 1 - lax.broadcasted_iota(jnp.int32, (bins, tile), 0)).astype(jnp.float32)
    gains = []
    for b in range(basis):
        rate = (8.0**b) / (2.0 * overall)
        gains.append((1.0 - jnp.exp(jnp.full((bins, tile), -rate, jnp.float32))) * jnp.exp(-rate * back))
    half = types // tile // 2
    for j in range(parts):
        for copy in copies[j]:
            copy.wait()
        for block in range(j * lanes // tile, (j + 1) * lanes // tile):
            at = slice(block * tile, (block + 1) * tile)
            impact = impact_of(counts, mark, at)
            if block >= half:
                out_ref[(block - half) * bins : (block - half + 1) * bins] = impact
            impact = impact.astype(jnp.float32)
            for b in range(basis):
                ends_ref[b : b + 1, at] = jnp.sum(impact * gains[b], axis=0, keepdims=True)
    rest = out_ref.shape[0] - half * bins
    out_ref[half * bins :] = jnp.zeros((rest, tile), jnp.bfloat16)


def carry_rows(half, basis):
    return -(-half * basis // 16) * 16


def impact_messages(counts, mark, dims, overall):
    basis, _, _, tile = dims
    bins, types = counts.shape
    half = types // tile // 2
    params = pltpu.CompilerParams(vmem_limit_bytes=56 << 20)
    one = pl.pallas_call(
        first_kernel,
        in_specs=[ANYWHERE, ANYWHERE],
        out_specs=VMEM,
        out_shape=jax.ShapeDtypeStruct((half * bins, tile), jnp.bfloat16),
        scratch_shapes=[
            pltpu.VMEM((bins, types // 2), jnp.int32),
            pltpu.VMEM((bins, types // 2), jnp.bfloat16),
            pltpu.SemaphoreType.DMA((2, 2)),
        ],
        compiler_params=params,
        name="first_message",
    )(counts, mark)
    two, ends = pl.pallas_call(
        functools.partial(second_kernel, basis, tile, overall),
        in_specs=[ANYWHERE, ANYWHERE],
        out_specs=[VMEM, VMEM],
        out_shape=[
            jax.ShapeDtypeStruct((half * bins + 2 * carry_rows(half, basis), tile), jnp.bfloat16),
            jax.ShapeDtypeStruct((basis, types), jnp.float32),
        ],
        scratch_shapes=[
            pltpu.VMEM((bins, types), jnp.int32),
            pltpu.VMEM((bins, types), jnp.bfloat16),
            pltpu.SemaphoreType.DMA((2, 2)),
        ],
        compiler_params=params,
        name="second_message",
    )(counts, mark)
    return one, two, ends


def carry_kernel(basis, bins, enter_ref, _, out_ref, held, sem):
    rows, tile = out_ref.shape
    half = enter_ref.shape[1] // tile // 2
    each = carry_rows(half, basis)
    carry = []
    for d in range(2):
        for q in range(half):
            carry.append(enter_ref[:, (d * half + q) * tile : (d * half + q + 1) * tile])
        if each > half * basis:
            carry.append(jnp.zeros((each - half * basis, tile), jnp.float32))
    held[...] = jnp.concatenate(carry, axis=0).astype(jnp.bfloat16)
    copy = pltpu.make_async_copy(held, out_ref.at[pl.ds(half * bins, 2 * each)], sem)
    copy.start()
    copy.wait()


def add_carry(enter, two, basis, bins):
    rows, tile = two.shape
    return pl.pallas_call(
        functools.partial(carry_kernel, basis, bins),
        in_specs=[VMEM, ANYWHERE],
        out_specs=ANYWHERE,
        out_shape=jax.ShapeDtypeStruct(two.shape, two.dtype),
        scratch_shapes=[
            pltpu.VMEM((rows % bins, tile), jnp.bfloat16),
            pltpu.SemaphoreType.DMA,
        ],
        input_output_aliases={1: 0},
        compiler_params=PARAMS,
        name="carry_rows",
    )(enter, two)


def ring_place(index, n):
    return jnp.where(index % 2 == 0, index // 2, n - 1 - index // 2)


def code_of(row, slot, block):
    return (row * 256 + slot) * 256 + block


def plan_kernel(shape, place_ref, col_ref, fill_ref, plan_ref):
    brows, slots, width, n, most = shape
    own = place_ref[0]
    entries = brows * slots
    tail = n * (most + 1)
    plan_ref[tail] = place_ref[1]
    for step in range(n):
        plan_ref[step * (most + 1)] = 0

    @pl.loop(0, brows)
    def _(row):
        fill = fill_ref[own * brows + row]
        plan_ref[tail + 1 + row] = fill

        @pl.loop(0, fill)
        def _(slot):
            column = col_ref[own * entries + row * slots + slot]
            source = lax.div(column, width)
            block = lax.rem(column, width)
            ahead = ring_place(source, n) - ring_place(own, n)
            ahead = jnp.where(ahead < 0, ahead + n, ahead)
            second = (block >= width // 2).astype(jnp.int32)
            whole = (ahead == 0) | (ahead == n // 2)
            behind = (ahead > n // 2).astype(jnp.int32)
            hops = jnp.where(behind == 1, n - ahead, ahead)
            call = jnp.where(whole, jnp.where(ahead == 0, 0, n - 1), 2 * hops - 1 + second)
            place = block - (width // 2) * (second - 1 + behind)
            base = call * (most + 1)
            count = plan_ref[base] + 1
            plan_ref[base] = count
            plan_ref[base + count] = code_of(row, slot, jnp.where(whole, block, place))

    for step in range(n):
        base = step * (most + 1)
        count = plan_ref[base]

        @pl.when(lax.rem(count, 2) == 1)
        def _(base=base, count=count):
            plan_ref[base + count + 1] = code_of(brows, 0, 0)


def make_plan(place, cols, fill, dims, width, n):
    _, brows, slots, _ = dims
    most = 2 * max(2, brows * slots // n)
    return pl.pallas_call(
        functools.partial(plan_kernel, (brows, slots, width, n, most)),
        in_specs=[SMEM] * 3,
        out_specs=SMEM,
        out_shape=jax.ShapeDtypeStruct((n * (most + 1) + 1 + brows,), jnp.int32),
        name="plan",
    )(place, cols, fill)


def start_kernel(tile, counts_ref, base_ref, total_ref):
    for row in range(total_ref.shape[0] - 1):
        at = slice(row * tile, (row + 1) * tile)
        total_ref[row] = (base_ref[:, at] - counts_ref[:, at].astype(jnp.float32)).T
    total_ref[total_ref.shape[0] - 1] = jnp.zeros(total_ref.shape[1:], jnp.float32)


def start_total(counts, base_rate, dims):
    _, brows, _, tile = dims
    return pl.pallas_call(
        functools.partial(start_kernel, tile),
        in_specs=[VMEM, VMEM],
        out_specs=VMEM,
        out_shape=jax.ShapeDtypeStruct((brows + 1, tile, counts.shape[0]), jnp.float32),
        compiler_params=PARAMS,
        name="base_less_counts",
    )(counts, base_rate)


def step_kernel(dims, n, call, seconds, plan_ref, *refs):
    basis, brows, slots, tile = dims
    lag_ref, power_ref, excite_ref = refs[4:7]
    total_in, states_ref, total_ref, built_ref, held, sems = refs[-6:]
    bins = lag_ref.shape[1]
    half = held.shape[0] // 2
    each = carry_rows(half, basis)
    most = (plan_ref.shape[0] - 1 - brows) // n - 1
    built_ref[...] = jnp.zeros_like(built_ref)
    total_ref[...] = total_in[...]
    for d in range(2):
        impact_ref, carry_ref = refs[2 * d : 2 * d + 2]
        first = half * bins + seconds[d] * each
        carry = carry_ref[first : first + each].astype(jnp.float32)
        for q in range(0, half, 2):
            both = jnp.concatenate(
                [impact_ref[(q + i) * bins : (q + i + 1) * bins] for i in range(2)], axis=1
            )
            for b in range(basis):
                state = jnp.dot(lag_ref[b], both, preferred_element_type=jnp.float32)
                for i in range(2):
                    row = (q + i) * basis + b
                    held[d * half + q + i, :, b * tile : (b + 1) * tile] = (
                        state[:, i * tile : (i + 1) * tile] + power_ref[b] * carry[row : row + 1]
                    ).astype(jnp.bfloat16)

    def entry_at(place):
        code = plan_ref[call * (most + 1) + 1 + place]
        return code >> 16, (code >> 8) & 255, code & 255

    def copy_at(place):
        row, slot, block = entry_at(place)
        return pltpu.make_async_copy(
            held.at[block], states_ref.at[row * slots + slot], sems.at[place]
        )

    pairs = (plan_ref[call * (most + 1)] + 1) // 2

    @pl.loop(0, pairs)
    def _(k):
        terms = []
        for i in range(2):
            row, slot, block = entry_at(2 * k + i)
            copy_at(2 * k + i).start()
            inside = jnp.minimum(row, brows - 1)
            weight = jnp.concatenate([excite_ref[b, inside, slot] for b in range(basis)], axis=1)
            terms.append(
                (
                    row,
                    lax.dot_general(
                        weight,
                        held[block],
                        (((1,), (1,)), ((), ())),
                        preferred_element_type=jnp.float32,
                    ),
                )
            )
        for row, term in terms:
            total_ref[row] += term

    @pl.loop(0, 2 * pairs)
    def _(place):
        copy_at(place).wait()


def take_step(call, seconds, plan, arrived, lag, power, excite, states, total, dims, n):
    basis, brows, slots, tile = dims
    bins = lag.shape[1]
    half = arrived[0].shape[0] // bins
    most = (plan.shape[0] - 1 - brows) // n - 1
    given = [total] if states is None else [states, total]
    return pl.pallas_call(
        functools.partial(step_kernel, dims, n, call, seconds),
        in_specs=[SMEM] + [VMEM] * 7 + [ANYWHERE] * (len(given) - 1) + [VMEM],
        out_specs=[ANYWHERE, VMEM, VMEM],
        out_shape=[
            jax.ShapeDtypeStruct((brows * slots + 1, bins, basis * tile), jnp.bfloat16),
            jax.ShapeDtypeStruct(total.shape, total.dtype),
            jax.ShapeDtypeStruct((8, tile), jnp.float32),
        ],
        scratch_shapes=[
            pltpu.VMEM((2 * half, bins, basis * tile), jnp.bfloat16),
            pltpu.SemaphoreType.DMA((most,)),
        ],
        input_output_aliases={} if states is None else {8: 0},
        compiler_params=PARAMS,
        cost_estimate=pl.CostEstimate(
            flops=8 * basis * bins * bins * tile * 4,
            bytes_accessed=4 * 1024 * 1024,
            transcendentals=0,
        ),
        name="ring_step",
    )(plan, *arrived, lag, power, excite, *given)


def products(turned_ref, states_ref, plan_ref, group, dims, sent_ref, kept_ref):
    basis, brows, slots, tile = dims
    tail = plan_ref.shape[0] - 1 - brows
    part = tile // 2
    for r, row in enumerate(rows_of(group, dims)):
        fill = plan_ref[tail + 1 + row]
        for s in range(slots):
            grad = jnp.dot(
                turned_ref[row], states_ref[row * slots + s], preferred_element_type=jnp.float32
            )
            grad = jnp.where(s < fill, grad, jnp.zeros_like(grad))
            for b in range(basis):
                at = slice(b * tile, (b + 1) * tile)
                kept_ref[b, r, s] = grad[:part, at]
                sent_ref[b, r, s] = grad[part:, at].astype(sent_ref.dtype)


def rows_of(group, dims):
    count = dims[1] // GROUPS
    return range(group * count, (group + 1) * count)


def weighted_kernel(dims, overall, plan_ref, total_ref, states_ref, sent_ref, kept_ref, *refs):
    _, brows, _, tile = dims
    turned_ref, rate_sent_ref, rate_kept_ref = refs
    half = plan_ref[plan_ref.shape[0] - 1 - brows]
    part = tile // 2
    rates = []
    for row in range(brows):
        weighted = (2.0 / overall) * total_ref[row]
        rates.append(
            lax.dot_general(
                jnp.ones((8, weighted.shape[1]), jnp.float32),
                weighted,
                (((1,), (1,)), ((), ())),
                precision=lax.Precision.HIGHEST,
                preferred_element_type=jnp.float32,
            )[:1]
        )
        weighted = weighted.astype(jnp.bfloat16)
        upper, lower = weighted[:part], weighted[part:]
        turned_ref[row, :part] = jnp.where(half == 0, upper, lower)
        turned_ref[row, part:] = jnp.where(half == 0, lower, upper)
    first_half = jnp.concatenate(rates[: brows // 2], axis=0)
    second_half = jnp.concatenate(rates[brows // 2 :], axis=0)
    rate_kept_ref[...] = jnp.where(half == 0, first_half, second_half)
    rate_sent_ref[...] = jnp.where(half == 0, second_half, first_half)
    products(turned_ref, states_ref, plan_ref, 0, dims, sent_ref, kept_ref)


def later_kernel(dims, group, plan_ref, turned_ref, states_ref, sent_ref, kept_ref):
    products(turned_ref, states_ref, plan_ref, group, dims, sent_ref, kept_ref)


def group_shape(dims, dtype):
    basis, brows, slots, tile = dims
    return jax.ShapeDtypeStruct((basis, brows // GROUPS, slots, tile // 2, tile), dtype)


def first_products(plan, total, states, dims, overall):
    _, brows, _, tile = dims
    turned = jax.ShapeDtypeStruct((brows, tile, total.shape[2]), jnp.bfloat16)
    rate = jax.ShapeDtypeStruct((brows // 2, tile), jnp.float32)
    return pl.pallas_call(
        functools.partial(weighted_kernel, dims, overall),
        in_specs=[SMEM, VMEM, VMEM],
        out_specs=[VMEM] * 5,
        out_shape=[
            group_shape(dims, jnp.bfloat16),
            group_shape(dims, jnp.float32),
            turned,
            rate,
            rate,
        ],
        compiler_params=PARAMS,
        name="weighted_products",
    )(plan, total, states)


def later_products(group, plan, turned, states, dims):
    return pl.pallas_call(
        functools.partial(later_kernel, dims, group),
        in_specs=[SMEM, VMEM, VMEM],
        out_specs=[VMEM, VMEM],
        out_shape=[group_shape(dims, jnp.bfloat16), group_shape(dims, jnp.float32)],
        compiler_params=PARAMS,
        name="products",
    )(plan, turned, states)


def add_kernel(dims, group, kept_ref, got_ref, *refs):
    basis, brows, _, _ = dims
    out_ref, held, sems = refs[-3:]
    if group == GROUPS - 1:
        rate_ref, rate_got_ref, rate_out_ref = refs[0], refs[1], refs[-4]
        out_ref, rate_out_ref = rate_out_ref, out_ref
        rate_out_ref[...] = rate_ref[...] + rate_got_ref[...]
    copies = []
    for r, row in enumerate(rows_of(group, dims)):
        for b in range(basis):
            held[b, r] = (kept_ref[b, r] + got_ref[b, r].astype(jnp.float32)).astype(jnp.bfloat16)
            copies.append(
                pltpu.make_async_copy(held.at[b, r], out_ref.at[b, row], sems.at[b, r])
            )
            copies[-1].start()
    for copy in copies:
        copy.wait()


def add_received(group, kept, got, rates, grad, dims):
    basis, brows, slots, tile = dims
    whole = jax.ShapeDtypeStruct((basis, brows, slots, tile // 2, tile), jnp.bfloat16)
    given = [] if grad is None else [grad]
    last = group == GROUPS - 1
    return pl.pallas_call(
        functools.partial(add_kernel, dims, group),
        in_specs=[VMEM] * (2 + len(rates)) + [ANYWHERE] * len(given),
        out_specs=[ANYWHERE, VMEM] if last else [ANYWHERE],
        out_shape=[whole] + ([jax.ShapeDtypeStruct(rates[0].shape, jnp.float32)] if last else []),
        scratch_shapes=[
            pltpu.VMEM(group_shape(dims, jnp.bfloat16).shape, jnp.bfloat16),
            pltpu.SemaphoreType.DMA((basis, brows // GROUPS)),
        ],
        input_output_aliases={2 + len(rates): 0} if given else {},
        compiler_params=PARAMS,
        name="add_received",
    )(kept, got, *rates, *given)


def shards(counts, mark_value, base_rate, excite, block_col, row_fill):
    dims = excite.shape[:4]
    basis, _, _, tile = dims
    bins = counts.shape[0]
    overall = bins * lax.axis_size("tm")
    n = lax.axis_size("types")
    place = jnp.stack([lax.axis_index("types"), lax.axis_index("tm")]).astype(jnp.int32)
    order = list(range(0, n, 2)) + list(range(1, n, 2))[::-1]
    up = [(order[i], order[(i + 1) % n]) for i in range(n)]
    down = [(b, a) for a, b in up]
    swap = [(0, 1), (1, 0)]

    one, two, ends = impact_messages(counts, mark_value, dims, overall)
    enter = lax.ppermute(ends, "tm", [(0, 1)])
    two = add_carry(enter, two, basis, bins)
    lag, power = lag_tables(bins, basis, overall, tile)
    plan = make_plan(place, block_col.reshape(-1), row_fill, dims, counts.shape[1] // tile, n)
    total = start_total(counts, base_rate.reshape(1, -1), dims)

    states = None
    built = []

    def step(call, seconds, arrived):
        nonlocal states, total
        states, total, done = take_step(
            call, seconds, plan, arrived, lag, power, excite, states, total, dims, n
        )
        built.append(done)

    def send(message, way, hop):
        if hop > 2:
            message = lax.optimization_barrier((message, built[2 * hop - 4]))[0]
        return lax.ppermute(message, "types", way)

    hops = n // 2
    at_up, at_down = [one, two], [one, two]
    for hop in range(1, hops + 1):
        if hop < hops:
            next_up, next_down = [None, None], [None, None]
            for second in range(2):
                next_up[second] = send(at_up[second], up, hop)
                next_down[second] = send(at_down[second], down, hop)
        else:
            next_up = [send(at_up[0], up, hop), None]
            next_down = [None, send(at_down[1], down, hop)]
        if hop == 1:
            step(0, (0, 1), [one, two, two, two])
        else:
            for second in range(2):
                step(
                    2 * hop - 3 + second,
                    (second, second),
                    [at_up[second], at_up[1], at_down[second], at_down[1]],
                )
        at_up, at_down = next_up, next_down
    step(n - 1, (0, 1), [at_up[0], at_down[1], at_down[1], at_down[1]])

    out, kept, turned, rate_sent, rate_kept = first_products(plan, total, states, dims, overall)
    kept = [kept]
    got = [lax.ppermute(out, "tm", swap)]
    rate_got = lax.ppermute(rate_sent, "tm", swap)
    for group in range(1, GROUPS):
        out, more = later_products(group, plan, turned, states, dims)
        kept.append(more)
        got.append(lax.ppermute(out, "tm", swap))
    grad = None
    for group in range(GROUPS):
        rates = [rate_kept, rate_got] if group == GROUPS - 1 else []
        grad, *rate = add_received(group, kept[group], got[group], rates, grad, dims)
    return grad, rate[0].reshape(-1)


def solution(mesh):
    return jax.shard_map(
        shards,
        mesh=mesh,
        in_specs=(
            P(("parts", "tm"), "types"),
            P(("parts", "tm"), "types"),
            P("types"),
            P(None, "types", None, None, None),
            P(),
            P(),
        ),
        out_specs=(P("parts", "types", None, "tm", None), P(("parts", "types", "tm"))),
        check_vma=False,
    )
```

time: 83.7 us -> 76.3 us (0.912)
  waiting for transfers between devices: 11.1 us -> 5.2 us
  Pallas kernels: 45.8 us -> 44.9 us
    ppermute x15, waiting for transfers between devices: 10.3 us -> 2.55 us  [the longest x14 2.54 us: send(): return lax.ppermute(message, 'types', way)]
    ppermute x1, waiting for transfers between devices: 0.01 us -> 1.22 us  [shards(): got = [lax.ppermute(out, 'tm', swap)]]
    pallas_call x14, Pallas kernels: 42.6 us -> 41.5 us  [the longest x8 30 us: take_step(): pl.pallas_call(functools.partial(step_kernel, dims, n, call, seconds), in...]
    ppermute x1, waiting for transfers between devices: 0.01 us -> 0.96 us  [shards(): rate_got = lax.ppermute(rate_sent, 'tm', swap)]
    ppermute x15, starting transfers between devices: 16.6 us -> 17.5 us  [the longest x14 17 us: send(): return lax.ppermute(message, 'types', way)]
    ppermute x1, starting transfers between devices: 2.36 us -> 1.46 us  [shards(): enter = lax.ppermute(ends, 'tm', [(0, 1)])]
    unnamed x11 -> x15, local copies, waits for them, and re-layouts: 3.49 us -> 3.52 us
  transfers between devices with their start and end apart: 18 -> 18, of which waited for: 7 -> 5; matrix products, arithmetic and copies ran while one was open for 3% -> 3% of each run, Pallas kernels for 41% -> 45%
where the time goes in v6:
time: 76.3 us; the launch traced here: 76 us
  Pallas kernels  44.9 us (59%)
  starting transfers between devices  19.1 us (25%)
  waiting for transfers between devices  5.2 us (7%)
  local copies, waits for them, and re-layouts  4.43 us (6%)
  other arithmetic  1.25 us (2%)
  between operations  1.11 us (1%)
    pallas_call x8, Pallas kernels, take_step(): pl.pallas_call(functools.partial(step_kernel, dims, n, call, seconds), in...  30 us
    ppermute x14, starting transfers between devices, send(): return lax.ppermute(message, 'types', way)  17 us
    unnamed x15, local copies, waits for them, and re-layouts  3.52 us
    pallas_call x2, Pallas kernels, add_received(): pl.pallas_call(functools.partial(add_kernel, dims, group), in_specs=[VMEM...  3.14 us
    ppermute x14, waiting for transfers between devices, send(): return lax.ppermute(message, 'types', way)  2.54 us
    pallas_call x1, Pallas kernels, impact_messages(): pl.pallas_call(functools.partial(second_kernel, basis, tile, overall), in...  2.46 us
    pallas_call x1, Pallas kernels, make_plan(): pl.pallas_call(functools.partial(plan_kernel, (brows, slots, width, n, mo...  2.46 us
    pallas_call x1, Pallas kernels, first_products(): pl.pallas_call(functools.partial(weighted_kernel, dims, overall), in_spec...  2.38 us
  transfers between devices with their start and end apart: 18, of which 5 were waited for; matrix products, arithmetic and copies ran while one was open for 3% of the time, Pallas kernels for 45%

profile of v6, /device:TPU:0, one launch (start us, length us, event | category | flops | bytes accessed | tf_op | source)
XLA Modules:
  0.0 76.0 jit_solution(5297897685754792035)
XLA Ops:
  0.7 2.0 %first_message.1.refs_0_ = bf16[1024,128]{1,0:T(8,128)(2,1)} custom-call(s32[256,1024]{1,0:T(8,128)} %counts_ref.1, bf16[256,1024]{1,0:T(8,128)(2,1)} %mark_hbm.3), custom_call_target="tpu_custom_call" | custom-call | tf_op jit(solution)/shard_map/first_message/pallas_call | solution.py:102
  2.7 3.1 %collective-permute-start = (bf16[1024,128]{1,0:T(8,128)(2,1)}, bf16[1024,128]{1,0:T(8,128)(2,1)}, u32[]{:S(2)}, u32[]{:S(2)}) collective-permute-start(bf16[1024,128]{1,0:T(8,128)(2,1)} %first_message.1.refs_0_), channel_id=1, source_target_pairs={{0,4},{4,8},{8,12},{12,14},{14,10},{10,6},{6,2},{2,0},{1,5},{5,9},... | collective-permute-start | bytes 786440 | tf_op jit(solution)/shard_map/ppermute | solution.py:503
  5.7 2.5 %second_message.1 = (bf16[1056,128]{1,0:T(8,128)(2,1)}, f32[4,1024]{1,0:T(4,128)}) custom-call(s32[256,1024]{1,0:T(8,128)} %counts_ref.1, bf16[256,1024]{1,0:T(8,128)(2,1)} %mark_hbm.3), custom_call_target="tpu_custom_call" | custom-call | tf_op jit(solution)/shard_map/second_message/pallas_call | solution.py:115
  8.2 1.5 %collective-permute-start.2 = (f32[4,1024]{1,0:T(4,128)}, f32[4,1024]{1,0:T(4,128)S(1)}, u32[]{:S(2)}, u32[]{:S(2)}) collective-permute-start(f32[4,1024]{1,0:T(4,128)} %get-tuple-element.37), channel_id=1, source_target_pairs={{0,1},{2,3},{4,5},{6,7},{8,9},{10,11},{12,13},{14,15},{16,17},{18,... | collective-permute-start | bytes 49160 | tf_op jit(solution)/shard_map/ppermute | solution.py:484
  11.3 1.8 %collective-permute-start.4 = (bf16[1056,128]{1,0:T(8,128)(2,1)}, bf16[1056,128]{1,0:T(8,128)(2,1)S(1)}, u32[]{:S(2)}, u32[]{:S(2)}) collective-permute-start(bf16[1056,128]{1,0:T(8,128)(2,1)} %carry_rows.1.refs_1_.refs_2_.refs_3_), channel_id=1, source_target_pairs={{4,0},{8,4},{12,8},{14,12},{10,14},{6,10},{2,6},{0,2},{5,1},{9,5},... | collective-permute-start | bytes 811016 | tf_op jit(solution)/shard_map/ppermute | solution.py:503
  15.0 2.5 %plan.1.plan_ref = s32[113]{0:T(128)} custom-call(s32[2]{0:T(128)} %pad_add_fusion.place_ref, s32[384]{0:T(512)} %reshape.90.col_ref, s32[64]{0:T(128)} %fill_ref.1), custom_call_target="tpu_custom_call" | custom-call | tf_op jit(solution)/shard_map/plan/pallas_call | solution.py:219
  17.6 2.1 %collective-permute-start.1 = (bf16[1024,128]{1,0:T(8,128)(2,1)}, bf16[1024,128]{1,0:T(8,128)(2,1)S(1)}, u32[]{:S(2)}, u32[]{:S(2)}) collective-permute-start(bf16[1024,128]{1,0:T(8,128)(2,1)} %collective-permute-done.refs_0_), channel_id=1, source_target_pairs={{0,4},{4,8},{8,12},{12,14},{14,10},{10,6},{6,2},{2,0},{1,5},{5,9},... | collective-permute-start | bytes 786440 | tf_op jit(solution)/shard_map/ppermute | solution.py:503
  20.4 1.7 %collective-permute-start.8 = (bf16[1056,128]{1,0:T(8,128)(2,1)S(1)}, bf16[1056,128]{1,0:T(8,128)(2,1)S(1)}, u32[]{:S(2)}, u32[]{:S(2)}) collective-permute-start(bf16[1056,128]{1,0:T(8,128)(2,1)S(1)} %collective-permute-done.4.refs_3_.refs_2_), channel_id=1, source_target_pairs={{4,0},{8,4},{12,8},{14,12},{10,14},{6,10},{2,6},{0,2},{5,1},{9,5},... | collective-permute-start | bytes 811016 | tf_op jit(solution)/shard_map/ppermute | solution.py:503
  22.3 2.8 %copy-done = bf16[4,8,6,128,128]{4,3,2,1,0:T(8,128)(2,1)S(1)} copy-done((bf16[4,8,6,128,128]{4,3,2,1,0:T(8,128)(2,1)S(1)}, bf16[4,8,6,128,128]{4,3,2,1,0:T(8,128)(2,1)}, u32[]{:S(2)}) %copy-start) | copy-done | bytes 6291480
  25.7 4.6 %ring_step.8 = (bf16[49,256,512]{2,1,0:T(8,128)(2,1)S(1)}, f32[9,128,256]{2,1,0:T(8,128)S(1)}, f32[8,128]{1,0:T(8,128)}) custom-call(s32[113]{0:T(128)S(1)} %copy-done.3, bf16[1024,128]{1,0:T(8,128)(2,1)S(1)} %copy-done.2, bf16[1056,128]{1,0:T(8,128)(2,1)} %carry_rows.1.refs_1_.refs_2_.refs_3_, bf16[1056,128]{1,0:T(8,128)(2,1)} %carry_rows.1.refs_1_.refs_2_.refs_3_, ...), custom_call_target="tpu_custom_call" | custom-call | flops 1073741824 | bytes 4194304 | tf_op jit(solution)/shard_map/ring_step/pallas_call | solution.py:318
  30.3 1.6 %collective-permute-start.9 = (bf16[1024,128]{1,0:T(8,128)(2,1)S(1)}, bf16[1024,128]{1,0:T(8,128)(2,1)S(1)}, u32[]{:S(2)}, u32[]{:S(2)}) collective-permute-start(bf16[1024,128]{1,0:T(8,128)(2,1)S(1)} %collective-permute-done.5.refs_2_), channel_id=1, source_target_pairs={{4,0},{8,4},{12,8},{14,12},{10,14},{6,10},{2,6},{0,2},{5,1},{9,5},... | collective-permute-start | bytes 786440 | tf_op jit(solution)/shard_map/ppermute | solution.py:503
  32.4 4.9 %ring_step.9 = (bf16[49,256,512]{2,1,0:T(8,128)(2,1)S(1)}, f32[9,128,256]{2,1,0:T(8,128)S(1)}, f32[8,128]{1,0:T(8,128)}) custom-call(s32[113]{0:T(128)S(1)} %copy-done.3, bf16[1024,128]{1,0:T(8,128)(2,1)} %collective-permute-done.refs_0_, bf16[1056,128]{1,0:T(8,128)(2,1)S(1)} %collective-permute-done.3.refs_1_.refs_0_, ...), custom_call_target="tpu_custom_call", output_to_operand_aliasing={{0}: (8, {})} | custom-call | flops 1073741824 | bytes 4194304 | tf_op jit(solution)/shard_map/ring_step/pallas_call | solution.py:318
  37.3 3.3 %ring_step.10 = (bf16[49,256,512]{2,1,0:T(8,128)(2,1)S(1)}, f32[9,128,256]{2,1,0:T(8,128)S(1)}, f32[8,128]{1,0:T(8,128)}) custom-call(s32[113]{0:T(128)S(1)} %copy-done.3, bf16[1056,128]{1,0:T(8,128)(2,1)S(1)} %collective-permute-done.3.refs_1_.refs_0_, ...), custom_call_target="tpu_custom_call", output_to_operand_aliasing={{0}: (8, {})} | custom-call | flops 1073741824 | bytes 4194304 | tf_op jit(solution)/shard_map/ring_step/pallas_call | solution.py:318
  40.7 2.0 %collective-permute-start.6 = (bf16[1024,128]{1,0:T(8,128)(2,1)S(1)}, bf16[1024,128]{1,0:T(8,128)(2,1)S(1)}, u32[]{:S(2)}, u32[]{:S(2)}) collective-permute-start(bf16[1024,128]{1,0:T(8,128)(2,1)S(1)} %collective-permute-done.1.refs_0_), channel_id=1, source_target_pairs={{0,4},{4,8},{8,12},{12,14},{14,10},{10,6},{6,2},{2,0},{1,5},{5,9},... | collective-permute-start | bytes 786440 | tf_op jit(solution)/shard_map/ppermute | solution.py:503
  43.3 1.5 %collective-permute-start.13 = (bf16[1056,128]{1,0:T(8,128)(2,1)S(1)}, bf16[1056,128]{1,0:T(8,128)(2,1)S(1)}, u32[]{:S(2)}, u32[]{:S(2)}) collective-permute-start(bf16[1056,128]{1,0:T(8,128)(2,1)S(1)} %collective-permute-done.7.refs_1_.refs_0_), channel_id=1, source_target_pairs={{0,4},{4,8},{8,12},{12,14},{14,10},{10,6},{6,2},{2,0},{1,5},{5,9},... | collective-permute-start | bytes 811016 | tf_op jit(solution)/shard_map/ppermute | solution.py:503
  44.8 3.3 %ring_step.11 = (bf16[49,256,512]{2,1,0:T(8,128)(2,1)S(1)}, f32[9,128,256]{2,1,0:T(8,128)S(1)}, f32[8,128]{1,0:T(8,128)}) custom-call(s32[113]{0:T(128)S(1)} %copy-done.4, bf16[1024,128]{1,0:T(8,128)(2,1)S(1)} %collective-permute-done.1.refs_0_, bf16[1056,128]{1,0:T(8,128)(2,1)S(1)} %collective-permute-done.7.refs_1_.refs_0_, ...), custom_call_target="tpu_custom_call", output_to_operand_aliasing={{0}: (8, {})} | custom-call | flops 1073741824 | bytes 4194304 | tf_op jit(solution)/shard_map/ring_step/pallas_call | solution.py:318
  48.1 3.3 %ring_step.12 = (bf16[49,256,512]{2,1,0:T(8,128)(2,1)S(1)}, f32[9,128,256]{2,1,0:T(8,128)S(1)}, f32[8,128]{1,0:T(8,128)}) custom-call(s32[113]{0:T(128)S(1)} %copy-done.4, bf16[1056,128]{1,0:T(8,128)(2,1)S(1)} %collective-permute-done.7.refs_1_.refs_0_, ...), custom_call_target="tpu_custom_call", output_to_operand_aliasing={{0}: (8, {})} | custom-call | flops 1073741824 | bytes 4194304 | tf_op jit(solution)/shard_map/ring_step/pallas_call | solution.py:318
  53.4 1.8 %collective-permute-done.14.refs_2_ = bf16[1024,128]{1,0:T(8,128)(2,1)S(1)} collective-permute-done((bf16[1024,128]{1,0:T(8,128)(2,1)S(1)}, bf16[1024,128]{1,0:T(8,128)(2,1)S(1)}, u32[]{:S(2)}, u32[]{:S(2)}) %collective-permute-start.14) | collective-permute-done | bytes 262176 | tf_op jit(solution)/shard_map/ppermute | solution.py:503
  55.2 2.6 %ring_step.13 = (bf16[49,256,512]{2,1,0:T(8,128)(2,1)S(1)}, f32[9,128,256]{2,1,0:T(8,128)S(1)}, f32[8,128]{1,0:T(8,128)}) custom-call(s32[113]{0:T(128)S(1)} %copy-done.4, bf16[1024,128]{1,0:T(8,128)(2,1)S(1)} %collective-permute-done.6.refs_0_, bf16[1056,128]{1,0:T(8,128)(2,1)S(1)} %collective-permute-done.13.refs_1_.refs_0_, ...), custom_call_target="tpu_custom_call", output_to_operand_aliasing={{0}: (8, {})} | custom-call | flops 1073741824 | bytes 4194304 | tf_op jit(solution)/shard_map/ring_step/pallas_call | solution.py:318
  57.8 3.9 %ring_step.14 = (bf16[49,256,512]{2,1,0:T(8,128)(2,1)S(1)}, f32[9,128,256]{2,1,0:T(8,128)S(1)}, f32[8,128]{1,0:T(8,128)}) custom-call(s32[113]{0:T(128)S(1)} %copy-done.4, bf16[1056,128]{1,0:T(8,128)(2,1)S(1)} %collective-permute-done.13.refs_1_.refs_0_, ...), custom_call_target="tpu_custom_call", output_to_operand_aliasing={{0}: (8, {})} | custom-call | flops 1073741824 | bytes 4194304 | tf_op jit(solution)/shard_map/ring_step/pallas_call | solution.py:318
  61.8 4.1 %ring_step.15 = (bf16[49,256,512]{2,1,0:T(8,128)(2,1)S(1)}, f32[9,128,256]{2,1,0:T(8,128)S(1)}, f32[8,128]{1,0:T(8,128)}) custom-call(s32[113]{0:T(128)S(1)} %copy-done.4, bf16[1024,128]{1,0:T(8,128)(2,1)S(1)} %collective-permute-done.10.refs_0_, ...), custom_call_target="tpu_custom_call", output_to_operand_aliasing={{0}: (8, {})} | custom-call | flops 1073741824 | bytes 4194304 | tf_op jit(solution)/shard_map/ring_step/pallas_call | solution.py:318
  65.9 2.4 %weighted_products.1 = (bf16[4,4,6,64,128]{4,3,2,1,0:T(8,128)(2,1)S(1)}, f32[4,4,6,64,128]{4,3,2,1,0:T(8,128)S(1)}, bf16[8,128,256]{2,1,0:T(8,128)(2,1)S(1)}, f32[4,128]{1,0:T(4,128)S(1)}, f32[4,128]{1,0:T(4,128)S(1)}) custom-call(s32[113]{0:T(128)S(1)} %copy-done.4, f32[9,128,256]{2,1,0:T(8,128)S(1)} %get-tuple-element.61.total_ref, ...), custom_call_target="tpu_custom_call" | custom-call | tf_op jit(solution)/shard_map/weighted_products/pallas_call | solution.py:405
  68.3 1.5 %products.1 = (bf16[4,4,6,64,128]{4,3,2,1,0:T(8,128)(2,1)S(1)}, f32[4,4,6,64,128]{4,3,2,1,0:T(8,128)S(1)}) custom-call(s32[113]{0:T(128)S(1)} %copy-done.4, bf16[8,128,256]{2,1,0:T(8,128)(2,1)S(1)} %get-tuple-element.63.turned_ref, bf16[49,256,512]{2,1,0:T(8,128)(2,1)S(1)} %get-tuple-element.62.states_ref), custom_call_target="tpu_custom_call" | custom-call | tf_op jit(solution)/shard_map/products/pallas_call | solution.py:422
  74.0 1.9 %add_received.3 = (bf16[4,8,6,64,128]{4,3,2,1,0:T(8,128)(2,1)}, f32[4,128]{1,0:T(4,128)}) custom-call(f32[4,4,6,64,128]{4,3,2,1,0:T(8,128)S(1)} %get-tuple-element.64.kept_ref, bf16[4,4,6,64,128]{4,3,2,1,0:T(8,128)(2,1)S(1)} %collective-permute-done.15.got_ref, f32[4,128]{1,0:T(4,128)S(1)} %get-tuple-element.66.refs_0_, ...), custom_call_target="tpu_custom_call", output_to_operand_aliasing={{0}: (4, {})} | custom-call | tf_op jit(solution)/shard_map/add_received/pallas_call | solution.py:456
  (53 shorter events, 12.5 us)
Async XLA Ops:
  0.6 14.0 %copy-start.1 = (s32[256,1024]{1,0:T(8,128)S(1)}, s32[256,1024]{1,0:T(8,128)}, u32[]{:S(2)}) copy-start(s32[256,1024]{1,0:T(8,128)} %counts_ref.1) | copy-start | bytes 3145732
  0.6 13.2 %copy-start.6 = (s32[64,6]{0,1:T(8,128)S(1)}, s32[64,6]{0,1:T(8,128)}, u32[]{:S(2)}) copy-start(s32[64,6]{0,1:T(8,128)} %param.10) | copy-start | bytes 4612
  0.7 14.0 %copy-start.5 = (f32[1024]{0:T(1024)S(1)}, f32[1024]{0:T(1024)}, u32[]{:S(2)}) copy-start(f32[1024]{0:T(1024)} %param.8) | copy-start | bytes 12292
  2.6 19.7 %copy-start.2 = (bf16[1024,128]{1,0:T(8,128)(2,1)S(1)}, bf16[1024,128]{1,0:T(8,128)(2,1)}, u32[]{:S(2)}) copy-start(bf16[1024,128]{1,0:T(8,128)(2,1)} %first_message.1.refs_0_) | copy-start | bytes 786436
  2.7 14.9 %collective-permute-start = (bf16[1024,128]{1,0:T(8,128)(2,1)}, bf16[1024,128]{1,0:T(8,128)(2,1)}, u32[]{:S(2)}, u32[]{:S(2)}) collective-permute-start(bf16[1024,128]{1,0:T(8,128)(2,1)} %first_message.1.refs_0_), channel_id=1, source_target_pairs={{0,4},{4,8},{8,12},{12,14},{14,10},{10,6},{6,2},{2,0},{1,5},{5,9},... | collective-permute-start | bytes 786440 | tf_op jit(solution)/shard_map/ppermute | solution.py:503
  5.7 24.6 %collective-permute-start.5 = (bf16[1024,128]{1,0:T(8,128)(2,1)}, bf16[1024,128]{1,0:T(8,128)(2,1)S(1)}, u32[]{:S(2)}, u32[]{:S(2)}) collective-permute-start(bf16[1024,128]{1,0:T(8,128)(2,1)} %first_message.1.refs_0_), channel_id=1, source_target_pairs={{4,0},{8,4},{12,8},{14,12},{10,14},{6,10},{2,6},{0,2},{5,1},{9,5},... | collective-permute-start | bytes 786440 | tf_op jit(solution)/shard_map/ppermute | solution.py:503
  8.2 2.5 %collective-permute-start.2 = (f32[4,1024]{1,0:T(4,128)}, f32[4,1024]{1,0:T(4,128)S(1)}, u32[]{:S(2)}, u32[]{:S(2)}) collective-permute-start(f32[4,1024]{1,0:T(4,128)} %get-tuple-element.37), channel_id=1, source_target_pairs={{0,1},{2,3},{4,5},{6,7},{8,9},{10,11},{12,13},{14,15},{16,17},{18,... | collective-permute-start | bytes 49160 | tf_op jit(solution)/shard_map/ppermute | solution.py:484
  11.3 9.1 %collective-permute-start.4 = (bf16[1056,128]{1,0:T(8,128)(2,1)}, bf16[1056,128]{1,0:T(8,128)(2,1)S(1)}, u32[]{:S(2)}, u32[]{:S(2)}) collective-permute-start(bf16[1056,128]{1,0:T(8,128)(2,1)} %carry_rows.1.refs_1_.refs_2_.refs_3_), channel_id=1, source_target_pairs={{4,0},{8,4},{12,8},{14,12},{10,14},{6,10},{2,6},{0,2},{5,1},{9,5},... | collective-permute-start | bytes 811016 | tf_op jit(solution)/shard_map/ppermute | solution.py:503
  17.4 14.5 %collective-permute-start.3 = (bf16[1056,128]{1,0:T(8,128)(2,1)}, bf16[1056,128]{1,0:T(8,128)(2,1)S(1)}, u32[]{:S(2)}, u32[]{:S(2)}) collective-permute-start(bf16[1056,128]{1,0:T(8,128)(2,1)} %carry_rows.1.refs_1_.refs_2_.refs_3_), channel_id=1, source_target_pairs={{0,4},{4,8},{8,12},{12,14},{14,10},{10,6},{6,2},{2,0},{1,5},{5,9},... | collective-permute-start | bytes 811016 | tf_op jit(solution)/shard_map/ppermute | solution.py:503
  17.6 23.1 %collective-permute-start.1 = (bf16[1024,128]{1,0:T(8,128)(2,1)}, bf16[1024,128]{1,0:T(8,128)(2,1)S(1)}, u32[]{:S(2)}, u32[]{:S(2)}) collective-permute-start(bf16[1024,128]{1,0:T(8,128)(2,1)} %collective-permute-done.refs_0_), channel_id=1, source_target_pairs={{0,4},{4,8},{8,12},{12,14},{14,10},{10,6},{6,2},{2,0},{1,5},{5,9},... | collective-permute-start | bytes 786440 | tf_op jit(solution)/shard_map/ppermute | solution.py:503
  20.4 20.2 %collective-permute-start.8 = (bf16[1056,128]{1,0:T(8,128)(2,1)S(1)}, bf16[1056,128]{1,0:T(8,128)(2,1)S(1)}, u32[]{:S(2)}, u32[]{:S(2)}) collective-permute-start(bf16[1056,128]{1,0:T(8,128)(2,1)S(1)} %collective-permute-done.4.refs_3_.refs_2_), channel_id=1, source_target_pairs={{4,0},{8,4},{12,8},{14,12},{10,14},{6,10},{2,6},{0,2},{5,1},{9,5},... | collective-permute-start | bytes 811016 | tf_op jit(solution)/shard_map/ppermute | solution.py:503
  22.3 2.8 %copy-start = (bf16[4,8,6,128,128]{4,3,2,1,0:T(8,128)(2,1)S(1)}, bf16[4,8,6,128,128]{4,3,2,1,0:T(8,128)(2,1)}, u32[]{:S(2)}) copy-start(bf16[4,8,6,128,128]{4,3,2,1,0:T(8,128)(2,1)} %refs_6_.15) | copy-start | bytes 18874372
  30.3 12.4 %collective-permute-start.9 = (bf16[1024,128]{1,0:T(8,128)(2,1)S(1)}, bf16[1024,128]{1,0:T(8,128)(2,1)S(1)}, u32[]{:S(2)}, u32[]{:S(2)}) collective-permute-start(bf16[1024,128]{1,0:T(8,128)(2,1)S(1)} %collective-permute-done.5.refs_2_), channel_id=1, source_target_pairs={{4,0},{8,4},{12,8},{14,12},{10,14},{6,10},{2,6},{0,2},{5,1},{9,5},... | collective-permute-start | bytes 786440 | tf_op jit(solution)/shard_map/ppermute | solution.py:503
  31.9 11.4 %collective-permute-start.7 = (bf16[1056,128]{1,0:T(8,128)(2,1)S(1)}, bf16[1056,128]{1,0:T(8,128)(2,1)S(1)}, u32[]{:S(2)}, u32[]{:S(2)}) collective-permute-start(bf16[1056,128]{1,0:T(8,128)(2,1)S(1)} %collective-permute-done.3.refs_1_.refs_0_), channel_id=1, source_target_pairs={{0,4},{4,8},{8,12},{12,14},{14,10},{10,6},{6,2},{2,0},{1,5},{5,9},... | collective-permute-start | bytes 811016 | tf_op jit(solution)/shard_map/ppermute | solution.py:503
  37.3 7.4 %copy-start.4 = (s32[113]{0:T(128)S(1)}, s32[113]{0:T(128)}, u32[]{:S(2)}) copy-start(s32[113]{0:T(128)} %plan.1.plan_ref) | copy-start | bytes 1360
  40.6 10.7 %collective-permute-start.11 = (bf16[1056,128]{1,0:T(8,128)(2,1)S(1)}, bf16[1056,128]{1,0:T(8,128)(2,1)S(1)}, u32[]{:S(2)}, u32[]{:S(2)}) collective-permute-start(bf16[1056,128]{1,0:T(8,128)(2,1)S(1)} %collective-permute-done.8.refs_3_.refs_2_), channel_id=1, source_target_pairs={{4,0},{8,4},{12,8},{14,12},{10,14},{6,10},{2,6},{0,2},{5,1},{9,5},... | collective-permute-start | bytes 811016 | tf_op jit(solution)/shard_map/ppermute | solution.py:503
  40.7 11.2 %collective-permute-start.6 = (bf16[1024,128]{1,0:T(8,128)(2,1)S(1)}, bf16[1024,128]{1,0:T(8,128)(2,1)S(1)}, u32[]{:S(2)}, u32[]{:S(2)}) collective-permute-start(bf16[1024,128]{1,0:T(8,128)(2,1)S(1)} %collective-permute-done.1.refs_0_), channel_id=1, source_target_pairs={{0,4},{4,8},{8,12},{12,14},{14,10},{10,6},{6,2},{2,0},{1,5},{5,9},... | collective-permute-start | bytes 786440 | tf_op jit(solution)/shard_map/ppermute | solution.py:503
  42.7 12.4 %collective-permute-start.14 = (bf16[1024,128]{1,0:T(8,128)(2,1)S(1)}, bf16[1024,128]{1,0:T(8,128)(2,1)S(1)}, u32[]{:S(2)}, u32[]{:S(2)}) collective-permute-start(bf16[1024,128]{1,0:T(8,128)(2,1)S(1)} %collective-permute-done.9.refs_2_), channel_id=1, source_target_pairs={{4,0},{8,4},{12,8},{14,12},{10,14},{6,10},{2,6},{0,2},{5,1},{9,5},... | collective-permute-start | bytes 786440 | tf_op jit(solution)/shard_map/ppermute | solution.py:503
  43.3 11.9 %collective-permute-start.13 = (bf16[1056,128]{1,0:T(8,128)(2,1)S(1)}, bf16[1056,128]{1,0:T(8,128)(2,1)S(1)}, u32[]{:S(2)}, u32[]{:S(2)}) collective-permute-start(bf16[1056,128]{1,0:T(8,128)(2,1)S(1)} %collective-permute-done.7.refs_1_.refs_0_), channel_id=1, source_target_pairs={{0,4},{4,8},{8,12},{12,14},{14,10},{10,6},{6,2},{2,0},{1,5},{5,9},... | collective-permute-start | bytes 811016 | tf_op jit(solution)/shard_map/ppermute | solution.py:503
  51.3 10.4 %collective-permute-start.12 = (bf16[1056,128]{1,0:T(8,128)(2,1)S(1)}, bf16[1056,128]{1,0:T(8,128)(2,1)S(1)}, u32[]{:S(2)}, u32[]{:S(2)}) collective-permute-start(bf16[1056,128]{1,0:T(8,128)(2,1)S(1)} %collective-permute-done.11.refs_3_.refs_2_), channel_id=1, source_target_pairs={{4,0},{8,4},{12,8},{14,12},{10,14},{6,10},{2,6},{0,2},{5,1},{9,5},... | collective-permute-start | bytes 811016 | tf_op jit(solution)/shard_map/ppermute | solution.py:503
  52.0 9.8 %collective-permute-start.10 = (bf16[1024,128]{1,0:T(8,128)(2,1)S(1)}, bf16[1024,128]{1,0:T(8,128)(2,1)S(1)}, u32[]{:S(2)}, u32[]{:S(2)}) collective-permute-start(bf16[1024,128]{1,0:T(8,128)(2,1)S(1)} %collective-permute-done.6.refs_0_), channel_id=1, source_target_pairs={{0,4},{4,8},{8,12},{12,14},{14,10},{10,6},{6,2},{2,0},{1,5},{5,9},... | collective-permute-start | bytes 786440 | tf_op jit(solution)/shard_map/ppermute | solution.py:503
  68.2 3.5 %collective-permute-start.17 = (bf16[4,4,6,64,128]{4,3,2,1,0:T(8,128)(2,1)S(1)}, bf16[4,4,6,64,128]{4,3,2,1,0:T(8,128)(2,1)S(1)}, u32[]{:S(2)}, u32[]{:S(2)}) collective-permute-start(bf16[4,4,6,64,128]{4,3,2,1,0:T(8,128)(2,1)S(1)} %get-tuple-element.69), channel_id=1, source_target_pairs={{0,1},{1,0},{2,3},{3,2},{4,5},{5,4},{6,7},{7,6},{8,9},{9,8},{10,11... | collective-permute-start | bytes 4718600 | tf_op jit(solution)/shard_map/ppermute | solution.py:530
  69.9 4.1 %collective-permute-start.15 = (bf16[4,4,6,64,128]{4,3,2,1,0:T(8,128)(2,1)S(1)}, bf16[4,4,6,64,128]{4,3,2,1,0:T(8,128)(2,1)S(1)}, u32[]{:S(2)}, u32[]{:S(2)}) collective-permute-start(bf16[4,4,6,64,128]{4,3,2,1,0:T(8,128)(2,1)S(1)} %get-tuple-element.65), channel_id=1, source_target_pairs={{0,1},{1,0},{2,3},{3,2},{4,5},{5,4},{6,7},{7,6},{8,9},{9,8},{10,11... | collective-permute-start | bytes 4718600 | tf_op jit(solution)/shard_map/ppermute | solution.py:535
  70.4 3.6 %collective-permute-start.16 = (f32[4,128]{1,0:T(4,128)S(1)}, f32[4,128]{1,0:T(4,128)S(1)}, u32[]{:S(2)}, u32[]{:S(2)}) collective-permute-start(f32[4,128]{1,0:T(4,128)S(1)} %get-tuple-element.67), channel_id=1, source_target_pairs={{0,1},{1,0},{2,3},{3,2},{4,5},{5,4},{6,7},{7,6},{8,9},{9,8},{10,11... | collective-permute-start | bytes 6152 | tf_op jit(solution)/shard_map/ppermute | solution.py:531
  (1 other events, 0.6 us)

commit v7 on v6

--- a/solution.py
+++ b/solution.py
@@ -172,12 +172,11 @@
     return (row * 256 + slot) * 256 + block
 
 
-def plan_kernel(shape, place_ref, col_ref, fill_ref, plan_ref):
+def plan_kernel(shape, col_ref, fill_ref, plan_ref):
     brows, slots, width, n, most = shape
-    own = place_ref[0]
-    entries = brows * slots
+    own = lax.axis_index("types")
     tail = n * (most + 1)
-    plan_ref[tail] = place_ref[1]
+    plan_ref[tail] = lax.axis_index("tm")
     for step in range(n):
         plan_ref[step * (most + 1)] = 0
 
@@ -188,7 +187,7 @@
 
         @pl.loop(0, fill)
         def _(slot):
-            column = col_ref[own * entries + row * slots + slot]
+            column = col_ref[own * brows + row, slot]
             source = lax.div(column, width)
             block = lax.rem(column, width)
             ahead = ring_place(source, n) - ring_place(own, n)
@@ -213,22 +212,23 @@
             plan_ref[base + count + 1] = code_of(brows, 0, 0)
 
 
-def make_plan(place, cols, fill, dims, width, n):
+def make_plan(cols, fill, dims, width, n):
     _, brows, slots, _ = dims
     most = 2 * max(2, brows * slots // n)
     return pl.pallas_call(
         functools.partial(plan_kernel, (brows, slots, width, n, most)),
-        in_specs=[SMEM] * 3,
+        in_specs=[SMEM] * 2,
         out_specs=SMEM,
         out_shape=jax.ShapeDtypeStruct((n * (most + 1) + 1 + brows,), jnp.int32),
+        compiler_params=PARAMS,
         name="plan",
-    )(place, cols, fill)
+    )(cols, fill)
 
 
 def start_kernel(tile, counts_ref, base_ref, total_ref):
     for row in range(total_ref.shape[0] - 1):
         at = slice(row * tile, (row + 1) * tile)
-        total_ref[row] = (base_ref[:, at] - counts_ref[:, at].astype(jnp.float32)).T
+        total_ref[row] = base_ref[:, at] - counts_ref[:, at].astype(jnp.float32)
     total_ref[total_ref.shape[0] - 1] = jnp.zeros(total_ref.shape[1:], jnp.float32)
 
 
@@ -238,7 +238,7 @@
         functools.partial(start_kernel, tile),
         in_specs=[VMEM, VMEM],
         out_specs=VMEM,
-        out_shape=jax.ShapeDtypeStruct((brows + 1, tile, counts.shape[0]), jnp.float32),
+        out_shape=jax.ShapeDtypeStruct((brows + 1, counts.shape[0], tile), jnp.float32),
         compiler_params=PARAMS,
         name="base_less_counts",
     )(counts, base_rate)
@@ -247,12 +247,36 @@
 def step_kernel(dims, n, call, seconds, plan_ref, *refs):
     basis, brows, slots, tile = dims
     lag_ref, power_ref, excite_ref = refs[4:7]
-    total_in, states_ref, total_ref, built_ref, held, sems = refs[-6:]
+    total_in, states_ref, total_ref, built_ref, held, weights, sems = refs[-7:]
     bins = lag_ref.shape[1]
     half = held.shape[0] // 2
     each = carry_rows(half, basis)
     most = (plan_ref.shape[0] - 1 - brows) // n - 1
     built_ref[...] = jnp.zeros_like(built_ref)
+    pairs = (plan_ref[call * (most + 1)] + 1) // 2
+
+    def entry_at(place):
+        code = plan_ref[call * (most + 1) + 1 + place]
+        return code >> 16, (code >> 8) & 255, code & 255
+
+    def weight_at(place):
+        row, slot, _ = entry_at(place)
+        return pltpu.make_async_copy(
+            excite_ref.at[:, jnp.minimum(row, brows - 1), slot],
+            weights.at[place],
+            sems.at[0, place],
+        )
+
+    def copy_at(place):
+        row, slot, block = entry_at(place)
+        return pltpu.make_async_copy(
+            held.at[block], states_ref.at[row * slots + slot], sems.at[1, place]
+        )
+
+    @pl.loop(0, 2 * pairs)
+    def _(place):
+        weight_at(place).start()
+
     total_ref[...] = total_in[...]
     for d in range(2):
         impact_ref, carry_ref = refs[2 * d : 2 * d + 2]
@@ -270,37 +294,18 @@
                         state[:, i * tile : (i + 1) * tile] + power_ref[b] * carry[row : row + 1]
                     ).astype(jnp.bfloat16)
 
-    def entry_at(place):
-        code = plan_ref[call * (most + 1) + 1 + place]
-        return code >> 16, (code >> 8) & 255, code & 255
-
-    def copy_at(place):
-        row, slot, block = entry_at(place)
-        return pltpu.make_async_copy(
-            held.at[block], states_ref.at[row * slots + slot], sems.at[place]
-        )
-
-    pairs = (plan_ref[call * (most + 1)] + 1) // 2
-
     @pl.loop(0, pairs)
     def _(k):
         terms = []
         for i in range(2):
-            row, slot, block = entry_at(2 * k + i)
+            row, _, block = entry_at(2 * k + i)
             copy_at(2 * k + i).start()
-            inside = jnp.minimum(row, brows - 1)
-            weight = jnp.concatenate([excite_ref[b, inside, slot] for b in range(basis)], axis=1)
-            terms.append(
-                (
-                    row,
-                    lax.dot_general(
-                        weight,
-                        held[block],
-                        (((1,), (1,)), ((), ())),
-                        preferred_element_type=jnp.float32,
-                    ),
-                )
+            weight_at(2 * k + i).wait()
+            weight = jnp.concatenate([weights[2 * k + i, b] for b in range(basis)], axis=1)
+            term = lax.dot_general(
+                held[block], weight, (((1,), (1,)), ((), ())), preferred_element_type=jnp.float32
             )
+            terms.append((row, term))
         for row, term in terms:
             total_ref[row] += term
 
@@ -317,7 +322,7 @@
     given = [total] if states is None else [states, total]
     return pl.pallas_call(
         functools.partial(step_kernel, dims, n, call, seconds),
-        in_specs=[SMEM] + [VMEM] * 7 + [ANYWHERE] * (len(given) - 1) + [VMEM],
+        in_specs=[SMEM] + [VMEM] * 6 + [ANYWHERE] * len(given) + [VMEM],
         out_specs=[ANYWHERE, VMEM, VMEM],
         out_shape=[
             jax.ShapeDtypeStruct((brows * slots + 1, bins, basis * tile), jnp.bfloat16),
@@ -326,7 +331,8 @@
         ],
         scratch_shapes=[
             pltpu.VMEM((2 * half, bins, basis * tile), jnp.bfloat16),
-            pltpu.SemaphoreType.DMA((most,)),
+            pltpu.VMEM((most, basis, tile, tile), jnp.bfloat16),
+            pltpu.SemaphoreType.DMA((2, most)),
         ],
         input_output_aliases={} if states is None else {8: 0},
         compiler_params=PARAMS,
@@ -369,16 +375,8 @@
     rates = []
     for row in range(brows):
         weighted = (2.0 / overall) * total_ref[row]
-        rates.append(
-            lax.dot_general(
-                jnp.ones((8, weighted.shape[1]), jnp.float32),
-                weighted,
-                (((1,), (1,)), ((), ())),
-                precision=lax.Precision.HIGHEST,
-                preferred_element_type=jnp.float32,
-            )[:1]
-        )
-        weighted = weighted.astype(jnp.bfloat16)
+        rates.append(jnp.sum(weighted, axis=0, keepdims=True))
+        weighted = weighted.T.astype(jnp.bfloat16)
         upper, lower = weighted[:part], weighted[part:]
         turned_ref[row, :part] = jnp.where(half == 0, upper, lower)
         turned_ref[row, part:] = jnp.where(half == 0, lower, upper)
@@ -400,7 +398,7 @@
 
 def first_products(plan, total, states, dims, overall):
     _, brows, _, tile = dims
-    turned = jax.ShapeDtypeStruct((brows, tile, total.shape[2]), jnp.bfloat16)
+    turned = jax.ShapeDtypeStruct((brows, tile, total.shape[1]), jnp.bfloat16)
     rate = jax.ShapeDtypeStruct((brows // 2, tile), jnp.float32)
     return pl.pallas_call(
         functools.partial(weighted_kernel, dims, overall),
@@ -474,7 +472,6 @@
     bins = counts.shape[0]
     overall = bins * lax.axis_size("tm")
     n = lax.axis_size("types")
-    place = jnp.stack([lax.axis_index("types"), lax.axis_index("tm")]).astype(jnp.int32)
     order = list(range(0, n, 2)) + list(range(1, n, 2))[::-1]
     up = [(order[i], order[(i + 1) % n]) for i in range(n)]
     down = [(b, a) for a, b in up]
@@ -484,7 +481,7 @@
     enter = lax.ppermute(ends, "tm", [(0, 1)])
     two = add_carry(enter, two, basis, bins)
     lag, power = lag_tables(bins, basis, overall, tile)
-    plan = make_plan(place, block_col.reshape(-1), row_fill, dims, counts.shape[1] // tile, n)
+    plan = make_plan(block_col, row_fill, dims, counts.shape[1] // tile, n)
     total = start_total(counts, base_rate.reshape(1, -1), dims)
 
     states = None

time: 76.3 us -> 74.1 us (0.971)
  local copies, waits for them, and re-layouts: 4.43 us -> 3.09 us
    ppermute x14, waiting for transfers between devices: 2.54 us -> 1.75 us  [send(): return lax.ppermute(message, 'types', way)]
    unnamed x15 -> x13, local copies, waits for them, and re-layouts: 3.52 us -> 2.9 us
  transfers between devices with their start and end apart: 18 -> 18, of which waited for: 5 -> 5; matrix products, arithmetic and copies ran while one was open for 3% -> 1% of each run, Pallas kernels for 45% -> 49%
where the time goes in v7:
time: 74.1 us; the launch traced here: 73.2 us
  Pallas kernels  44.4 us (60%)
  starting transfers between devices  19.3 us (26%)
  waiting for transfers between devices  4.71 us (6%)
  local copies, waits for them, and re-layouts  3.09 us (4%)
  between operations  1.1 us (1%)
    pallas_call x8, Pallas kernels, take_step(): pl.pallas_call(functools.partial(step_kernel, dims, n, call, seconds), in...  30 us
    ppermute x14, starting transfers between devices, send(): return lax.ppermute(message, 'types', way)  17.2 us
    pallas_call x2, Pallas kernels, add_received(): pl.pallas_call(functools.partial(add_kernel, dims, group), in_specs=[VMEM...  3.15 us
    unnamed x13, local copies, waits for them, and re-layouts  2.9 us
    pallas_call x1, Pallas kernels, make_plan(): pl.pallas_call(functools.partial(plan_kernel, (brows, slots, width, n, mo...  2.88 us
    pallas_call x1, Pallas kernels, impact_messages(): pl.pallas_call(functools.partial(second_kernel, basis, tile, overall), in...  2.46 us
    pallas_call x1, Pallas kernels, impact_messages(): pl.pallas_call(first_kernel, in_specs=[ANYWHERE, ANYWHERE], out_specs=VME...  1.98 us
    ppermute x14, waiting for transfers between devices, send(): return lax.ppermute(message, 'types', way)  1.75 us
  transfers between devices with their start and end apart: 18, of which 5 were waited for; matrix products, arithmetic and copies ran while one was open for 1% of the time, Pallas kernels for 49%

profile of v7, /device:TPU:0, one launch (start us, length us, event | category | flops | bytes accessed | tf_op | source)
XLA Modules:
  0.0 73.2 jit_solution(12206894248381114402)
XLA Ops:
  0.7 2.0 %first_message.1.refs_0_ = bf16[1024,128]{1,0:T(8,128)(2,1)} custom-call(s32[256,1024]{1,0:T(8,128)} %counts_ref.1, bf16[256,1024]{1,0:T(8,128)(2,1)} %mark_hbm.3), custom_call_target="tpu_custom_call" | custom-call | tf_op jit(solution)/shard_map/first_message/pallas_call | solution.py:102
  2.7 3.1 %collective-permute-start = (bf16[1024,128]{1,0:T(8,128)(2,1)}, bf16[1024,128]{1,0:T(8,128)(2,1)S(1)}, u32[]{:S(2)}, u32[]{:S(2)}) collective-permute-start(bf16[1024,128]{1,0:T(8,128)(2,1)} %first_message.1.refs_0_), channel_id=1, source_target_pairs={{0,4},{4,8},{8,12},{12,14},{14,10},{10,6},{6,2},{2,0},{1,5},{5,9},... | collective-permute-start | bytes 786440 | tf_op jit(solution)/shard_map/ppermute | solution.py:500
  5.8 2.5 %second_message.1 = (bf16[1056,128]{1,0:T(8,128)(2,1)}, f32[4,1024]{1,0:T(4,128)}) custom-call(s32[256,1024]{1,0:T(8,128)} %counts_ref.1, bf16[256,1024]{1,0:T(8,128)(2,1)} %mark_hbm.3), custom_call_target="tpu_custom_call" | custom-call | tf_op jit(solution)/shard_map/second_message/pallas_call | solution.py:115
  8.2 1.5 %collective-permute-start.2 = (f32[4,1024]{1,0:T(4,128)}, f32[4,1024]{1,0:T(4,128)S(1)}, u32[]{:S(2)}, u32[]{:S(2)}) collective-permute-start(f32[4,1024]{1,0:T(4,128)} %get-tuple-element.37), channel_id=1, source_target_pairs={{0,1},{2,3},{4,5},{6,7},{8,9},{10,11},{12,13},{14,15},{16,17},{18,... | collective-permute-start | bytes 49160 | tf_op jit(solution)/shard_map/ppermute | solution.py:481
  11.3 1.8 %collective-permute-start.4 = (bf16[1056,128]{1,0:T(8,128)(2,1)}, bf16[1056,128]{1,0:T(8,128)(2,1)S(1)}, u32[]{:S(2)}, u32[]{:S(2)}) collective-permute-start(bf16[1056,128]{1,0:T(8,128)(2,1)} %carry_rows.1.refs_1_.refs_2_.refs_3_), channel_id=1, source_target_pairs={{4,0},{8,4},{12,8},{14,12},{10,14},{6,10},{2,6},{0,2},{5,1},{9,5},... | collective-permute-start | bytes 811016 | tf_op jit(solution)/shard_map/ppermute | solution.py:500
  13.7 2.9 %plan.1.plan_ref = s32[113]{0:T(128)S(1)} custom-call(s32[64,6]{1,0:T(8,128)S(1)} %copy.17.col_ref, s32[64]{0:T(128)S(1)} %copy-done.4), custom_call_target="tpu_custom_call" | custom-call | tf_op jit(solution)/shard_map/plan/pallas_call | solution.py:218
  16.9 2.1 %collective-permute-start.1 = (bf16[1024,128]{1,0:T(8,128)(2,1)S(1)}, bf16[1024,128]{1,0:T(8,128)(2,1)S(1)}, u32[]{:S(2)}, u32[]{:S(2)}) collective-permute-start(bf16[1024,128]{1,0:T(8,128)(2,1)S(1)} %collective-permute-done.refs_0_), channel_id=1, source_target_pairs={{0,4},{4,8},{8,12},{12,14},{14,10},{10,6},{6,2},{2,0},{1,5},{5,9},... | collective-permute-start | bytes 786440 | tf_op jit(solution)/shard_map/ppermute | solution.py:500
  19.0 1.5 %collective-permute-done.4.refs_3_.refs_2_ = bf16[1056,128]{1,0:T(8,128)(2,1)S(1)} collective-permute-done((bf16[1056,128]{1,0:T(8,128)(2,1)}, bf16[1056,128]{1,0:T(8,128)(2,1)S(1)}, u32[]{:S(2)}, u32[]{:S(2)}) %collective-permute-start.4) | collective-permute-done | bytes 270368 | tf_op jit(solution)/shard_map/ppermute | solution.py:500
  20.4 1.7 %collective-permute-start.8 = (bf16[1056,128]{1,0:T(8,128)(2,1)S(1)}, bf16[1056,128]{1,0:T(8,128)(2,1)S(1)}, u32[]{:S(2)}, u32[]{:S(2)}) collective-permute-start(bf16[1056,128]{1,0:T(8,128)(2,1)S(1)} %collective-permute-done.4.refs_3_.refs_2_), channel_id=1, source_target_pairs={{4,0},{8,4},{12,8},{14,12},{10,14},{6,10},{2,6},{0,2},{5,1},{9,5},... | collective-permute-start | bytes 811016 | tf_op jit(solution)/shard_map/ppermute | solution.py:500
  22.3 2.8 %copy-done = bf16[4,8,6,128,128]{4,3,2,1,0:T(8,128)(2,1)S(1)} copy-done((bf16[4,8,6,128,128]{4,3,2,1,0:T(8,128)(2,1)S(1)}, bf16[4,8,6,128,128]{4,3,2,1,0:T(8,128)(2,1)}, u32[]{:S(2)}) %copy-start) | copy-done | bytes 6291480
  25.1 4.7 %ring_step.8 = (bf16[49,256,512]{2,1,0:T(8,128)(2,1)S(1)}, f32[9,256,128]{2,1,0:T(8,128)S(1)}, f32[8,128]{1,0:T(8,128)}) custom-call(s32[113]{0:T(128)S(1)} %plan.1.plan_ref, bf16[1024,128]{1,0:T(8,128)(2,1)S(1)} %copy-done.2, bf16[1056,128]{1,0:T(8,128)(2,1)} %carry_rows.1.refs_1_.refs_2_.refs_3_, bf16[1056,128]{1,0:T(8,128)(2,1)} %carry_rows.1.refs_1_.refs_2_.refs_3_, ...), custom_call_target="tpu_custom_call" | custom-call | flops 1073741824 | bytes 4194304 | tf_op jit(solution)/shard_map/ring_step/pallas_call | solution.py:323
  31.9 3.4 %ring_step.9 = (bf16[49,256,512]{2,1,0:T(8,128)(2,1)S(1)}, f32[9,256,128]{2,1,0:T(8,128)S(1)}, f32[8,128]{1,0:T(8,128)}) custom-call(s32[113]{0:T(128)S(1)} %plan.1.plan_ref, bf16[1024,128]{1,0:T(8,128)(2,1)S(1)} %collective-permute-done.refs_0_, bf16[1056,128]{1,0:T(8,128)(2,1)S(1)} %collective-permute-done.3.refs_1_.refs_0_, ...), custom_call_target="tpu_custom_call", output_to_operand_aliasing={{0}: (8, {})} | custom-call | flops 1073741824 | bytes 4194304 | tf_op jit(solution)/shard_map/ring_step/pallas_call | solution.py:323
  35.4 4.0 %ring_step.10 = (bf16[49,256,512]{2,1,0:T(8,128)(2,1)S(1)}, f32[9,256,128]{2,1,0:T(8,128)S(1)}, f32[8,128]{1,0:T(8,128)}) custom-call(s32[113]{0:T(128)S(1)} %plan.1.plan_ref, bf16[1056,128]{1,0:T(8,128)(2,1)S(1)} %collective-permute-done.3.refs_1_.refs_0_, ...), custom_call_target="tpu_custom_call", output_to_operand_aliasing={{0}: (8, {})} | custom-call | flops 1073741824 | bytes 4194304 | tf_op jit(solution)/shard_map/ring_step/pallas_call | solution.py:323
  39.8 1.7 %collective-permute-start.6 = (bf16[1024,128]{1,0:T(8,128)(2,1)S(1)}, bf16[1024,128]{1,0:T(8,128)(2,1)S(1)}, u32[]{:S(2)}, u32[]{:S(2)}) collective-permute-start(bf16[1024,128]{1,0:T(8,128)(2,1)S(1)} %collective-permute-done.1.refs_0_), channel_id=1, source_target_pairs={{0,4},{4,8},{8,12},{12,14},{14,10},{10,6},{6,2},{2,0},{1,5},{5,9},... | collective-permute-start | bytes 786440 | tf_op jit(solution)/shard_map/ppermute | solution.py:500
  42.2 1.3 %collective-permute-start.13 = (bf16[1056,128]{1,0:T(8,128)(2,1)S(1)}, bf16[1056,128]{1,0:T(8,128)(2,1)S(1)}, u32[]{:S(2)}, u32[]{:S(2)}) collective-permute-start(bf16[1056,128]{1,0:T(8,128)(2,1)S(1)} %collective-permute-done.7.refs_1_.refs_0_), channel_id=1, source_target_pairs={{0,4},{4,8},{8,12},{12,14},{14,10},{10,6},{6,2},{2,0},{1,5},{5,9},... | collective-permute-start | bytes 811016 | tf_op jit(solution)/shard_map/ppermute | solution.py:500
  43.5 4.0 %ring_step.11 = (bf16[49,256,512]{2,1,0:T(8,128)(2,1)S(1)}, f32[9,256,128]{2,1,0:T(8,128)S(1)}, f32[8,128]{1,0:T(8,128)}) custom-call(s32[113]{0:T(128)S(1)} %plan.1.plan_ref, bf16[1024,128]{1,0:T(8,128)(2,1)S(1)} %collective-permute-done.1.refs_0_, bf16[1056,128]{1,0:T(8,128)(2,1)S(1)} %collective-permute-done.7.refs_1_.refs_0_, ...), custom_call_target="tpu_custom_call", output_to_operand_aliasing={{0}: (8, {})} | custom-call | flops 1073741824 | bytes 4194304 | tf_op jit(solution)/shard_map/ring_step/pallas_call | solution.py:323
  47.6 3.4 %ring_step.12 = (bf16[49,256,512]{2,1,0:T(8,128)(2,1)S(1)}, f32[9,256,128]{2,1,0:T(8,128)S(1)}, f32[8,128]{1,0:T(8,128)}) custom-call(s32[113]{0:T(128)S(1)} %plan.1.plan_ref, bf16[1056,128]{1,0:T(8,128)(2,1)S(1)} %collective-permute-done.7.refs_1_.refs_0_, ...), custom_call_target="tpu_custom_call", output_to_operand_aliasing={{0}: (8, {})} | custom-call | flops 1073741824 | bytes 4194304 | tf_op jit(solution)/shard_map/ring_step/pallas_call | solution.py:323
  51.0 1.4 %collective-permute-start.12 = (bf16[1056,128]{1,0:T(8,128)(2,1)S(1)}, bf16[1056,128]{1,0:T(8,128)(2,1)S(1)}, u32[]{:S(2)}, u32[]{:S(2)}) collective-permute-start(bf16[1056,128]{1,0:T(8,128)(2,1)S(1)} %collective-permute-done.11.refs_3_.refs_2_), channel_id=1, source_target_pairs={{4,0},{8,4},{12,8},{14,12},{10,14},{6,10},{2,6},{0,2},{5,1},{9,5},... | collective-permute-start | bytes 811016 | tf_op jit(solution)/shard_map/ppermute | solution.py:500
  53.3 3.4 %ring_step.13 = (bf16[49,256,512]{2,1,0:T(8,128)(2,1)S(1)}, f32[9,256,128]{2,1,0:T(8,128)S(1)}, f32[8,128]{1,0:T(8,128)}) custom-call(s32[113]{0:T(128)S(1)} %plan.1.plan_ref, bf16[1024,128]{1,0:T(8,128)(2,1)S(1)} %collective-permute-done.6.refs_0_, bf16[1056,128]{1,0:T(8,128)(2,1)S(1)} %collective-permute-done.13.refs_1_.refs_0_, ...), custom_call_target="tpu_custom_call", output_to_operand_aliasing={{0}: (8, {})} | custom-call | flops 1073741824 | bytes 4194304 | tf_op jit(solution)/shard_map/ring_step/pallas_call | solution.py:323
  56.8 4.0 %ring_step.14 = (bf16[49,256,512]{2,1,0:T(8,128)(2,1)S(1)}, f32[9,256,128]{2,1,0:T(8,128)S(1)}, f32[8,128]{1,0:T(8,128)}) custom-call(s32[113]{0:T(128)S(1)} %plan.1.plan_ref, bf16[1056,128]{1,0:T(8,128)(2,1)S(1)} %collective-permute-done.13.refs_1_.refs_0_, ...), custom_call_target="tpu_custom_call", output_to_operand_aliasing={{0}: (8, {})} | custom-call | flops 1073741824 | bytes 4194304 | tf_op jit(solution)/shard_map/ring_step/pallas_call | solution.py:323
  60.8 3.0 %ring_step.15 = (bf16[49,256,512]{2,1,0:T(8,128)(2,1)S(1)}, f32[9,256,128]{2,1,0:T(8,128)S(1)}, f32[8,128]{1,0:T(8,128)}) custom-call(s32[113]{0:T(128)S(1)} %plan.1.plan_ref, bf16[1024,128]{1,0:T(8,128)(2,1)S(1)} %collective-permute-done.10.refs_0_, ...), custom_call_target="tpu_custom_call", output_to_operand_aliasing={{0}: (8, {})} | custom-call | flops 1073741824 | bytes 4194304 | tf_op jit(solution)/shard_map/ring_step/pallas_call | solution.py:323
  63.8 1.6 %weighted_products.1 = (bf16[4,4,6,64,128]{4,3,2,1,0:T(8,128)(2,1)S(1)}, f32[4,4,6,64,128]{4,3,2,1,0:T(8,128)S(1)}, bf16[8,128,256]{2,1,0:T(8,128)(2,1)S(1)}, f32[4,128]{1,0:T(4,128)S(1)}, f32[4,128]{1,0:T(4,128)S(1)}) custom-call(s32[113]{0:T(128)S(1)} %plan.1.plan_ref, f32[9,256,128]{2,1,0:T(8,128)S(1)} %get-tuple-element.61.total_ref, ...), custom_call_target="tpu_custom_call" | custom-call | tf_op jit(solution)/shard_map/weighted_products/pallas_call | solution.py:403
  65.5 1.5 %products.1 = (bf16[4,4,6,64,128]{4,3,2,1,0:T(8,128)(2,1)S(1)}, f32[4,4,6,64,128]{4,3,2,1,0:T(8,128)S(1)}) custom-call(s32[113]{0:T(128)S(1)} %plan.1.plan_ref, bf16[8,128,256]{2,1,0:T(8,128)(2,1)S(1)} %get-tuple-element.63.turned_ref, bf16[49,256,512]{2,1,0:T(8,128)(2,1)S(1)} %get-tuple-element.62.states_ref), custom_call_target="tpu_custom_call" | custom-call | tf_op jit(solution)/shard_map/products/pallas_call | solution.py:420
  71.2 1.9 %add_received.3 = (bf16[4,8,6,64,128]{4,3,2,1,0:T(8,128)(2,1)}, f32[4,128]{1,0:T(4,128)}) custom-call(f32[4,4,6,64,128]{4,3,2,1,0:T(8,128)S(1)} %get-tuple-element.64.kept_ref, bf16[4,4,6,64,128]{4,3,2,1,0:T(8,128)(2,1)S(1)} %collective-permute-done.15.got_ref, f32[4,128]{1,0:T(4,128)S(1)} %get-tuple-element.66.refs_0_, ...), custom_call_target="tpu_custom_call", output_to_operand_aliasing={{0}: (4, {})} | custom-call | tf_op jit(solution)/shard_map/add_received/pallas_call | solution.py:454
  (49 shorter events, 10.9 us)
Async XLA Ops:
  0.6 13.0 %copy-start.1 = (s32[256,1024]{1,0:T(8,128)S(1)}, s32[256,1024]{1,0:T(8,128)}, u32[]{:S(2)}) copy-start(s32[256,1024]{1,0:T(8,128)} %counts_ref.1) | copy-start | bytes 3145732
  0.6 12.8 %copy-start.5 = (s32[64,6]{0,1:T(8,128)S(1)}, s32[64,6]{0,1:T(8,128)}, u32[]{:S(2)}) copy-start(s32[64,6]{0,1:T(8,128)} %param.10) | copy-start | bytes 4612
  0.7 12.9 %copy-start.3 = (f32[1024]{0:T(1024)S(1)}, f32[1024]{0:T(1024)}, u32[]{:S(2)}) copy-start(f32[1024]{0:T(1024)} %param.8) | copy-start | bytes 12292
  2.6 11.1 %copy-start.4 = (s32[64]{0:T(128)S(1)}, s32[64]{0:T(128)}, u32[]{:S(2)}) copy-start(s32[64]{0:T(128)} %fill_ref.1) | copy-start | bytes 772
  2.7 19.7 %copy-start.2 = (bf16[1024,128]{1,0:T(8,128)(2,1)S(1)}, bf16[1024,128]{1,0:T(8,128)(2,1)}, u32[]{:S(2)}) copy-start(bf16[1024,128]{1,0:T(8,128)(2,1)} %first_message.1.refs_0_) | copy-start | bytes 786436
  2.7 14.2 %collective-permute-start = (bf16[1024,128]{1,0:T(8,128)(2,1)}, bf16[1024,128]{1,0:T(8,128)(2,1)S(1)}, u32[]{:S(2)}, u32[]{:S(2)}) collective-permute-start(bf16[1024,128]{1,0:T(8,128)(2,1)} %first_message.1.refs_0_), channel_id=1, source_target_pairs={{0,4},{4,8},{8,12},{12,14},{14,10},{10,6},{6,2},{2,0},{1,5},{5,9},... | collective-permute-start | bytes 786440 | tf_op jit(solution)/shard_map/ppermute | solution.py:500
  5.7 24.1 %collective-permute-start.5 = (bf16[1024,128]{1,0:T(8,128)(2,1)}, bf16[1024,128]{1,0:T(8,128)(2,1)S(1)}, u32[]{:S(2)}, u32[]{:S(2)}) collective-permute-start(bf16[1024,128]{1,0:T(8,128)(2,1)} %first_message.1.refs_0_), channel_id=1, source_target_pairs={{4,0},{8,4},{12,8},{14,12},{10,14},{6,10},{2,6},{0,2},{5,1},{9,5},... | collective-permute-start | bytes 786440 | tf_op jit(solution)/shard_map/ppermute | solution.py:500
  8.2 2.5 %collective-permute-start.2 = (f32[4,1024]{1,0:T(4,128)}, f32[4,1024]{1,0:T(4,128)S(1)}, u32[]{:S(2)}, u32[]{:S(2)}) collective-permute-start(f32[4,1024]{1,0:T(4,128)} %get-tuple-element.37), channel_id=1, source_target_pairs={{0,1},{2,3},{4,5},{6,7},{8,9},{10,11},{12,13},{14,15},{16,17},{18,... | collective-permute-start | bytes 49160 | tf_op jit(solution)/shard_map/ppermute | solution.py:481
  11.3 9.1 %collective-permute-start.4 = (bf16[1056,128]{1,0:T(8,128)(2,1)}, bf16[1056,128]{1,0:T(8,128)(2,1)S(1)}, u32[]{:S(2)}, u32[]{:S(2)}) collective-permute-start(bf16[1056,128]{1,0:T(8,128)(2,1)} %carry_rows.1.refs_1_.refs_2_.refs_3_), channel_id=1, source_target_pairs={{4,0},{8,4},{12,8},{14,12},{10,14},{6,10},{2,6},{0,2},{5,1},{9,5},... | collective-permute-start | bytes 811016 | tf_op jit(solution)/shard_map/ppermute | solution.py:500
  16.6 14.3 %collective-permute-start.3 = (bf16[1056,128]{1,0:T(8,128)(2,1)}, bf16[1056,128]{1,0:T(8,128)(2,1)S(1)}, u32[]{:S(2)}, u32[]{:S(2)}) collective-permute-start(bf16[1056,128]{1,0:T(8,128)(2,1)} %carry_rows.1.refs_1_.refs_2_.refs_3_), channel_id=1, source_target_pairs={{0,4},{4,8},{8,12},{12,14},{14,10},{10,6},{6,2},{2,0},{1,5},{5,9},... | collective-permute-start | bytes 811016 | tf_op jit(solution)/shard_map/ppermute | solution.py:500
  16.9 22.9 %collective-permute-start.1 = (bf16[1024,128]{1,0:T(8,128)(2,1)S(1)}, bf16[1024,128]{1,0:T(8,128)(2,1)S(1)}, u32[]{:S(2)}, u32[]{:S(2)}) collective-permute-start(bf16[1024,128]{1,0:T(8,128)(2,1)S(1)} %collective-permute-done.refs_0_), channel_id=1, source_target_pairs={{0,4},{4,8},{8,12},{12,14},{14,10},{10,6},{6,2},{2,0},{1,5},{5,9},... | collective-permute-start | bytes 786440 | tf_op jit(solution)/shard_map/ppermute | solution.py:500
  20.4 19.0 %collective-permute-start.8 = (bf16[1056,128]{1,0:T(8,128)(2,1)S(1)}, bf16[1056,128]{1,0:T(8,128)(2,1)S(1)}, u32[]{:S(2)}, u32[]{:S(2)}) collective-permute-start(bf16[1056,128]{1,0:T(8,128)(2,1)S(1)} %collective-permute-done.4.refs_3_.refs_2_), channel_id=1, source_target_pairs={{4,0},{8,4},{12,8},{14,12},{10,14},{6,10},{2,6},{0,2},{5,1},{9,5},... | collective-permute-start | bytes 811016 | tf_op jit(solution)/shard_map/ppermute | solution.py:500
  22.3 2.8 %copy-start = (bf16[4,8,6,128,128]{4,3,2,1,0:T(8,128)(2,1)S(1)}, bf16[4,8,6,128,128]{4,3,2,1,0:T(8,128)(2,1)}, u32[]{:S(2)}) copy-start(bf16[4,8,6,128,128]{4,3,2,1,0:T(8,128)(2,1)} %refs_6_.15) | copy-start | bytes 18874372
  29.8 11.7 %collective-permute-start.9 = (bf16[1024,128]{1,0:T(8,128)(2,1)S(1)}, bf16[1024,128]{1,0:T(8,128)(2,1)S(1)}, u32[]{:S(2)}, u32[]{:S(2)}) collective-permute-start(bf16[1024,128]{1,0:T(8,128)(2,1)S(1)} %collective-permute-done.5.refs_2_), channel_id=1, source_target_pairs={{4,0},{8,4},{12,8},{14,12},{10,14},{6,10},{2,6},{0,2},{5,1},{9,5},... | collective-permute-start | bytes 786440 | tf_op jit(solution)/shard_map/ppermute | solution.py:500
  30.9 11.4 %collective-permute-start.7 = (bf16[1056,128]{1,0:T(8,128)(2,1)S(1)}, bf16[1056,128]{1,0:T(8,128)(2,1)S(1)}, u32[]{:S(2)}, u32[]{:S(2)}) collective-permute-start(bf16[1056,128]{1,0:T(8,128)(2,1)S(1)} %collective-permute-done.3.refs_1_.refs_0_), channel_id=1, source_target_pairs={{0,4},{4,8},{8,12},{12,14},{14,10},{10,6},{6,2},{2,0},{1,5},{5,9},... | collective-permute-start | bytes 811016 | tf_op jit(solution)/shard_map/ppermute | solution.py:500
  39.4 11.6 %collective-permute-start.11 = (bf16[1056,128]{1,0:T(8,128)(2,1)S(1)}, bf16[1056,128]{1,0:T(8,128)(2,1)S(1)}, u32[]{:S(2)}, u32[]{:S(2)}) collective-permute-start(bf16[1056,128]{1,0:T(8,128)(2,1)S(1)} %collective-permute-done.8.refs_3_.refs_2_), channel_id=1, source_target_pairs={{4,0},{8,4},{12,8},{14,12},{10,14},{6,10},{2,6},{0,2},{5,1},{9,5},... | collective-permute-start | bytes 811016 | tf_op jit(solution)/shard_map/ppermute | solution.py:500
  39.8 12.6 %collective-permute-start.6 = (bf16[1024,128]{1,0:T(8,128)(2,1)S(1)}, bf16[1024,128]{1,0:T(8,128)(2,1)S(1)}, u32[]{:S(2)}, u32[]{:S(2)}) collective-permute-start(bf16[1024,128]{1,0:T(8,128)(2,1)S(1)} %collective-permute-done.1.refs_0_), channel_id=1, source_target_pairs={{0,4},{4,8},{8,12},{12,14},{14,10},{10,6},{6,2},{2,0},{1,5},{5,9},... | collective-permute-start | bytes 786440 | tf_op jit(solution)/shard_map/ppermute | solution.py:500
  41.5 11.6 %collective-permute-start.14 = (bf16[1024,128]{1,0:T(8,128)(2,1)S(1)}, bf16[1024,128]{1,0:T(8,128)(2,1)S(1)}, u32[]{:S(2)}, u32[]{:S(2)}) collective-permute-start(bf16[1024,128]{1,0:T(8,128)(2,1)S(1)} %collective-permute-done.9.refs_2_), channel_id=1, source_target_pairs={{4,0},{8,4},{12,8},{14,12},{10,14},{6,10},{2,6},{0,2},{5,1},{9,5},... | collective-permute-start | bytes 786440 | tf_op jit(solution)/shard_map/ppermute | solution.py:500
  42.2 11.1 %collective-permute-start.13 = (bf16[1056,128]{1,0:T(8,128)(2,1)S(1)}, bf16[1056,128]{1,0:T(8,128)(2,1)S(1)}, u32[]{:S(2)}, u32[]{:S(2)}) collective-permute-start(bf16[1056,128]{1,0:T(8,128)(2,1)S(1)} %collective-permute-done.7.refs_1_.refs_0_), channel_id=1, source_target_pairs={{0,4},{4,8},{8,12},{12,14},{14,10},{10,6},{6,2},{2,0},{1,5},{5,9},... | collective-permute-start | bytes 811016 | tf_op jit(solution)/shard_map/ppermute | solution.py:500
  51.0 9.8 %collective-permute-start.12 = (bf16[1056,128]{1,0:T(8,128)(2,1)S(1)}, bf16[1056,128]{1,0:T(8,128)(2,1)S(1)}, u32[]{:S(2)}, u32[]{:S(2)}) collective-permute-start(bf16[1056,128]{1,0:T(8,128)(2,1)S(1)} %collective-permute-done.11.refs_3_.refs_2_), channel_id=1, source_target_pairs={{4,0},{8,4},{12,8},{14,12},{10,14},{6,10},{2,6},{0,2},{5,1},{9,5},... | collective-permute-start | bytes 811016 | tf_op jit(solution)/shard_map/ppermute | solution.py:500
  52.4 8.4 %collective-permute-start.10 = (bf16[1024,128]{1,0:T(8,128)(2,1)S(1)}, bf16[1024,128]{1,0:T(8,128)(2,1)S(1)}, u32[]{:S(2)}, u32[]{:S(2)}) collective-permute-start(bf16[1024,128]{1,0:T(8,128)(2,1)S(1)} %collective-permute-done.6.refs_0_), channel_id=1, source_target_pairs={{0,4},{4,8},{8,12},{12,14},{14,10},{10,6},{6,2},{2,0},{1,5},{5,9},... | collective-permute-start | bytes 786440 | tf_op jit(solution)/shard_map/ppermute | solution.py:500
  65.4 3.5 %collective-permute-start.17 = (bf16[4,4,6,64,128]{4,3,2,1,0:T(8,128)(2,1)S(1)}, bf16[4,4,6,64,128]{4,3,2,1,0:T(8,128)(2,1)S(1)}, u32[]{:S(2)}, u32[]{:S(2)}) collective-permute-start(bf16[4,4,6,64,128]{4,3,2,1,0:T(8,128)(2,1)S(1)} %get-tuple-element.69), channel_id=1, source_target_pairs={{0,1},{1,0},{2,3},{3,2},{4,5},{5,4},{6,7},{7,6},{8,9},{9,8},{10,11... | collective-permute-start | bytes 4718600 | tf_op jit(solution)/shard_map/ppermute | solution.py:527
  67.1 4.1 %collective-permute-start.15 = (bf16[4,4,6,64,128]{4,3,2,1,0:T(8,128)(2,1)S(1)}, bf16[4,4,6,64,128]{4,3,2,1,0:T(8,128)(2,1)S(1)}, u32[]{:S(2)}, u32[]{:S(2)}) collective-permute-start(bf16[4,4,6,64,128]{4,3,2,1,0:T(8,128)(2,1)S(1)} %get-tuple-element.65), channel_id=1, source_target_pairs={{0,1},{1,0},{2,3},{3,2},{4,5},{5,4},{6,7},{7,6},{8,9},{9,8},{10,11... | collective-permute-start | bytes 4718600 | tf_op jit(solution)/shard_map/ppermute | solution.py:532
  67.6 3.5 %collective-permute-start.16 = (f32[4,128]{1,0:T(4,128)S(1)}, f32[4,128]{1,0:T(4,128)S(1)}, u32[]{:S(2)}, u32[]{:S(2)}) collective-permute-start(f32[4,128]{1,0:T(4,128)S(1)} %get-tuple-element.67), channel_id=1, source_target_pairs={{0,1},{1,0},{2,3},{3,2},{4,5},{5,4},{6,7},{7,6},{8,9},{9,8},{10,11... | collective-permute-start | bytes 6152 | tf_op jit(solution)/shard_map/ppermute | solution.py:528

commit v8 on v7

--- a/solution.py
+++ b/solution.py
@@ -175,9 +175,10 @@
 def plan_kernel(shape, col_ref, fill_ref, plan_ref):
     brows, slots, width, n, most = shape
     own = lax.axis_index("types")
-    tail = n * (most + 1)
+    calls = n // 2 + 1
+    tail = calls * (most + 1)
     plan_ref[tail] = lax.axis_index("tm")
-    for step in range(n):
+    for step in range(calls):
         plan_ref[step * (most + 1)] = 0
 
     @pl.loop(0, brows)
@@ -192,18 +193,14 @@
             block = lax.rem(column, width)
             ahead = ring_place(source, n) - ring_place(own, n)
             ahead = jnp.where(ahead < 0, ahead + n, ahead)
-            second = (block >= width // 2).astype(jnp.int32)
-            whole = (ahead == 0) | (ahead == n // 2)
-            behind = (ahead > n // 2).astype(jnp.int32)
-            hops = jnp.where(behind == 1, n - ahead, ahead)
-            call = jnp.where(whole, jnp.where(ahead == 0, 0, n - 1), 2 * hops - 1 + second)
-            place = block - (width // 2) * (second - 1 + behind)
+            call = jnp.minimum(ahead, n - ahead)
+            down = (ahead > 0) & (ahead < n // 2)
             base = call * (most + 1)
             count = plan_ref[base] + 1
             plan_ref[base] = count
-            plan_ref[base + count] = code_of(row, slot, jnp.where(whole, block, place))
-
-    for step in range(n):
+            plan_ref[base + count] = code_of(row, slot, jnp.where(down, width + block, block))
+
+    for step in range(calls):
         base = step * (most + 1)
         count = plan_ref[base]
 
@@ -219,7 +216,7 @@
         functools.partial(plan_kernel, (brows, slots, width, n, most)),
         in_specs=[SMEM] * 2,
         out_specs=SMEM,
-        out_shape=jax.ShapeDtypeStruct((n * (most + 1) + 1 + brows,), jnp.int32),
+        out_shape=jax.ShapeDtypeStruct(((n // 2 + 1) * (most + 1) + 1 + brows,), jnp.int32),
         compiler_params=PARAMS,
         name="plan",
     )(cols, fill)
@@ -244,14 +241,14 @@
     )(counts, base_rate)
 
 
-def step_kernel(dims, n, call, seconds, plan_ref, *refs):
+def step_kernel(dims, n, call, groups, plan_ref, *refs):
     basis, brows, slots, tile = dims
-    lag_ref, power_ref, excite_ref = refs[4:7]
+    lag_ref, power_ref, excite_ref = refs[len(groups) : len(groups) + 3]
     total_in, states_ref, total_ref, built_ref, held, weights, sems = refs[-7:]
     bins = lag_ref.shape[1]
-    half = held.shape[0] // 2
+    half = held.shape[0] // len(groups)
     each = carry_rows(half, basis)
-    most = (plan_ref.shape[0] - 1 - brows) // n - 1
+    most = (plan_ref.shape[0] - 1 - brows) // (n // 2 + 1) - 1
     built_ref[...] = jnp.zeros_like(built_ref)
     pairs = (plan_ref[call * (most + 1)] + 1) // 2
 
@@ -278,9 +275,9 @@
         weight_at(place).start()
 
     total_ref[...] = total_in[...]
-    for d in range(2):
-        impact_ref, carry_ref = refs[2 * d : 2 * d + 2]
-        first = half * bins + seconds[d] * each
+    for d, (carried_by, second) in enumerate(groups):
+        impact_ref, carry_ref = refs[d], refs[carried_by]
+        first = half * bins + second * each
         carry = carry_ref[first : first + each].astype(jnp.float32)
         for q in range(0, half, 2):
             both = jnp.concatenate(
@@ -314,15 +311,15 @@
         copy_at(place).wait()
 
 
-def take_step(call, seconds, plan, arrived, lag, power, excite, states, total, dims, n):
+def take_step(call, groups, plan, arrived, lag, power, excite, states, total, dims, n):
     basis, brows, slots, tile = dims
     bins = lag.shape[1]
     half = arrived[0].shape[0] // bins
-    most = (plan.shape[0] - 1 - brows) // n - 1
+    most = (plan.shape[0] - 1 - brows) // (n // 2 + 1) - 1
     given = [total] if states is None else [states, total]
     return pl.pallas_call(
-        functools.partial(step_kernel, dims, n, call, seconds),
-        in_specs=[SMEM] + [VMEM] * 6 + [ANYWHERE] * len(given) + [VMEM],
+        functools.partial(step_kernel, dims, n, call, groups),
+        in_specs=[SMEM] + [VMEM] * (len(groups) + 2) + [ANYWHERE] * len(given) + [VMEM],
         out_specs=[ANYWHERE, VMEM, VMEM],
         out_shape=[
             jax.ShapeDtypeStruct((brows * slots + 1, bins, basis * tile), jnp.bfloat16),
@@ -330,11 +327,11 @@
             jax.ShapeDtypeStruct((8, tile), jnp.float32),
         ],
         scratch_shapes=[
-            pltpu.VMEM((2 * half, bins, basis * tile), jnp.bfloat16),
+            pltpu.VMEM((len(groups) * half, bins, basis * tile), jnp.bfloat16),
             pltpu.VMEM((most, basis, tile, tile), jnp.bfloat16),
             pltpu.SemaphoreType.DMA((2, most)),
         ],
-        input_output_aliases={} if states is None else {8: 0},
+        input_output_aliases={} if states is None else {len(groups) + 4: 0},
         compiler_params=PARAMS,
         cost_estimate=pl.CostEstimate(
             flops=8 * basis * bins * bins * tile * 4,
@@ -481,24 +478,26 @@
     enter = lax.ppermute(ends, "tm", [(0, 1)])
     two = add_carry(enter, two, basis, bins)
     lag, power = lag_tables(bins, basis, overall, tile)
-    plan = make_plan(block_col, row_fill, dims, counts.shape[1] // tile, n)
-    total = start_total(counts, base_rate.reshape(1, -1), dims)
 
     states = None
     built = []
 
-    def step(call, seconds, arrived):
+    def after(value, message):
+        return lax.optimization_barrier((value, message))[0]
+
+    def step(groups, arrived):
         nonlocal states, total
         states, total, done = take_step(
-            call, seconds, plan, arrived, lag, power, excite, states, total, dims, n
+            len(built), groups, plan, arrived, lag, power, excite, states, total, dims, n
         )
         built.append(done)
 
     def send(message, way, hop):
         if hop > 2:
-            message = lax.optimization_barrier((message, built[2 * hop - 4]))[0]
+            message = after(message, built[hop - 2])
         return lax.ppermute(message, "types", way)
 
+    two_groups = ((1, 0), (1, 1))
     hops = n // 2
     at_up, at_down = [one, two], [one, two]
     for hop in range(1, hops + 1):
@@ -511,16 +510,15 @@
             next_up = [send(at_up[0], up, hop), None]
             next_down = [None, send(at_down[1], down, hop)]
         if hop == 1:
-            step(0, (0, 1), [one, two, two, two])
+            cols = after(block_col, next_up[0])
+            plan = make_plan(cols, row_fill, dims, counts.shape[1] // tile, n)
+            total = start_total(counts, base_rate.reshape(1, -1), dims)
+            total = after(total, next_up[1])
+            step(two_groups, [one, two])
         else:
-            for second in range(2):
-                step(
-                    2 * hop - 3 + second,
-                    (second, second),
-                    [at_up[second], at_up[1], at_down[second], at_down[1]],
-                )
+            step(((1, 0), (1, 1), (3, 0), (3, 1)), [*at_up, *at_down])
         at_up, at_down = next_up, next_down
-    step(n - 1, (0, 1), [at_up[0], at_down[1], at_down[1], at_down[1]])
+    step(two_groups, [at_up[0], at_down[1]])
 
     out, kept, turned, rate_sent, rate_kept = first_products(plan, total, states, dims, overall)
     kept = [kept]

time: 74.1 us -> 76.8 us (1.036)
  waiting for transfers between devices: 4.71 us -> 12.4 us
  Pallas kernels: 44.4 us -> 37.5 us
  starting transfers between devices: 19.3 us -> 21.2 us
    ppermute x14, waiting for transfers between devices: 1.75 us -> 9.45 us  [send(): return lax.ppermute(message, 'types', way)]
    pallas_call x8 -> x5, Pallas kernels: 30 us -> 23.5 us  [take_step(): pl.pallas_call(functools.partial(step_kernel, dims, n, call, groups), in_...]
    ppermute x14, starting transfers between devices: 17.2 us -> 19 us  [send(): return lax.ppermute(message, 'types', way)]
    unnamed x13 -> x12, local copies, waits for them, and re-layouts: 2.9 us -> 2.81 us
  transfers between devices with their start and end apart: 18 -> 18, of which waited for: 5 -> 6; matrix products, arithmetic and copies ran while one was open for 1% -> 1% of each run, Pallas kernels for 49% -> 38%
where the time goes in v8:
time: 76.8 us; the launch traced here: 75.9 us
  Pallas kernels  37.5 us (49%)
  starting transfers between devices  21.2 us (28%)
  waiting for transfers between devices  12.4 us (16%)
  local copies, waits for them, and re-layouts  3.09 us (4%)
  between operations  1.07 us (1%)
    pallas_call x5, Pallas kernels, take_step(): pl.pallas_call(functools.partial(step_kernel, dims, n, call, groups), in_...  23.5 us
    ppermute x14, starting transfers between devices, send(): return lax.ppermute(message, 'types', way)  19 us
    ppermute x14, waiting for transfers between devices, send(): return lax.ppermute(message, 'types', way)  9.45 us
    pallas_call x2, Pallas kernels, add_received(): pl.pallas_call(functools.partial(add_kernel, dims, group), in_specs=[VMEM...  3.14 us
    unnamed x12, local copies, waits for them, and re-layouts  2.81 us
    pallas_call x1, Pallas kernels, make_plan(): pl.pallas_call(functools.partial(plan_kernel, (brows, slots, width, n, mo...  2.6 us
    pallas_call x1, Pallas kernels, impact_messages(): pl.pallas_call(functools.partial(second_kernel, basis, tile, overall), in...  2.46 us
    pallas_call x1, Pallas kernels, impact_messages(): pl.pallas_call(first_kernel, in_specs=[ANYWHERE, ANYWHERE], out_specs=VME...  1.97 us
  transfers between devices with their start and end apart: 18, of which 6 were waited for; matrix products, arithmetic and copies ran while one was open for 1% of the time, Pallas kernels for 38%

profile of v8, /device:TPU:0, one launch (start us, length us, event | category | flops | bytes accessed | tf_op | source)
XLA Modules:
  0.0 75.9 jit_solution(6868139377517875713)
XLA Ops:
  0.7 2.0 %first_message.1.refs_0_ = bf16[1024,128]{1,0:T(8,128)(2,1)} custom-call(s32[256,1024]{1,0:T(8,128)} %counts_ref.1, bf16[256,1024]{1,0:T(8,128)(2,1)} %mark_hbm.3), custom_call_target="tpu_custom_call" | custom-call | tf_op jit(solution)/shard_map/first_message/pallas_call | solution.py:102
  2.7 3.1 %collective-permute-start = (bf16[1024,128]{1,0:T(8,128)(2,1)}, bf16[1024,128]{1,0:T(8,128)(2,1)S(1)}, u32[]{:S(2)}, u32[]{:S(2)}) collective-permute-start(bf16[1024,128]{1,0:T(8,128)(2,1)} %first_message.1.refs_0_), channel_id=1, source_target_pairs={{0,4},{4,8},{8,12},{12,14},{14,10},{10,6},{6,2},{2,0},{1,5},{5,9},... | collective-permute-start | bytes 786440 | tf_op jit(solution)/shard_map/ppermute | solution.py:498
  5.8 2.5 %second_message.1 = (bf16[1056,128]{1,0:T(8,128)(2,1)}, f32[4,1024]{1,0:T(4,128)}) custom-call(s32[256,1024]{1,0:T(8,128)} %counts_ref.1, bf16[256,1024]{1,0:T(8,128)(2,1)} %mark_hbm.3), custom_call_target="tpu_custom_call" | custom-call | tf_op jit(solution)/shard_map/second_message/pallas_call | solution.py:115
  8.2 1.5 %collective-permute-start.2 = (f32[4,1024]{1,0:T(4,128)}, f32[4,1024]{1,0:T(4,128)S(1)}, u32[]{:S(2)}, u32[]{:S(2)}) collective-permute-start(f32[4,1024]{1,0:T(4,128)} %get-tuple-element.34), channel_id=1, source_target_pairs={{0,1},{2,3},{4,5},{6,7},{8,9},{10,11},{12,13},{14,15},{16,17},{18,... | collective-permute-start | bytes 49160 | tf_op jit(solution)/shard_map/ppermute | solution.py:478
  11.3 1.8 %collective-permute-start.5 = (bf16[1056,128]{1,0:T(8,128)(2,1)}, bf16[1056,128]{1,0:T(8,128)(2,1)S(1)}, u32[]{:S(2)}, u32[]{:S(2)}) collective-permute-start(bf16[1056,128]{1,0:T(8,128)(2,1)} %carry_rows.1.refs_1_), channel_id=1, source_target_pairs={{4,0},{8,4},{12,8},{14,12},{10,14},{6,10},{2,6},{0,2},{5,1},{9,5},... | collective-permute-start | bytes 811016 | tf_op jit(solution)/shard_map/ppermute | solution.py:498
  13.8 1.9 %collective-permute-start.1 = (bf16[1024,128]{1,0:T(8,128)(2,1)S(1)}, bf16[1024,128]{1,0:T(8,128)(2,1)}, u32[]{:S(2)}, u32[]{:S(2)}) collective-permute-start(bf16[1024,128]{1,0:T(8,128)(2,1)S(1)} %collective-permute-done.refs_0_), channel_id=1, source_target_pairs={{0,4},{4,8},{8,12},{12,14},{14,10},{10,6},{6,2},{2,0},{1,5},{5,9},... | collective-permute-start | bytes 786440 | tf_op jit(solution)/shard_map/ppermute | solution.py:498
  15.7 4.8 %collective-permute-done.5.refs_3_ = bf16[1056,128]{1,0:T(8,128)(2,1)S(1)} collective-permute-done((bf16[1056,128]{1,0:T(8,128)(2,1)}, bf16[1056,128]{1,0:T(8,128)(2,1)S(1)}, u32[]{:S(2)}, u32[]{:S(2)}) %collective-permute-start.5) | collective-permute-done | bytes 270368 | tf_op jit(solution)/shard_map/ppermute | solution.py:498
  20.4 1.7 %collective-permute-start.9 = (bf16[1056,128]{1,0:T(8,128)(2,1)S(1)}, bf16[1056,128]{1,0:T(8,128)(2,1)S(1)}, u32[]{:S(2)}, u32[]{:S(2)}) collective-permute-start(bf16[1056,128]{1,0:T(8,128)(2,1)S(1)} %collective-permute-done.5.refs_3_), channel_id=1, source_target_pairs={{4,0},{8,4},{12,8},{14,12},{10,14},{6,10},{2,6},{0,2},{5,1},{9,5},... | collective-permute-start | bytes 811016 | tf_op jit(solution)/shard_map/ppermute | solution.py:498
  22.4 2.6 %plan.1.plan_ref = s32[74]{0:T(128)S(1)} custom-call(s32[64,6]{1,0:T(8,128)S(1)} %copy.14.col_ref, s32[64]{0:T(128)S(1)} %copy-done.4), custom_call_target="tpu_custom_call" | custom-call | tf_op jit(solution)/shard_map/plan/pallas_call | solution.py:215
  25.0 1.7 %collective-permute-start.8 = (bf16[1024,128]{1,0:T(8,128)(2,1)S(1)}, bf16[1024,128]{1,0:T(8,128)(2,1)S(1)}, u32[]{:S(2)}, u32[]{:S(2)}) collective-permute-start(bf16[1024,128]{1,0:T(8,128)(2,1)S(1)} %collective-permute-done.4.refs_2_), channel_id=1, source_target_pairs={{4,0},{8,4},{12,8},{14,12},{10,14},{6,10},{2,6},{0,2},{5,1},{9,5},... | collective-permute-start | bytes 786440 | tf_op jit(solution)/shard_map/ppermute | solution.py:498
  27.3 2.8 %copy-done = bf16[4,8,6,128,128]{4,3,2,1,0:T(8,128)(2,1)S(1)} copy-done((bf16[4,8,6,128,128]{4,3,2,1,0:T(8,128)(2,1)S(1)}, bf16[4,8,6,128,128]{4,3,2,1,0:T(8,128)(2,1)}, u32[]{:S(2)}) %copy-start) | copy-done | bytes 6291480
  30.1 4.4 %ring_step.5 = (bf16[49,256,512]{2,1,0:T(8,128)(2,1)S(1)}, f32[9,256,128]{2,1,0:T(8,128)S(1)}, f32[8,128]{1,0:T(8,128)}) custom-call(s32[74]{0:T(128)S(1)} %plan.1.plan_ref, bf16[1024,128]{1,0:T(8,128)(2,1)S(1)} %copy-done.2, bf16[1056,128]{1,0:T(8,128)(2,1)} %carry_rows.1.refs_1_, bf16[4,256,256]{2,1,0:T(8,128)(2,1)S(1)} %select_convert_fusion.refs_2_.refs_4_, ...), custom_call_target="tpu_custom_call" | custom-call | flops 1073741824 | bytes 4194304 | tf_op jit(solution)/shard_map/ring_step/pallas_call | solution.py:320
  34.6 4.0 %ring_step.6 = (bf16[49,256,512]{2,1,0:T(8,128)(2,1)S(1)}, f32[9,256,128]{2,1,0:T(8,128)S(1)}, f32[8,128]{1,0:T(8,128)}) custom-call(s32[74]{0:T(128)S(1)} %plan.1.plan_ref, bf16[1024,128]{1,0:T(8,128)(2,1)S(1)} %collective-permute-done.refs_0_, bf16[1056,128]{1,0:T(8,128)(2,1)S(1)} %collective-permute-done.3.refs_1_, ...), custom_call_target="tpu_custom_call", output_to_operand_aliasing={{0}: (8, {})} | custom-call | flops 1073741824 | bytes 4194304 | tf_op jit(solution)/shard_map/ring_step/pallas_call | solution.py:320
  38.6 1.7 %collective-permute-start.11 = (bf16[1056,128]{1,0:T(8,128)(2,1)S(1)}, bf16[1056,128]{1,0:T(8,128)(2,1)S(1)}, u32[]{:S(2)}, u32[]{:S(2)}) collective-permute-start(bf16[1056,128]{1,0:T(8,128)(2,1)S(1)} %collective-permute-done.9.refs_3_), channel_id=1, source_target_pairs={{4,0},{8,4},{12,8},{14,12},{10,14},{6,10},{2,6},{0,2},{5,1},{9,5},... | collective-permute-start | bytes 811016 | tf_op jit(solution)/shard_map/ppermute | solution.py:498
  40.6 3.3 %collective-permute-start.14 = (bf16[1024,128]{1,0:T(8,128)(2,1)S(1)}, bf16[1024,128]{1,0:T(8,128)(2,1)S(1)}, u32[]{:S(2)}, u32[]{:S(2)}) collective-permute-start(bf16[1024,128]{1,0:T(8,128)(2,1)S(1)} %collective-permute-done.8.refs_2_), channel_id=1, source_target_pairs={{4,0},{8,4},{12,8},{14,12},{10,14},{6,10},{2,6},{0,2},{5,1},{9,5},... | collective-permute-start | bytes 786440 | tf_op jit(solution)/shard_map/ppermute | solution.py:498
  44.0 5.7 %ring_step.7 = (bf16[49,256,512]{2,1,0:T(8,128)(2,1)S(1)}, f32[9,256,128]{2,1,0:T(8,128)S(1)}, f32[8,128]{1,0:T(8,128)}) custom-call(s32[74]{0:T(128)S(1)} %plan.1.plan_ref, bf16[1024,128]{1,0:T(8,128)(2,1)} %collective-permute-done.1.refs_0_, bf16[1056,128]{1,0:T(8,128)(2,1)S(1)} %collective-permute-done.7.refs_1_, ...), custom_call_target="tpu_custom_call", output_to_operand_aliasing={{0}: (8, {})} | custom-call | flops 1073741824 | bytes 4194304 | tf_op jit(solution)/shard_map/ring_step/pallas_call | solution.py:320
  49.6 2.7 %collective-permute-start.12 = (bf16[1056,128]{1,0:T(8,128)(2,1)S(1)}, bf16[1056,128]{1,0:T(8,128)(2,1)S(1)}, u32[]{:S(2)}, u32[]{:S(2)}) collective-permute-start(bf16[1056,128]{1,0:T(8,128)(2,1)S(1)} %collective-permute-done.11.refs_3_), channel_id=1, source_target_pairs={{4,0},{8,4},{12,8},{14,12},{10,14},{6,10},{2,6},{0,2},{5,1},{9,5},... | collective-permute-start | bytes 811016 | tf_op jit(solution)/shard_map/ppermute | solution.py:498
  52.5 4.6 %collective-permute-done.13.refs_1_ = bf16[1056,128]{1,0:T(8,128)(2,1)S(1)} collective-permute-done((bf16[1056,128]{1,0:T(8,128)(2,1)S(1)}, bf16[1056,128]{1,0:T(8,128)(2,1)S(1)}, u32[]{:S(2)}, u32[]{:S(2)}) %collective-permute-start.13) | collective-permute-done | bytes 270368 | tf_op jit(solution)/shard_map/ppermute | solution.py:498
  57.0 5.8 %ring_step.8 = (bf16[49,256,512]{2,1,0:T(8,128)(2,1)S(1)}, f32[9,256,128]{2,1,0:T(8,128)S(1)}, f32[8,128]{1,0:T(8,128)}) custom-call(s32[74]{0:T(128)S(1)} %plan.1.plan_ref, bf16[1024,128]{1,0:T(8,128)(2,1)S(1)} %collective-permute-done.6.refs_0_, bf16[1056,128]{1,0:T(8,128)(2,1)S(1)} %collective-permute-done.13.refs_1_, ...), custom_call_target="tpu_custom_call", output_to_operand_aliasing={{0}: (8, {})} | custom-call | flops 1073741824 | bytes 4194304 | tf_op jit(solution)/shard_map/ring_step/pallas_call | solution.py:320
  62.9 3.6 %ring_step.9 = (bf16[49,256,512]{2,1,0:T(8,128)(2,1)S(1)}, f32[9,256,128]{2,1,0:T(8,128)S(1)}, f32[8,128]{1,0:T(8,128)}) custom-call(s32[74]{0:T(128)S(1)} %plan.1.plan_ref, bf16[1024,128]{1,0:T(8,128)(2,1)S(1)} %collective-permute-done.10.refs_0_, bf16[1056,128]{1,0:T(8,128)(2,1)S(1)} %collective-permute-done.12.refs_1_, ...), custom_call_target="tpu_custom_call", output_to_operand_aliasing={{0}: (6, {})} | custom-call | flops 1073741824 | bytes 4194304 | tf_op jit(solution)/shard_map/ring_step/pallas_call | solution.py:320
  66.5 1.6 %weighted_products.1 = (bf16[4,4,6,64,128]{4,3,2,1,0:T(8,128)(2,1)S(1)}, f32[4,4,6,64,128]{4,3,2,1,0:T(8,128)S(1)}, bf16[8,128,256]{2,1,0:T(8,128)(2,1)S(1)}, f32[4,128]{1,0:T(4,128)S(1)}, f32[4,128]{1,0:T(4,128)S(1)}) custom-call(s32[74]{0:T(128)S(1)} %plan.1.plan_ref, f32[9,256,128]{2,1,0:T(8,128)S(1)} %get-tuple-element.53.total_ref, ...), custom_call_target="tpu_custom_call" | custom-call | tf_op jit(solution)/shard_map/weighted_products/pallas_call | solution.py:400
  68.2 1.5 %products.1 = (bf16[4,4,6,64,128]{4,3,2,1,0:T(8,128)(2,1)S(1)}, f32[4,4,6,64,128]{4,3,2,1,0:T(8,128)S(1)}) custom-call(s32[74]{0:T(128)S(1)} %plan.1.plan_ref, bf16[8,128,256]{2,1,0:T(8,128)(2,1)S(1)} %get-tuple-element.55.turned_ref, bf16[49,256,512]{2,1,0:T(8,128)(2,1)S(1)} %get-tuple-element.54.states_ref), custom_call_target="tpu_custom_call" | custom-call | tf_op jit(solution)/shard_map/products/pallas_call | solution.py:417
  71.6 1.3 %add_received.2.refs_2_ = bf16[4,8,6,64,128]{4,3,2,1,0:T(8,128)(2,1)} custom-call(f32[4,4,6,64,128]{4,3,2,1,0:T(8,128)S(1)} %get-tuple-element.60.kept_ref, bf16[4,4,6,64,128]{4,3,2,1,0:T(8,128)(2,1)S(1)} %collective-permute-done.17.got_ref), custom_call_target="tpu_custom_call" | custom-call | tf_op jit(solution)/shard_map/add_received/pallas_call | solution.py:451
  73.8 1.9 %add_received.3 = (bf16[4,8,6,64,128]{4,3,2,1,0:T(8,128)(2,1)}, f32[4,128]{1,0:T(4,128)}) custom-call(f32[4,4,6,64,128]{4,3,2,1,0:T(8,128)S(1)} %get-tuple-element.56.kept_ref, bf16[4,4,6,64,128]{4,3,2,1,0:T(8,128)(2,1)S(1)} %collective-permute-done.15.got_ref, f32[4,128]{1,0:T(4,128)S(1)} %get-tuple-element.58.refs_0_, ...), custom_call_target="tpu_custom_call", output_to_operand_aliasing={{0}: (4, {})} | custom-call | tf_op jit(solution)/shard_map/add_received/pallas_call | solution.py:451
  (46 shorter events, 6.5 us)
Async XLA Ops:
  0.6 21.6 %copy-start.1 = (s32[256,1024]{1,0:T(8,128)S(1)}, s32[256,1024]{1,0:T(8,128)}, u32[]{:S(2)}) copy-start(s32[256,1024]{1,0:T(8,128)} %counts_ref.1) | copy-start | bytes 3145732
  0.6 21.6 %copy-start.3 = (f32[1024]{0:T(1024)S(1)}, f32[1024]{0:T(1024)}, u32[]{:S(2)}) copy-start(f32[1024]{0:T(1024)} %param.8) | copy-start | bytes 12292
  2.6 19.7 %copy-start.5 = (s32[64,6]{0,1:T(8,128)S(1)}, s32[64,6]{0,1:T(8,128)}, u32[]{:S(2)}) copy-start(s32[64,6]{0,1:T(8,128)} %param.10) | copy-start | bytes 4612
  2.6 19.8 %copy-start.4 = (s32[64]{0:T(128)S(1)}, s32[64]{0:T(128)}, u32[]{:S(2)}) copy-start(s32[64]{0:T(128)} %fill_ref.1) | copy-start | bytes 772
  2.7 24.7 %copy-start.2 = (bf16[1024,128]{1,0:T(8,128)(2,1)S(1)}, bf16[1024,128]{1,0:T(8,128)(2,1)}, u32[]{:S(2)}) copy-start(bf16[1024,128]{1,0:T(8,128)(2,1)} %first_message.1.refs_0_) | copy-start | bytes 786436
  2.7 11.1 %collective-permute-start = (bf16[1024,128]{1,0:T(8,128)(2,1)}, bf16[1024,128]{1,0:T(8,128)(2,1)S(1)}, u32[]{:S(2)}, u32[]{:S(2)}) collective-permute-start(bf16[1024,128]{1,0:T(8,128)(2,1)} %first_message.1.refs_0_), channel_id=1, source_target_pairs={{0,4},{4,8},{8,12},{12,14},{14,10},{10,6},{6,2},{2,0},{1,5},{5,9},... | collective-permute-start | bytes 786440 | tf_op jit(solution)/shard_map/ppermute | solution.py:498
  5.7 19.3 %collective-permute-start.4 = (bf16[1024,128]{1,0:T(8,128)(2,1)}, bf16[1024,128]{1,0:T(8,128)(2,1)S(1)}, u32[]{:S(2)}, u32[]{:S(2)}) collective-permute-start(bf16[1024,128]{1,0:T(8,128)(2,1)} %first_message.1.refs_0_), channel_id=1, source_target_pairs={{4,0},{8,4},{12,8},{14,12},{10,14},{6,10},{2,6},{0,2},{5,1},{9,5},... | collective-permute-start | bytes 786440 | tf_op jit(solution)/shard_map/ppermute | solution.py:498
  8.2 2.5 %collective-permute-start.2 = (f32[4,1024]{1,0:T(4,128)}, f32[4,1024]{1,0:T(4,128)S(1)}, u32[]{:S(2)}, u32[]{:S(2)}) collective-permute-start(f32[4,1024]{1,0:T(4,128)} %get-tuple-element.34), channel_id=1, source_target_pairs={{0,1},{2,3},{4,5},{6,7},{8,9},{10,11},{12,13},{14,15},{16,17},{18,... | collective-permute-start | bytes 49160 | tf_op jit(solution)/shard_map/ppermute | solution.py:478
  11.3 9.1 %collective-permute-start.5 = (bf16[1056,128]{1,0:T(8,128)(2,1)}, bf16[1056,128]{1,0:T(8,128)(2,1)S(1)}, u32[]{:S(2)}, u32[]{:S(2)}) collective-permute-start(bf16[1056,128]{1,0:T(8,128)(2,1)} %carry_rows.1.refs_1_), channel_id=1, source_target_pairs={{4,0},{8,4},{12,8},{14,12},{10,14},{6,10},{2,6},{0,2},{5,1},{9,5},... | collective-permute-start | bytes 811016 | tf_op jit(solution)/shard_map/ppermute | solution.py:498
  13.2 13.5 %collective-permute-start.3 = (bf16[1056,128]{1,0:T(8,128)(2,1)}, bf16[1056,128]{1,0:T(8,128)(2,1)S(1)}, u32[]{:S(2)}, u32[]{:S(2)}) collective-permute-start(bf16[1056,128]{1,0:T(8,128)(2,1)} %carry_rows.1.refs_1_), channel_id=1, source_target_pairs={{0,4},{4,8},{8,12},{12,14},{14,10},{10,6},{6,2},{2,0},{1,5},{5,9},... | collective-permute-start | bytes 811016 | tf_op jit(solution)/shard_map/ppermute | solution.py:498
  13.8 26.5 %collective-permute-start.1 = (bf16[1024,128]{1,0:T(8,128)(2,1)S(1)}, bf16[1024,128]{1,0:T(8,128)(2,1)}, u32[]{:S(2)}, u32[]{:S(2)}) collective-permute-start(bf16[1024,128]{1,0:T(8,128)(2,1)S(1)} %collective-permute-done.refs_0_), channel_id=1, source_target_pairs={{0,4},{4,8},{8,12},{12,14},{14,10},{10,6},{6,2},{2,0},{1,5},{5,9},... | collective-permute-start | bytes 786440 | tf_op jit(solution)/shard_map/ppermute | solution.py:498
  20.4 18.1 %collective-permute-start.9 = (bf16[1056,128]{1,0:T(8,128)(2,1)S(1)}, bf16[1056,128]{1,0:T(8,128)(2,1)S(1)}, u32[]{:S(2)}, u32[]{:S(2)}) collective-permute-start(bf16[1056,128]{1,0:T(8,128)(2,1)S(1)} %collective-permute-done.5.refs_3_), channel_id=1, source_target_pairs={{4,0},{8,4},{12,8},{14,12},{10,14},{6,10},{2,6},{0,2},{5,1},{9,5},... | collective-permute-start | bytes 811016 | tf_op jit(solution)/shard_map/ppermute | solution.py:498
  25.0 15.6 %collective-permute-start.8 = (bf16[1024,128]{1,0:T(8,128)(2,1)S(1)}, bf16[1024,128]{1,0:T(8,128)(2,1)S(1)}, u32[]{:S(2)}, u32[]{:S(2)}) collective-permute-start(bf16[1024,128]{1,0:T(8,128)(2,1)S(1)} %collective-permute-done.4.refs_2_), channel_id=1, source_target_pairs={{4,0},{8,4},{12,8},{14,12},{10,14},{6,10},{2,6},{0,2},{5,1},{9,5},... | collective-permute-start | bytes 786440 | tf_op jit(solution)/shard_map/ppermute | solution.py:498
  26.7 17.3 %collective-permute-start.7 = (bf16[1056,128]{1,0:T(8,128)(2,1)S(1)}, bf16[1056,128]{1,0:T(8,128)(2,1)S(1)}, u32[]{:S(2)}, u32[]{:S(2)}) collective-permute-start(bf16[1056,128]{1,0:T(8,128)(2,1)S(1)} %collective-permute-done.3.refs_1_), channel_id=1, source_target_pairs={{0,4},{4,8},{8,12},{12,14},{14,10},{10,6},{6,2},{2,0},{1,5},{5,9},... | collective-permute-start | bytes 811016 | tf_op jit(solution)/shard_map/ppermute | solution.py:498
  27.3 2.8 %copy-start = (bf16[4,8,6,128,128]{4,3,2,1,0:T(8,128)(2,1)S(1)}, bf16[4,8,6,128,128]{4,3,2,1,0:T(8,128)(2,1)}, u32[]{:S(2)}) copy-start(bf16[4,8,6,128,128]{4,3,2,1,0:T(8,128)(2,1)} %refs_4_.3) | copy-start | bytes 18874372
  38.6 11.1 %collective-permute-start.11 = (bf16[1056,128]{1,0:T(8,128)(2,1)S(1)}, bf16[1056,128]{1,0:T(8,128)(2,1)S(1)}, u32[]{:S(2)}, u32[]{:S(2)}) collective-permute-start(bf16[1056,128]{1,0:T(8,128)(2,1)S(1)} %collective-permute-done.9.refs_3_), channel_id=1, source_target_pairs={{4,0},{8,4},{12,8},{14,12},{10,14},{6,10},{2,6},{0,2},{5,1},{9,5},... | collective-permute-start | bytes 811016 | tf_op jit(solution)/shard_map/ppermute | solution.py:498
  40.2 12.1 %collective-permute-start.6 = (bf16[1024,128]{1,0:T(8,128)(2,1)}, bf16[1024,128]{1,0:T(8,128)(2,1)S(1)}, u32[]{:S(2)}, u32[]{:S(2)}) collective-permute-start(bf16[1024,128]{1,0:T(8,128)(2,1)} %collective-permute-done.1.refs_0_), channel_id=1, source_target_pairs={{0,4},{4,8},{8,12},{12,14},{14,10},{10,6},{6,2},{2,0},{1,5},{5,9},... | collective-permute-start | bytes 786440 | tf_op jit(solution)/shard_map/ppermute | solution.py:498
  40.6 11.8 %collective-permute-start.14 = (bf16[1024,128]{1,0:T(8,128)(2,1)S(1)}, bf16[1024,128]{1,0:T(8,128)(2,1)S(1)}, u32[]{:S(2)}, u32[]{:S(2)}) collective-permute-start(bf16[1024,128]{1,0:T(8,128)(2,1)S(1)} %collective-permute-done.8.refs_2_), channel_id=1, source_target_pairs={{4,0},{8,4},{12,8},{14,12},{10,14},{6,10},{2,6},{0,2},{5,1},{9,5},... | collective-permute-start | bytes 786440 | tf_op jit(solution)/shard_map/ppermute | solution.py:498
  44.0 13.0 %collective-permute-start.13 = (bf16[1056,128]{1,0:T(8,128)(2,1)S(1)}, bf16[1056,128]{1,0:T(8,128)(2,1)S(1)}, u32[]{:S(2)}, u32[]{:S(2)}) collective-permute-start(bf16[1056,128]{1,0:T(8,128)(2,1)S(1)} %collective-permute-done.7.refs_1_), channel_id=1, source_target_pairs={{0,4},{4,8},{8,12},{12,14},{14,10},{10,6},{6,2},{2,0},{1,5},{5,9},... | collective-permute-start | bytes 811016 | tf_op jit(solution)/shard_map/ppermute | solution.py:498
  49.6 13.2 %collective-permute-start.12 = (bf16[1056,128]{1,0:T(8,128)(2,1)S(1)}, bf16[1056,128]{1,0:T(8,128)(2,1)S(1)}, u32[]{:S(2)}, u32[]{:S(2)}) collective-permute-start(bf16[1056,128]{1,0:T(8,128)(2,1)S(1)} %collective-permute-done.11.refs_3_), channel_id=1, source_target_pairs={{4,0},{8,4},{12,8},{14,12},{10,14},{6,10},{2,6},{0,2},{5,1},{9,5},... | collective-permute-start | bytes 811016 | tf_op jit(solution)/shard_map/ppermute | solution.py:498
  52.4 10.5 %collective-permute-start.10 = (bf16[1024,128]{1,0:T(8,128)(2,1)S(1)}, bf16[1024,128]{1,0:T(8,128)(2,1)S(1)}, u32[]{:S(2)}, u32[]{:S(2)}) collective-permute-start(bf16[1024,128]{1,0:T(8,128)(2,1)S(1)} %collective-permute-done.6.refs_0_), channel_id=1, source_target_pairs={{0,4},{4,8},{8,12},{12,14},{14,10},{10,6},{6,2},{2,0},{1,5},{5,9},... | collective-permute-start | bytes 786440 | tf_op jit(solution)/shard_map/ppermute | solution.py:498
  68.1 3.5 %collective-permute-start.17 = (bf16[4,4,6,64,128]{4,3,2,1,0:T(8,128)(2,1)S(1)}, bf16[4,4,6,64,128]{4,3,2,1,0:T(8,128)(2,1)S(1)}, u32[]{:S(2)}, u32[]{:S(2)}) collective-permute-start(bf16[4,4,6,64,128]{4,3,2,1,0:T(8,128)(2,1)S(1)} %get-tuple-element.61), channel_id=1, source_target_pairs={{0,1},{1,0},{2,3},{3,2},{4,5},{5,4},{6,7},{7,6},{8,9},{9,8},{10,11... | collective-permute-start | bytes 4718600 | tf_op jit(solution)/shard_map/ppermute | solution.py:525
  69.7 4.1 %collective-permute-start.15 = (bf16[4,4,6,64,128]{4,3,2,1,0:T(8,128)(2,1)S(1)}, bf16[4,4,6,64,128]{4,3,2,1,0:T(8,128)(2,1)S(1)}, u32[]{:S(2)}, u32[]{:S(2)}) collective-permute-start(bf16[4,4,6,64,128]{4,3,2,1,0:T(8,128)(2,1)S(1)} %get-tuple-element.57), channel_id=1, source_target_pairs={{0,1},{1,0},{2,3},{3,2},{4,5},{5,4},{6,7},{7,6},{8,9},{9,8},{10,11... | collective-permute-start | bytes 4718600 | tf_op jit(solution)/shard_map/ppermute | solution.py:530
  70.3 3.5 %collective-permute-start.16 = (f32[4,128]{1,0:T(4,128)S(1)}, f32[4,128]{1,0:T(4,128)S(1)}, u32[]{:S(2)}, u32[]{:S(2)}) collective-permute-start(f32[4,128]{1,0:T(4,128)S(1)} %get-tuple-element.59), channel_id=1, source_target_pairs={{0,1},{1,0},{2,3},{3,2},{4,5},{5,4},{6,7},{7,6},{8,9},{9,8},{10,11... | collective-permute-start | bytes 6152 | tf_op jit(solution)/shard_map/ppermute | solution.py:526
